TPU v7x, 32 devices: a whole 2x2x4 slice. The times are simulated.
32 devices in a mesh: ctx: 16 (over z, y, x), tp: 2 (over core).
Axes of the slice: x: 2, y: 2, z: 4, core: 2. Of those that a mesh axis runs over, the one named last changes fastest.
Arguments:
- tokens: bfloat16 [8192, 8192], P('ctx', 'tp'), may hold values from -18 to 18
- w_query: bfloat16 [8192, 8192], P('ctx', 'tp'), may hold values from -0.0625 to 0.0625
- key_weight: bfloat16 [8192, 1024], P('ctx', 'tp'), may hold values from -0.0625 to 0.0625
- value_weight: bfloat16 [8192, 1024], P('ctx', 'tp'), may hold values from -0.0625 to 0.0625
- prefix_cache_blocks: bfloat16 [8, 128, 2, 128, 128], P('tp', 'ctx'), may hold values from -6 to 6
- selected_owner: int32 [8, 64, 8], P('tp', 'ctx'), may hold values from 0 to 15, all different within a row; in each aligned block of 4 rows (0 to 3, 4 to 7, ..., all dimensions but the last counted through in order) at most 3 rows name the same one
- selected_offset: int32 [8, 64, 8], P('tp', 'ctx'), may hold values from 0 to 7
- selected_alive_mask: int32 [8, 64, 8], P('tp', 'ctx'), may hold values 0 or 1
Outputs:
- attended: bfloat16 [8192, 8192], P('ctx', 'tp')
Inputs may be any that keep to these rules, and one draw needn't show every extreme that they name: `selected_owner`: each row names 8 different indices of ctx. In the rows of one device (aligned runs of 4 query blocks of one head) no index is named more than 3 times.
All inputs are finite; a program needn't handle non-finite values. No bound on the sum of `selected_alive_mask` on one device may be relied on, other than what follows from the above.
Results may differ from a plain program's by a relative error of at most 0.017.
Values may be sent and summed in bfloat16 or wider, within the bound.
No kernel may reach another device: no remote copies, remote signals or barrier semaphores. Data moves between devices by JAX's collectives and lax.ppermute only.
A program may use at most 192 MiB of HBM per device.

v0:
```python
import jax
import jax.numpy as jnp
from jax import lax
from jax.sharding import PartitionSpec as P

rope_base = 500000.0
neg_fill = -1e30


def apply_rotation(values, token_positions):
    half_dim = values.shape[-1] // 2
    steps = jnp.arange(half_dim).astype(jnp.float32)
    inverse = jnp.power(jnp.float32(rope_base), -2.0 * steps / values.shape[-1])
    angle = token_positions.astype(jnp.float32)[:, None] * inverse[None, :]
    cosine = jnp.cos(angle)[:, None, :]
    sine_part = jnp.sin(angle)[:, None, :]
    lower_half = values[..., :half_dim]
    upper_half = values[..., half_dim:]
    return jnp.concatenate(
        [
            lower_half * cosine - upper_half * sine_part,
            upper_half * cosine + lower_half * sine_part,
        ],
        axis=-1,
    )


def attend(query, selected, live_slots, own_keys, own_values):
    scaling = 1.0 / jnp.sqrt(jnp.float32(query.shape[-1]))
    far_scores = (
        jnp.einsum(
            "bihgd,hbskd->bhgisk", query, selected[:, :, :, 0], preferred_element_type=jnp.float32
        )
        * scaling
    )
    alive = jnp.transpose(live_slots, (1, 0, 2))[:, :, None, None, :, None] > 0
    far_scores = jnp.where(alive, far_scores, neg_fill)
    near_scores = (
        jnp.einsum("bihgd,bjhd->bhgij", query, own_keys, preferred_element_type=jnp.float32)
        * scaling
    )
    row_ids = jnp.arange(query.shape[1])
    causal = row_ids[:, None] >= row_ids[None, :]
    near_scores = jnp.where(causal, near_scores, neg_fill)
    row_max = jnp.maximum(jnp.max(far_scores, axis=(4, 5)), jnp.max(near_scores, axis=4))
    far_exp = jnp.exp(far_scores - row_max[..., None, None])
    near_exp = jnp.exp(near_scores - row_max[..., None])
    denominator = jnp.sum(far_exp, axis=(4, 5)) + jnp.sum(near_exp, axis=4)
    far_prob = (far_exp / denominator[..., None, None]).astype(jnp.bfloat16)
    near_prob = (near_exp / denominator[..., None]).astype(jnp.bfloat16)
    mixed = jnp.einsum(
        "bhgisk,hbskd->bihgd", far_prob, selected[:, :, :, 1], preferred_element_type=jnp.float32
    )
    mixed = mixed + jnp.einsum(
        "bhgij,bjhd->bihgd", near_prob, own_values, preferred_element_type=jnp.float32
    )
    return mixed


def per_device(
    tokens,
    w_query,
    key_weight,
    value_weight,
    prefix_cache_blocks,
    selected_owner,
    selected_offset,
    selected_alive_mask,
):
    tok_rows = tokens.shape[0]
    ctx_devices = lax.axis_size("ctx")
    kv_heads = prefix_cache_blocks.shape[0]
    blocks_dev = prefix_cache_blocks.shape[1]
    block_len = prefix_cache_blocks.shape[3]
    head_dim = prefix_cache_blocks.shape[4]
    query_blocks = selected_owner.shape[1]
    selections = selected_owner.shape[2]
    query_heads = w_query.shape[1] // head_dim
    query_group_width = query_heads // kv_heads
    capacity = min(query_blocks, (query_blocks * selections + ctx_devices - 1) // ctx_devices + 1)
    gathered = lax.all_gather(tokens, "tp", axis=1, tiled=True)
    pieces = (
        lax.all_gather(w_query, "ctx", axis=0, tiled=True),
        lax.all_gather(key_weight, "ctx", axis=0, tiled=True),
        lax.all_gather(value_weight, "ctx", axis=0, tiled=True),
    )
    query_proj, key_projected, value_projected = tuple(
        (jnp.dot(gathered, shard_rows, preferred_element_type=jnp.float32) for shard_rows in pieces)
    )
    requests = query_blocks * selections
    owners = selected_owner.reshape(kv_heads, requests)
    offsets = selected_offset.reshape(kv_heads, requests)
    owner_hot = (owners[:, :, None] == jnp.arange(ctx_devices, dtype=jnp.int32)).astype(jnp.int32)
    earlier = jnp.cumsum(owner_hot, axis=1) - owner_hot
    ordinal = jnp.sum(earlier * owner_hot, axis=2)
    slot_count = kv_heads * capacity
    slot_index = jnp.arange(kv_heads, dtype=jnp.int32)[:, None] * capacity + ordinal
    slot_hot = (slot_index[:, :, None] == jnp.arange(slot_count, dtype=jnp.int32)).astype(jnp.int32)
    entries = jnp.arange(kv_heads, dtype=jnp.int32)[:, None] * blocks_dev + offsets
    outgoing = jnp.einsum("hrn,hrs->ns", owner_hot * entries[:, :, None], slot_hot)
    cache_table = prefix_cache_blocks.reshape(kv_heads * blocks_dev, 2, block_len, head_dim)
    found_blocks = jnp.take(
        cache_table,
        lax.all_to_all(outgoing, "ctx", split_axis=0, concat_axis=0, tiled=True),
        axis=0,
    )
    arrived = lax.all_to_all(found_blocks, "ctx", split_axis=0, concat_axis=0, tiled=True)
    flattened = arrived.reshape(ctx_devices * slot_count, 2, block_len, head_dim)
    locator = owners * slot_count + slot_index
    picked = jnp.take(flattened, locator.reshape(-1), axis=0)
    selected = picked.reshape(kv_heads, query_blocks, selections, 2, block_len, head_dim)
    token_positions = (
        blocks_dev * ctx_devices * block_len
        + lax.axis_index("ctx") * tok_rows
        + jnp.arange(tok_rows, dtype=jnp.int32)
    )
    rotated_queries = apply_rotation(
        query_proj.reshape(tok_rows, query_heads, head_dim), token_positions
    ).astype(jnp.bfloat16)
    rotated_keys = apply_rotation(
        key_projected.reshape(tok_rows, kv_heads, head_dim), token_positions
    ).astype(jnp.bfloat16)
    fresh_values = value_projected.astype(jnp.bfloat16)
    q_local = rotated_queries.reshape(
        query_blocks, block_len, kv_heads, query_group_width, head_dim
    )
    k_local = rotated_keys.reshape(query_blocks, block_len, kv_heads, head_dim)
    v_local = fresh_values.reshape(query_blocks, block_len, kv_heads, head_dim)
    mixed = attend(q_local, selected, selected_alive_mask, k_local, v_local)
    return mixed.astype(jnp.bfloat16).reshape(tok_rows, query_heads * head_dim)


def solution(mesh):
    return jax.shard_map(
        per_device,
        mesh=mesh,
        in_specs=(
            P("ctx", "tp"),
            P("ctx", "tp"),
            P("ctx", "tp"),
            P("ctx", "tp"),
            P("tp", "ctx", None, None, None),
            P("tp", "ctx", None),
            P("tp", "ctx", None),
            P("tp", "ctx", None),
        ),
        out_specs=P("ctx", "tp"),
        check_vma=False,
    )
```

profile of v0, /device:TPU:0, one launch (start us, length us, event | category | flops | bytes accessed | tf_op | source)
XLA Modules:
  0.0 1356.7 jit_solution(11716201783375165183)
XLA Ops:
  6.5 0.7 all-gather.5.cloned.1.call-update
  7.3 0.7 all-gather.11.cloned.1.call-update
  8.1 0.7 all-gather.9.cloned.1.call-update
  8.8 0.5 all-gather.7.cloned.1.call-update
  9.3 0.1 eq.28
  9.4 0.1 reshape.258
  9.5 0.1 fusion.17
  9.6 0.1 reduce_window_sum.11
  9.7 0.2 select_reduce_fusion
  9.9 0.1 broadcast_add_fusion
  10.0 0.3 fusion.15
  10.3 15.4 %all_to_all.20 = s32[16,1,12]{2,1,0:T(1,128)S(1)} all-to-all(s32[16,1,12]{2,1,0:T(1,128)S(1)} %bitcast.108), channel_id=1, replica_groups=mesh['ctx'=16,'tp'=2] {'ctx'}, dimensions={0} | all-to-all | bytes 1536 | tf_op jit(solution)/shard_map/all_to_all | solution.py:104
  25.7 0.1 reshape.267
  25.8 8.2 gather_fusion
  34.0 10.8 broadcast_select_fusion
  44.8 5.2 all-to-all-start.1
  50.1 0.1 add.145
  50.1 0.1 reduce_sum.30
  50.3 0.1 mul.161
  50.4 0.1 compare_and_fusion.1
  50.5 0.5 multiply_cosine_fusion
  51.1 303.2 %all-gather.11.cloned.1.call-done = bf16[8192,512]{1,0:T(8,128)(2,1)} async-done(((bf16[512,512]{1,0:T(8,128)(2,1)}), bf16[8192,512]{1,0:T(8,128)(2,1)}) %all-gather.11.cloned.1.call-update) | async-done | bytes 8388624 | tf_op jit(solution)/shard_map/all_gather | solution.py:85
  354.3 10.2 convolution_convert_fusion
  364.6 0.9 reshape.263
  365.5 131.6 %all-gather.9.cloned.1.call-done = bf16[8192,512]{1,0:T(8,128)(2,1)} async-done(((bf16[512,512]{1,0:T(8,128)(2,1)}), bf16[8192,512]{1,0:T(8,128)(2,1)}) %all-gather.9.cloned.1.call-update) | async-done | bytes 8388624 | tf_op jit(solution)/shard_map/all_gather | solution.py:84
  497.2 9.4 fusion.31
  506.6 0.2 subtract_convert_fusion.1
  506.8 0.1 concatenate.21
  506.9 0.3 copy.42
  507.2 0.3 copy.43
  507.6 13.0 gather_fusion.1
  520.5 7.4 copy_select_fusion
  528.0 638.8 %all-gather.7.cloned.1.call-done = bf16[8192,4096]{1,0:T(8,128)(2,1)} async-done(((bf16[512,4096]{1,0:T(8,128)(2,1)}), bf16[8192,4096]{1,0:T(8,128)(2,1)}) %all-gather.7.cloned.1.call-update) | async-done | bytes 67108880 | tf_op jit(solution)/shard_map/all_gather | solution.py:83
  1166.8 43.6 %fusion.30 = f32[512,4096]{0,1:T(8,128)} fusion(bf16[512,8192]{1,0:T(8,128)(2,1)} %all-gather.5.cloned.1.call-done, bf16[8192,4096]{1,0:T(8,128)(2,1)} %all-gather.7.cloned.1.call-done), kind=kOutput, calls=%fused_computation.73 | convolution fusion | flops 34359738368 | bytes 83886080 | tf_op jit(solution)/shard_map/reshape | solution.py:118
  1210.4 6.2 subtract_convert_fusion
  1216.6 4.0 concatenate.18
  1220.6 5.9 copy.40
  1226.5 2.1 concatenate.19
  1228.5 5.9 copy.41
  1234.4 27.8 %bitcast_reduce_fusion = (f32[4,4,8,128]{3,2,1,0:T(8,128)S(1)}, f32[4,4,8,128,128,8]{4,3,5,2,1,0:T(8,128)}) fusion(pred[4,4,8]{2,1,0:T(4,128)(4,1)S(1)} %copy.37, bf16[4,128,4,8,64]{4,1,3,2,0:T(8,128)(2,1)} %copy.41, bf16[4,128,4,8,64]{4,1,3,2,0:T(8,128)(2,1)} %copy.40, bf16[4,4,8,2,128,128]{5,4,2,0,1,3:T(8,128)(2,1)} %copy_select_fusion), kind=kOutput, calls=%fused_computation.3 | convolution fusion | flops 4353671168 | bytes 79757440 | tf_op jit(solution)/shard_map/bihgd,hbskd->bhgisk/dot_general | solution.py:31
  1262.3 6.1 fusion.5
  1268.4 3.2 copy-done.2
  1271.6 2.7 fusion.4
  1274.3 21.4 %fusion.1 = f32[4,4,8,128]{3,2,1,0:T(8,128)S(1)} fusion(f32[4,4,8,128,128,8]{4,3,5,2,1,0:T(8,128)} %get-tuple-element.12, f32[4,4,8,128]{3,2,1,0:T(8,128)S(1)} %max.11, pred[4,4,8]{2,1,0:T(4,128)(4,1)S(1)} %copy.37), kind=kLoop, calls=%fused_computation.7 | loop fusion | flops 67092480 | bytes 67240064 | tf_op jit(solution)/shard_map/reduce_sum | solution.py:48
  1295.7 9.3 fusion.9
  1305.0 30.1 %fusion.6 = bf16[4,128,4,8,128]{1,4,3,2,0:T(8,128)(2,1)} fusion(f32[4,4,128,8,128]{4,2,3,1,0:T(8,128)} %fusion.9, f32[4,4,8,128,128,8]{4,3,5,2,1,0:T(8,128)} %get-tuple-element.12, f32[4,4,8,128]{3,2,1,0:T(8,128)S(1)} %add.153, f32[4,4,8,128]{3,2,1,0:T(8,128)S(1)} %max.11, pred[4,4,8]{2,1,0:T(4,128)(4,1)S(1)} %copy.37, ...), kind=kOutput, calls=%fused_computation.18 | convolution fusion | flops 4383047680 | bytes 84017280 | tf_op jit(solution)/shard_map/bhgisk,hbskd->bihgd/dot_general | solution.py:51
  1335.1 7.9 copy.48
  1342.9 7.3 reshape.264
  (36 shorter events, 0.3 us)
Async XLA Ops:
  6.5 19.3 %copy-start = (bf16[4,8,2,128,128]{4,3,2,1,0:T(8,128)(2,1)S(1)}, bf16[4,8,2,128,128]{4,3,2,1,0:T(8,128)(2,1)}, u32[]{:S(2)}) copy-start(bf16[4,8,2,128,128]{4,3,2,1,0:T(8,128)(2,1)} %param.12) | copy-start | bytes 6291460
  6.5 2.8 copy-start.4
  6.5 2.9 copy-start.5
  6.5 44.6 %all-gather.5.cloned.1.call-start = ((), (), s32[]{:S(2)}) async-start(), calls=%async_computation.2 | async-start | bytes 12582912 | tf_op jit(solution)/shard_map/all_gather | solution.py:81
  7.3 347.1 %all-gather.11.cloned.1.call-start = ((), (), s32[]{:S(2)}) async-start(), calls=%async_computation.5 | async-start | bytes 8912896 | tf_op jit(solution)/shard_map/all_gather | solution.py:85
  8.0 489.1 %all-gather.9.cloned.1.call-start = ((), (), s32[]{:S(2)}) async-start(), calls=%async_computation.4 | async-start | bytes 8912896 | tf_op jit(solution)/shard_map/all_gather | solution.py:84
  8.7 1158.0 %all-gather.7.cloned.1.call-start = ((), (), s32[]{:S(2)}) async-start(), calls=%async_computation.3 | async-start | bytes 71303168 | tf_op jit(solution)/shard_map/all_gather | solution.py:83
  44.8 5.4 copy-start.6
  44.8 462.8 %all-to-all-start.1 = ((bf16[16,12,2,128,128]{4,3,2,1,0:T(8,128)(2,1)}), bf16[16,12,2,128,128]{4,3,2,1,0:T(8,128)(2,1)}, u32[]{:S(2)}, u32[]{:S(2)}) async-start(bf16[16,12,2,128,128]{4,3,2,1,0:T(8,128)(2,1)} %broadcast_select_fusion), calls=%async_computation.1 | async-start | bytes 25165824 | tf_op jit(solution)/shard_map/all_to_all | solution.py:107
  1268.4 3.2 copy-start.2
  1274.3 21.4 %copy-start.3 = (bf16[4,128,4,128]{3,2,1,0:T(4,128)(2,1)S(1)}, bf16[4,128,4,128]{3,2,1,0:T(4,128)(2,1)}, u32[]{:S(2)}) copy-start(bf16[4,128,4,128]{3,2,1,0:T(4,128)(2,1)} %reshape.263) | copy-start | bytes 1572868
  1305.0 45.2 %copy-start.1 = (bf16[4,8,2,128,128]{4,3,2,1,0:T(8,128)(2,1)S(1)}, bf16[4,8,2,128,128]{4,3,2,1,0:T(8,128)(2,1)}, u32[]{:S(2)}) copy-start(bf16[4,8,2,128,128]{4,3,2,1,0:T(8,128)(2,1)} %param.12) | copy-start | bytes 6291460
Sparse Core Ops, SparseCore 0:
  8.9 22.5 all-gather.4
  34.3 320.0 all-gather.10
  357.1 139.9 all-gather.8
  499.8 666.9 all-gather.6
where the time goes:
time: 1360 us
  waiting for transfers between devices  1080 us (79%)
  matrix products  137 us (10%)
  local copies, waits for them, and re-layouts  59.6 us (4%)
  other arithmetic  49.8 us (4%)
  blocking collectives  15.4 us (1%)
    all_gather x1, waiting for transfers between devices, per_device(): lax.all_gather(w_query, 'ctx', axis=0, tiled=True)  639 us
    all_gather x1, waiting for transfers between devices, per_device(): lax.all_gather(value_weight, 'ctx', axis=0, tiled=True)  303 us
    all_gather x1, waiting for transfers between devices, per_device(): lax.all_gather(key_weight, 'ctx', axis=0, tiled=True)  132 us
    reshape x1, matrix products, per_device(): query_proj.reshape(tok_rows, query_heads, head_dim)  43.6 us
    dot_general x1, matrix products, attend(): jnp.einsum('bhgisk,hbskd->bihgd', far_prob, selected[:, :, :, 1], preferr...  30.1 us
    dot_general x1, matrix products, attend(): jnp.einsum('bihgd,hbskd->bhgisk', query, selected[:, :, :, 0], preferred_...  27.8 us
  transfers between devices with their start and end apart: 5, of which 3 were waited for; matrix products, arithmetic and copies ran while one was open for 5% of the time, Pallas kernels for 0%

commit v1 on v0

--- a/solution.py
+++ b/solution.py
@@ -1,6 +1,10 @@
+import functools
+
 import jax
 import jax.numpy as jnp
 from jax import lax
+from jax.experimental import pallas as pl
+from jax.experimental.pallas import tpu as pltpu
 from jax.sharding import PartitionSpec as P
 
 rope_base = 500000.0
@@ -130,9 +134,243 @@
     return mixed.astype(jnp.bfloat16).reshape(tok_rows, query_heads * head_dim)
 
 
+def swap(values, mask):
+    pairs = [(i, i ^ mask) for i in range(lax.axis_size("ctx"))]
+    return lax.ppermute(values, "ctx", pairs)
+
+
+def project_kernel(rotated, order, *refs):
+    own, other, pieces = refs[0:4], refs[4:8], refs[8:16]
+    cosine, sine, out, total, piece = refs[16:]
+    step = pl.program_id(0)
+    rows = own[0].shape[0]
+
+    @pl.when(step == 0)
+    def _():
+        total[...] = jnp.zeros_like(total)
+
+    for number in range(8):
+
+        @pl.when(step == number)
+        def _(number=number):
+            piece[...] = pieces[number][...]
+
+    def add(parts):
+        for number in range(4):
+            total[pl.ds(number * rows, rows), :] += jnp.dot(
+                parts[number][...], piece[...], preferred_element_type=jnp.float32
+            )
+
+    @pl.when(order[16 + step] == 1)
+    def _():
+        add(own)
+
+    @pl.when(order[16 + step] == 0)
+    def _():
+        add(other)
+
+    @pl.when(step == 7)
+    def _():
+        for number, turn in enumerate(rotated):
+            columns = pl.ds(number * 128, 128)
+            value = total[:, columns]
+            if turn:
+                value = value * cosine[...] + pltpu.roll(value, 64, 1) * sine[...]
+            out[:, columns] = value.astype(out.dtype)
+
+
+def project(order, own, other, pieces, cosine, sine, rotated):
+    rows, depth, width = own[0].shape[0], pieces[0].shape[0], pieces[0].shape[1]
+    whole = lambda shape: pl.BlockSpec(shape, lambda s, o: (0, 0))
+    return pl.pallas_call(
+        functools.partial(project_kernel, rotated),
+        out_shape=jax.ShapeDtypeStruct((4 * rows, width), jnp.bfloat16),
+        grid_spec=pltpu.PrefetchScalarGridSpec(
+            num_scalar_prefetch=1,
+            grid=(8,),
+            in_specs=[pl.BlockSpec((rows, depth), lambda s, o: (0, o[s]))] * 4
+            + [pl.BlockSpec((rows, depth), lambda s, o: (0, o[8 + s]))] * 4
+            + [whole((depth, width))] * 8
+            + [whole(cosine.shape)] * 2,
+            out_specs=whole((4 * rows, width)),
+            scratch_shapes=[
+                pltpu.VMEM((4 * rows, width), jnp.float32),
+                pltpu.VMEM((depth, width), jnp.bfloat16),
+            ],
+        ),
+        compiler_params=pltpu.CompilerParams(vmem_limit_bytes=48 * 1024 * 1024),
+        cost_estimate=pl.CostEstimate(
+            flops=2 * 4 * rows * 8 * depth * width,
+            bytes_accessed=2 * 4 * rows * 8 * depth + 2 * 8 * depth * width,
+            transcendentals=0,
+        ),
+    )(order, *own, *other, *pieces, cosine, sine)
+
+
+def attend_kernel(chosen, alive, query, fresh, cache, out):
+    block = pl.program_id(0)
+    tokens, heads, slots = query.shape[0], query.shape[1] // 128, 8
+    scaling = 1.4426950408889634 / 128.0**0.5
+    stacked = jnp.concatenate([query[:, pl.ds(h * 128, 128)] for h in range(heads)], axis=0)
+    places = [chosen[block * slots + s] for s in range(slots)]
+    keys = jnp.concatenate([cache[p, 0] for p in places] + [fresh[:, pl.ds(0, 128)]], axis=0)
+    values = jnp.concatenate([cache[p, 1] for p in places] + [fresh[:, pl.ds(128, 128)]], axis=0)
+    scores = lax.dot_general(
+        stacked, keys, (((1,), (1,)), ((), ())), preferred_element_type=jnp.float32
+    )
+    parts = [
+        jnp.where(alive[block * slots + s] > 0, scores[:, s * 128 : (s + 1) * 128], neg_fill)
+        for s in range(slots)
+    ]
+    row = lax.rem(lax.broadcasted_iota(jnp.int32, (heads * tokens, tokens), 0), tokens)
+    column = lax.broadcasted_iota(jnp.int32, (heads * tokens, tokens), 1)
+    parts.append(jnp.where(row >= column, scores[:, slots * 128 :], neg_fill))
+    top = jnp.max(functools.reduce(jnp.maximum, parts), axis=1, keepdims=True) * scaling
+    weights = [jnp.exp2(part * scaling - top) for part in parts]
+    total = jnp.sum(functools.reduce(jnp.add, weights), axis=1, keepdims=True)
+    probs = jnp.concatenate([w.astype(jnp.bfloat16) for w in weights], axis=1)
+    mixed = jnp.dot(probs, values, preferred_element_type=jnp.float32) / total
+    for h in range(heads):
+        out[:, pl.ds(h * 128, 128)] = mixed[h * tokens : (h + 1) * tokens].astype(out.dtype)
+
+
+def attend_chunk(chosen, alive, query, fresh, cache):
+    rows, width = query.shape
+    blocks = rows // 128
+    heads = width // 128
+    return pl.pallas_call(
+        attend_kernel,
+        out_shape=jax.ShapeDtypeStruct((rows, width), jnp.bfloat16),
+        grid_spec=pltpu.PrefetchScalarGridSpec(
+            num_scalar_prefetch=2,
+            grid=(blocks,),
+            in_specs=[
+                pl.BlockSpec((128, width), lambda b, c, a: (b, 0)),
+                pl.BlockSpec((128, 256), lambda b, c, a: (b, 0)),
+                pl.BlockSpec(cache.shape, lambda b, c, a: (0, 0, 0, 0)),
+            ],
+            out_specs=pl.BlockSpec((128, width), lambda b, c, a: (b, 0)),
+        ),
+        compiler_params=pltpu.CompilerParams(vmem_limit_bytes=48 * 1024 * 1024),
+        cost_estimate=pl.CostEstimate(
+            flops=4 * rows * heads * 1152 * 128 * 2,
+            bytes_accessed=cache.size * 2 + rows * width * 4,
+            transcendentals=rows * heads * 1152,
+        ),
+    )(chosen, alive, query, fresh, cache)
+
+
+def grouped(
+    tokens,
+    w_query,
+    key_weight,
+    value_weight,
+    prefix_cache_blocks,
+    selected_owner,
+    selected_offset,
+    selected_alive_mask,
+):
+    rows, half = tokens.shape
+    heads, blocks_dev, _, block_len, head_dim = prefix_cache_blocks.shape
+    query_blocks, selections = selected_owner.shape[1:]
+    ctx_devices = lax.axis_size("ctx")
+    me = lax.axis_index("ctx")
+    x, y, z = me & 1, (me >> 1) & 1, me >> 2
+    low = z & 1
+    mine = 2 * low + x
+    group = (0, 1, 4, 5)
+    chunks = 4
+    width = w_query.shape[1] // heads // chunks
+
+    def pick(values, index):
+        return lax.dynamic_index_in_dim(values, index, 0, keepdims=False)
+
+    def route(by_head):
+        by_head = by_head.reshape((2, 2) + by_head.shape[1:])
+        kept = lax.dynamic_index_in_dim(by_head, x, 1, keepdims=False)
+        got = swap(lax.dynamic_index_in_dim(by_head, 1 - x, 1, keepdims=False), 1)
+
+        def joined(index):
+            one, two = pick(kept, index), pick(got, index)
+            return jnp.concatenate([jnp.where(x == 0, one, two), jnp.where(x == 0, two, one)], axis=0)
+
+        here, there = joined(low), joined(1 - low)
+        planes = [here, swap(there, 4), swap(here, 8), swap(there, 12)]
+        return [piece for plane in planes for piece in (plane, swap(plane, 2))]
+
+    by_head = w_query.reshape(rows, heads, chunks, width).transpose(1, 2, 0, 3)
+    fresh_weight = jnp.concatenate(
+        [key_weight.reshape(rows, heads, head_dim), value_weight.reshape(rows, heads, head_dim)], axis=2
+    ).transpose(1, 0, 2)
+
+    over_x, over_z = swap(tokens, 1), swap(tokens, 4)
+    own = [tokens, over_x, over_z, swap(over_z, 1)]
+    other = [lax.ppermute(t, "tp", [(0, 1), (1, 0)]) for t in own]
+
+    fresh_pieces = route(fresh_weight)
+    cache = jnp.concatenate(route(prefix_cache_blocks), axis=0)
+    query_pieces = [route(by_head[:, c]) for c in range(chunks)]
+
+    codes = (selected_owner * blocks_dev + selected_offset) * 2 + selected_alive_mask
+    codes = jnp.stack([pick(codes, mine)] + [swap(pick(codes, mine ^ m), (0, 1, 4, 5)[m]) for m in (1, 2, 3)])
+    codes = codes.reshape(-1)
+    alive = codes & 1
+    offset = (codes >> 1) % blocks_dev
+    owner = (codes >> 1) // blocks_dev
+    piece = ((owner >> 2) ^ z) * 2 + (((owner >> 1) & 1) ^ y)
+    chosen = (piece * 2 + (owner & 1)) * blocks_dev + offset
+
+    start = blocks_dev * ctx_devices * block_len
+    positions = jnp.concatenate(
+        [start + (me ^ m) * rows + jnp.arange(rows, dtype=jnp.int32) for m in group]
+    )
+    steps = jnp.arange(head_dim // 2).astype(jnp.float32)
+    inverse = jnp.power(jnp.float32(rope_base), -2.0 * steps / head_dim)
+    angle = positions.astype(jnp.float32)[:, None] * inverse[None, :]
+    cosine, sine = jnp.cos(angle), jnp.sin(angle)
+    cosine = jnp.concatenate([cosine, cosine], axis=1)
+    sine = jnp.concatenate([-sine, sine], axis=1)
+
+    place = jnp.arange(8, dtype=jnp.int32)
+    column = (((place >> 1) ^ z) * 2 + ((place & 1) ^ y)) & 3
+    early, late = column[jnp.minimum(place, 3)], column[jnp.maximum(place, 4)]
+    own_first = lax.axis_index("tp") == (z >> 1)
+    order = jnp.concatenate(
+        [
+            jnp.where(own_first, early, late),
+            jnp.where(own_first, late, early),
+            ((place < 4) == own_first).astype(jnp.int32),
+        ]
+    )
+
+    fresh = project(order, own, other, fresh_pieces, cosine, sine, (True, False))
+    out = jnp.zeros((rows, heads * chunks * width), tokens.dtype)
+    for c in range(chunks):
+        query = project(order, own, other, query_pieces[c], cosine, sine, (True,) * (width // head_dim))
+        mixed = attend_chunk(chosen, alive, query, fresh, cache).reshape(4, rows, width)
+        for m in range(4):
+            part = swap(mixed[m], group[m]) if m else mixed[0]
+            out = lax.dynamic_update_slice(out, part, (0, ((mine ^ m) * chunks + c) * width))
+    return out
+
+
 def solution(mesh):
+    def per_shard(*args):
+        tokens, w_query, cache = args[0], args[1], args[4]
+        fits = (
+            mesh.shape["ctx"] == 16
+            and mesh.shape["tp"] == 2
+            and cache.shape[0] == 4
+            and cache.shape[3] == 128
+            and cache.shape[4] == 128
+            and w_query.shape[1] == 4096
+            and tokens.shape == (512, 4096)
+            and args[5].shape[2] == 8
+        )
+        return grouped(*args) if fits else per_device(*args)
+
     return jax.shard_map(
-        per_device,
+        per_shard,
         mesh=mesh,
         in_specs=(
             P("ctx", "tp"),

time: 1360 us -> 909 us (0.67)
  waiting for transfers between devices: 1080 us -> 529 us
  Pallas kernels: 0 us -> 169 us
  matrix products: 137 us -> 0 us
  starting transfers between devices: 5.36 us -> 125 us
  other arithmetic: 49.8 us -> 21.5 us
  blocking collectives: 15.4 us -> 0 us
    all_gather x4 -> x0, waiting for transfers between devices: 1070 us -> none  [the longest x1 639 us: per_device(): lax.all_gather(w_query, 'ctx', axis=0, tiled=True)]
    ppermute x0 -> x70, waiting for transfers between devices: none -> 529 us  [the longest x66 529 us: swap(): return lax.ppermute(values, 'ctx', pairs)]
    pallas_call x0 -> x9, Pallas kernels: none -> 169 us  [the longest x5 98.5 us: project(): pl.pallas_call(functools.partial(project_kernel, rotated), out_shape=jax....]
    ppermute x0 -> x70, starting transfers between devices: none -> 125 us  [the longest x66 124 us: swap(): return lax.ppermute(values, 'ctx', pairs)]
    dot_general x7 -> x0, matrix products: 93.3 us -> none  [the longest x1 30.1 us: attend(): jnp.einsum('bhgisk,hbskd->bihgd', far_prob, selected[:, :, :, 1], preferr...]
    reshape x1 -> x0, matrix products: 43.6 us -> none  [per_device(): query_proj.reshape(tok_rows, query_heads, head_dim)]
    reduce_sum x3 -> x0, other arithmetic: 24.3 us -> none  [the longest x2 24 us: attend(): denominator = jnp.sum(far_exp, axis=(4, 5)) + jnp.sum(near_exp, axis=4)]
    gather x2, local copies, waits for them, and re-layouts: 21.2 us -> 1.29 us  [grouped(): early, late = (column[jnp.minimum(place, 3)], column[jnp.maximum(place, 4)])]
  transfers between devices with their start and end apart: 5 -> 70, of which waited for: 3 -> 27; matrix products, arithmetic and copies ran while one was open for 5% -> 8% of each run, Pallas kernels for 0% -> 19%
where the time goes in v1:
time: 909 us; the launch traced here: 906 us
  waiting for transfers between devices  529 us (58%)
  Pallas kernels  169 us (19%)
  starting transfers between devices  125 us (14%)
  local copies, waits for them, and re-layouts  60.9 us (7%)
  other arithmetic  21.5 us (2%)
    ppermute x66, waiting for transfers between devices, swap(): return lax.ppermute(values, 'ctx', pairs)  529 us
    ppermute x66, starting transfers between devices, swap(): return lax.ppermute(values, 'ctx', pairs)  124 us
    pallas_call x5, Pallas kernels, project(): pl.pallas_call(functools.partial(project_kernel, rotated), out_shape=jax....  98.5 us
    pallas_call x4, Pallas kernels, attend_chunk(): pl.pallas_call(attend_kernel, out_shape=jax.ShapeDtypeStruct((rows, width...  70.4 us
    unnamed x68, local copies, waits for them, and re-layouts  19.5 us
  transfers between devices with their start and end apart: 70, of which 27 were waited for; matrix products, arithmetic and copies ran while one was open for 8% of the time, Pallas kernels for 19%

profile of v1, /device:TPU:0, one launch (start us, length us, event | category | flops | bytes accessed | tf_op | source)
XLA Modules:
  0.0 906.0 jit_solution(123288244877229209)
XLA Ops:
  0.0 3.0 collective-permute-start.4
  3.0 7.8 reshape.125
  10.8 14.6 %fusion.5 = (bf16[4,1,512,256]{3,1,0,2:T(2,128)(2,1)S(1)}, bf16[4,1,512,256]{3,1,0,2:T(2,128)(2,1)}, bf16[4,1,512,256]{3,1,0,2:T(2,128)(2,1)}, bf16[4,1,512,256]{3,1,0,2:T(2,128)(2,1)S(1)}) fusion(bf16[4,4,512,256]{3,1,0,2:T(4,128)(2,1)} %bitcast.110), kind=kLoop, calls=%fused_computation.107 | loop fusion | bytes 8388608 | tf_op jit(solution)/shard_map/slice | solution.py:312
  42.7 8.9 collective-permute-done
  53.0 41.0 %collective-permute-done.1 = s32[4,8]{1,0:T(4,128)S(1)} collective-permute-done((s32[4,8]{1,0:T(4,128)S(1)}, s32[4,8]{1,0:T(4,128)S(1)}, u32[]{:S(2)}, u32[]{:S(2)}) %collective-permute-start.1) | collective-permute-done | bytes 160 | tf_op jit(solution)/shard_map/ppermute | solution.py:139
  102.0 7.2 collective-permute-done.37
  110.9 9.5 %collective-permute-done.48 = bf16[2,512,256]{2,1,0:T(8,128)(2,1)} collective-permute-done((bf16[2,512,256]{2,1,0:T(8,128)(2,1)}, bf16[2,512,256]{2,1,0:T(8,128)(2,1)}, u32[]{:S(2)}, u32[]{:S(2)}) %collective-permute-start.48) | collective-permute-done | bytes 524320 | tf_op jit(solution)/shard_map/ppermute | solution.py:139
  120.4 2.8 collective-permute-start.14
  123.2 186.4 %collective-permute-done.59 = bf16[2,512,256]{2,1,0:T(8,128)(2,1)} collective-permute-done((bf16[2,512,256]{2,1,0:T(8,128)(2,1)S(1)}, bf16[2,512,256]{2,1,0:T(8,128)(2,1)}, u32[]{:S(2)}, u32[]{:S(2)}) %collective-permute-start.59) | collective-permute-done | bytes 524320 | tf_op jit(solution)/shard_map/ppermute | solution.py:139
  311.0 3.6 collective-permute-start.16
  317.3 7.2 collective-permute-done.16.refs_14_
  324.5 10.8 %collective-permute-start.20 = (bf16[1024,256]{1,0:T(8,128)(2,1)S(1)}, bf16[1024,256]{1,0:T(8,128)(2,1)S(1)}, u32[]{:S(2)}, u32[]{:S(2)}) collective-permute-start(bf16[1024,256]{1,0:T(8,128)(2,1)S(1)} %pad_maximum_fusion.7), channel_id=1, source_target_pairs={{0,8},{2,10},{4,12},{6,14},{8,0},{10,2},{12,4},{14,6},{16,24},{18,... | collective-permute-start | bytes 1572872 | tf_op jit(solution)/shard_map/ppermute | solution.py:139
  340.4 15.7 %collective-permute-done.20.refs_10_ = bf16[1024,256]{1,0:T(8,128)(2,1)S(1)} collective-permute-done((bf16[1024,256]{1,0:T(8,128)(2,1)S(1)}, bf16[1024,256]{1,0:T(8,128)(2,1)S(1)}, u32[]{:S(2)}, u32[]{:S(2)}) %collective-permute-start.20) | collective-permute-done | bytes 524320 | tf_op jit(solution)/shard_map/ppermute | solution.py:139
  357.7 16.0 %collective-permute-done.22.refs_12_ = bf16[1024,256]{1,0:T(8,128)(2,1)S(1)} collective-permute-done((bf16[1024,256]{1,0:T(8,128)(2,1)S(1)}, bf16[1024,256]{1,0:T(8,128)(2,1)S(1)}, u32[]{:S(2)}, u32[]{:S(2)}) %collective-permute-start.22) | collective-permute-done | bytes 524320 | tf_op jit(solution)/shard_map/ppermute | solution.py:139
  380.0 3.7 collective-permute-done.39.refs_10_
  386.3 23.1 %collective-permute-done.13.refs_11_ = bf16[1024,256]{1,0:T(8,128)(2,1)S(1)} collective-permute-done((bf16[1024,256]{1,0:T(8,128)(2,1)S(1)}, bf16[1024,256]{1,0:T(8,128)(2,1)S(1)}, u32[]{:S(2)}, u32[]{:S(2)}) %collective-permute-start.13) | collective-permute-done | bytes 524320 | tf_op jit(solution)/shard_map/ppermute | solution.py:139
  410.3 11.4 %collective-permute-start.28 = (bf16[16,2,128,128]{3,2,1,0:T(8,128)(2,1)}, bf16[16,2,128,128]{3,2,1,0:T(8,128)(2,1)}, u32[]{:S(2)}, u32[]{:S(2)}) collective-permute-start(bf16[16,2,128,128]{3,2,1,0:T(8,128)(2,1)} %pad_maximum_fusion.3), channel_id=1, source_target_pairs={{0,8},{2,10},{4,12},{6,14},{8,0},{10,2},{12,4},{14,6},{16,24},{18,... | collective-permute-start | bytes 3145736 | tf_op jit(solution)/shard_map/ppermute | solution.py:139
  422.5 6.3 collective-permute-start.30
  429.8 3.4 collective-permute-start.32
  433.2 18.5 %collective-permute-done.28 = bf16[16,2,128,128]{3,2,1,0:T(8,128)(2,1)} collective-permute-done((bf16[16,2,128,128]{3,2,1,0:T(8,128)(2,1)}, bf16[16,2,128,128]{3,2,1,0:T(8,128)(2,1)}, u32[]{:S(2)}, u32[]{:S(2)}) %collective-permute-start.28) | collective-permute-done | bytes 1048608 | tf_op jit(solution)/shard_map/ppermute | solution.py:139
  451.7 46.2 %collective-permute-done.30 = bf16[16,2,128,128]{3,2,1,0:T(8,128)(2,1)} collective-permute-done((bf16[16,2,128,128]{3,2,1,0:T(8,128)(2,1)}, bf16[16,2,128,128]{3,2,1,0:T(8,128)(2,1)}, u32[]{:S(2)}, u32[]{:S(2)}) %collective-permute-start.30) | collective-permute-done | bytes 1048608 | tf_op jit(solution)/shard_map/ppermute | solution.py:139
  501.6 3.7 fusion
  505.4 20.5 %collective-permute-done.29 = bf16[16,2,128,128]{3,2,1,0:T(8,128)(2,1)} collective-permute-done((bf16[16,2,128,128]{3,2,1,0:T(8,128)(2,1)}, bf16[16,2,128,128]{3,2,1,0:T(8,128)(2,1)}, u32[]{:S(2)}, u32[]{:S(2)}) %collective-permute-start.29) | collective-permute-done | bytes 1048608 | tf_op jit(solution)/shard_map/ppermute | solution.py:139
  532.7 18.2 %collective-permute-done.31 = bf16[16,2,128,128]{3,2,1,0:T(8,128)(2,1)} collective-permute-done((bf16[16,2,128,128]{3,2,1,0:T(8,128)(2,1)}, bf16[16,2,128,128]{3,2,1,0:T(8,128)(2,1)}, u32[]{:S(2)}, u32[]{:S(2)}) %collective-permute-start.31) | collective-permute-done | bytes 1048608 | tf_op jit(solution)/shard_map/ppermute | solution.py:139
  559.7 15.2 %collective-permute-done.33 = bf16[16,2,128,128]{3,2,1,0:T(8,128)(2,1)S(1)} collective-permute-done((bf16[16,2,128,128]{3,2,1,0:T(8,128)(2,1)}, bf16[16,2,128,128]{3,2,1,0:T(8,128)(2,1)S(1)}, u32[]{:S(2)}, u32[]{:S(2)}) %collective-permute-start.33) | collective-permute-done | bytes 1048608 | tf_op jit(solution)/shard_map/ppermute | solution.py:139
  586.6 3.6 collective-permute-start.43
  590.2 13.2 %collective-permute-start.41 = (bf16[1024,256]{1,0:T(8,128)(2,1)S(1)}, bf16[1024,256]{1,0:T(8,128)(2,1)S(1)}, u32[]{:S(2)}, u32[]{:S(2)}) collective-permute-start(bf16[1024,256]{1,0:T(8,128)(2,1)S(1)} %pad_maximum_fusion.8.refs_8_), channel_id=1, source_target_pairs={{0,16},{2,18},{4,20},{6,22},{8,24},{10,26},{12,28},{14,30},{16,0},... | collective-permute-start | bytes 1572872 | tf_op jit(solution)/shard_map/ppermute | solution.py:139
  606.9 19.8 %shard_map.82.query = bf16[2048,256]{1,0:T(8,128)(2,1)S(1)} custom-call(s32[24]{0:T(128)S(1)} %pad_add_fusion.1.order, bf16[512,4096]{1,0:T(8,128)(2,1)} %refs_0_.9, bf16[512,4096]{1,0:T(8,128)(2,1)} %collective-permute-done.3.refs_1_, bf16[512,4096]{1,0:T(8,128)(2,1)} %collective-permute-done.4.refs_2_, bf16[512,4096]{1,0:T(8,128)(2,1)} %collective-permute-done.5.refs_3_, ...), custom_call_target="tpu_custom_call" | custom-call | flops 8589934592 | bytes 37748736 | tf_op jit(solution)/shard_map/pallas_call | solution.py:185
  626.7 6.2 collective-permute-done.41.refs_12_
  637.7 19.5 %shard_map.83.fresh = bf16[2048,256]{1,0:T(8,128)(2,1)S(1)} custom-call(s32[24]{0:T(128)S(1)} %pad_add_fusion.1.order, bf16[512,4096]{1,0:T(8,128)(2,1)} %refs_0_.9, bf16[512,4096]{1,0:T(8,128)(2,1)} %collective-permute-done.3.refs_1_, bf16[512,4096]{1,0:T(8,128)(2,1)} %collective-permute-done.4.refs_2_, bf16[512,4096]{1,0:T(8,128)(2,1)} %collective-permute-done.5.refs_3_, ...), custom_call_target="tpu_custom_call" | custom-call | flops 8589934592 | bytes 37748736 | tf_op jit(solution)/shard_map/pallas_call | solution.py:185
  657.2 2.6 collective-permute-start.54
  660.4 9.8 %collective-permute-done.42.refs_13_ = bf16[1024,256]{1,0:T(8,128)(2,1)S(1)} collective-permute-done((bf16[1024,256]{1,0:T(8,128)(2,1)S(1)}, bf16[1024,256]{1,0:T(8,128)(2,1)S(1)}, u32[]{:S(2)}, u32[]{:S(2)}) %collective-permute-start.42) | collective-permute-done | bytes 524320 | tf_op jit(solution)/shard_map/ppermute | solution.py:139
  671.7 9.7 %collective-permute-done.44.refs_15_ = bf16[1024,256]{1,0:T(8,128)(2,1)S(1)} collective-permute-done((bf16[1024,256]{1,0:T(8,128)(2,1)S(1)}, bf16[1024,256]{1,0:T(8,128)(2,1)S(1)}, u32[]{:S(2)}, u32[]{:S(2)}) %collective-permute-start.44) | collective-permute-done | bytes 524320 | tf_op jit(solution)/shard_map/ppermute | solution.py:139
  682.1 19.8 %shard_map.85.query = bf16[2048,256]{1,0:T(8,128)(2,1)S(1)} custom-call(s32[24]{0:T(128)S(1)} %pad_add_fusion.1.order, bf16[512,4096]{1,0:T(8,128)(2,1)} %refs_0_.9, bf16[512,4096]{1,0:T(8,128)(2,1)} %collective-permute-done.3.refs_1_, bf16[512,4096]{1,0:T(8,128)(2,1)} %collective-permute-done.4.refs_2_, bf16[512,4096]{1,0:T(8,128)(2,1)} %collective-permute-done.5.refs_3_, ...), custom_call_target="tpu_custom_call" | custom-call | flops 8589934592 | bytes 37748736 | tf_op jit(solution)/shard_map/pallas_call | solution.py:185
  704.4 23.0 %collective-permute-done.52.refs_12_ = bf16[1024,256]{1,0:T(8,128)(2,1)S(1)} collective-permute-done((bf16[1024,256]{1,0:T(8,128)(2,1)S(1)}, bf16[1024,256]{1,0:T(8,128)(2,1)S(1)}, u32[]{:S(2)}, u32[]{:S(2)}) %collective-permute-start.52) | collective-permute-done | bytes 524320 | tf_op jit(solution)/shard_map/ppermute | solution.py:139
  731.0 17.8 %shard_map.84 = bf16[2048,256]{1,0:T(8,128)(2,1)S(1)} custom-call(s32[128]{0:T(128)S(1)} %fusion.4.chosen, s32[128]{0:T(128)S(1)} %and.46.alive, bf16[2048,256]{1,0:T(8,128)(2,1)S(1)} %shard_map.82.query, bf16[2048,256]{1,0:T(8,128)(2,1)S(1)} %shard_map.83.fresh, bf16[128,2,128,128]{3,2,1,0:T(8,128)(2,1)} %constant_dynamic-update-slice_fusion.cache), custom_call_target="tpu_custom_call" | custom-call | flops 4831838208 | bytes 10485760 | tf_op jit(solution)/shard_map/pallas_call | solution.py:241
  755.0 9.7 %collective-permute-done.55.refs_15_ = bf16[1024,256]{1,0:T(8,128)(2,1)S(1)} collective-permute-done((bf16[1024,256]{1,0:T(8,128)(2,1)S(1)}, bf16[1024,256]{1,0:T(8,128)(2,1)S(1)}, u32[]{:S(2)}, u32[]{:S(2)}) %collective-permute-start.55) | collective-permute-done | bytes 524320 | tf_op jit(solution)/shard_map/ppermute | solution.py:139
  765.1 19.8 %shard_map.87.query = bf16[2048,256]{1,0:T(8,128)(2,1)S(1)} custom-call(s32[24]{0:T(128)S(1)} %pad_add_fusion.1.order, bf16[512,4096]{1,0:T(8,128)(2,1)} %refs_0_.9, bf16[512,4096]{1,0:T(8,128)(2,1)} %collective-permute-done.3.refs_1_, bf16[512,4096]{1,0:T(8,128)(2,1)} %collective-permute-done.4.refs_2_, bf16[512,4096]{1,0:T(8,128)(2,1)} %collective-permute-done.5.refs_3_, ...), custom_call_target="tpu_custom_call" | custom-call | flops 8589934592 | bytes 37748736 | tf_op jit(solution)/shard_map/pallas_call | solution.py:185
  788.0 10.4 %collective-permute-done.66.refs_15_ = bf16[1024,256]{1,0:T(8,128)(2,1)S(1)} collective-permute-done((bf16[1024,256]{1,0:T(8,128)(2,1)S(1)}, bf16[1024,256]{1,0:T(8,128)(2,1)S(1)}, u32[]{:S(2)}, u32[]{:S(2)}) %collective-permute-start.66) | collective-permute-done | bytes 524320 | tf_op jit(solution)/shard_map/ppermute | solution.py:139
  798.4 10.2 %collective-permute-done.64.refs_13_ = bf16[1024,256]{1,0:T(8,128)(2,1)S(1)} collective-permute-done((bf16[1024,256]{1,0:T(8,128)(2,1)S(1)}, bf16[1024,256]{1,0:T(8,128)(2,1)S(1)}, u32[]{:S(2)}, u32[]{:S(2)}) %collective-permute-start.64) | collective-permute-done | bytes 524320 | tf_op jit(solution)/shard_map/ppermute | solution.py:139
  808.6 19.8 %shard_map.89.query = bf16[2048,256]{1,0:T(8,128)(2,1)S(1)} custom-call(s32[24]{0:T(128)S(1)} %pad_add_fusion.1.order, bf16[512,4096]{1,0:T(8,128)(2,1)} %refs_0_.9, bf16[512,4096]{1,0:T(8,128)(2,1)} %collective-permute-done.3.refs_1_, bf16[512,4096]{1,0:T(8,128)(2,1)} %collective-permute-done.4.refs_2_, bf16[512,4096]{1,0:T(8,128)(2,1)} %collective-permute-done.5.refs_3_, ...), custom_call_target="tpu_custom_call" | custom-call | flops 8589934592 | bytes 37748736 | tf_op jit(solution)/shard_map/pallas_call | solution.py:185
  828.4 17.6 %shard_map.86 = bf16[2048,256]{1,0:T(8,128)(2,1)S(1)} custom-call(s32[128]{0:T(128)S(1)} %fusion.4.chosen, s32[128]{0:T(128)S(1)} %and.46.alive, bf16[2048,256]{1,0:T(8,128)(2,1)S(1)} %shard_map.85.query, bf16[2048,256]{1,0:T(8,128)(2,1)S(1)} %shard_map.83.fresh, bf16[128,2,128,128]{3,2,1,0:T(8,128)(2,1)} %constant_dynamic-update-slice_fusion.cache), custom_call_target="tpu_custom_call" | custom-call | flops 4831838208 | bytes 10485760 | tf_op jit(solution)/shard_map/pallas_call | solution.py:241
  847.5 3.1 collective-permute-start.47
  850.7 17.5 %shard_map.88 = bf16[2048,256]{1,0:T(8,128)(2,1)S(1)} custom-call(s32[128]{0:T(128)S(1)} %fusion.4.chosen, s32[128]{0:T(128)S(1)} %and.46.alive, bf16[2048,256]{1,0:T(8,128)(2,1)S(1)} %shard_map.87.query, bf16[2048,256]{1,0:T(8,128)(2,1)S(1)} %shard_map.83.fresh, bf16[128,2,128,128]{3,2,1,0:T(8,128)(2,1)} %constant_dynamic-update-slice_fusion.cache), custom_call_target="tpu_custom_call" | custom-call | flops 4831838208 | bytes 10485760 | tf_op jit(solution)/shard_map/pallas_call | solution.py:241
  869.1 2.9 collective-permute-start.58
  872.0 17.5 %shard_map.90 = bf16[2048,256]{1,0:T(8,128)(2,1)S(1)} custom-call(s32[128]{0:T(128)S(1)} %fusion.4.chosen, s32[128]{0:T(128)S(1)} %and.46.alive, bf16[2048,256]{1,0:T(8,128)(2,1)S(1)} %shard_map.89.query, bf16[2048,256]{1,0:T(8,128)(2,1)S(1)} %shard_map.83.fresh, bf16[128,2,128,128]{3,2,1,0:T(8,128)(2,1)} %constant_dynamic-update-slice_fusion.cache), custom_call_target="tpu_custom_call" | custom-call | flops 4831838208 | bytes 10485760 | tf_op jit(solution)/shard_map/pallas_call | solution.py:241
  893.2 2.9 collective-permute-start.69
  896.1 5.9 collective-permute-done.67
  (244 shorter events, 117.8 us)
Async XLA Ops:
  0.0 97.6 %collective-permute-start.4 = (bf16[512,4096]{1,0:T(8,128)(2,1)}, bf16[512,4096]{1,0:T(8,128)(2,1)}, u32[]{:S(2)}, u32[]{:S(2)}) collective-permute-start(bf16[512,4096]{1,0:T(8,128)(2,1)} %refs_0_.9), channel_id=1, source_target_pairs={{0,8},{2,10},{4,12},{6,14},{8,0},{10,2},{12,4},{14,6},{16,24},{18,... | collective-permute-start | bytes 12582920 | tf_op jit(solution)/shard_map/ppermute | solution.py:139
  26.6 69.4 %collective-permute-start.10 = (bf16[2,512,256]{2,1,0:T(8,128)(2,1)}, bf16[2,512,256]{2,1,0:T(8,128)(2,1)}, u32[]{:S(2)}, u32[]{:S(2)}) collective-permute-start(bf16[2,512,256]{2,1,0:T(8,128)(2,1)} %dynamic-slice_bitcast_fusion.5), channel_id=1, source_target_pairs={{0,2},{2,0},{4,6},{6,4},{8,10},{10,8},{12,14},{14,12},{16,18},{18,... | collective-permute-start | bytes 1572872 | tf_op jit(solution)/shard_map/ppermute | solution.py:139
  35.8 64.4 %collective-permute-start.18 = (bf16[2,512,256]{2,1,0:T(8,128)(2,1)}, bf16[2,512,256]{2,1,0:T(8,128)(2,1)}, u32[]{:S(2)}, u32[]{:S(2)}) collective-permute-start(bf16[2,512,256]{2,1,0:T(8,128)(2,1)} %dynamic-slice_bitcast_fusion.4), channel_id=1, source_target_pairs={{0,2},{2,0},{4,6},{6,4},{8,10},{10,8},{12,14},{14,12},{16,18},{18,... | collective-permute-start | bytes 1572872 | tf_op jit(solution)/shard_map/ppermute | solution.py:139
  38.0 56.0 %collective-permute-start.1 = (s32[4,8]{1,0:T(4,128)S(1)}, s32[4,8]{1,0:T(4,128)S(1)}, u32[]{:S(2)}, u32[]{:S(2)}) collective-permute-start(s32[4,8]{1,0:T(4,128)S(1)} %get-tuple-element.58), channel_id=1, source_target_pairs={{0,8},{2,10},{4,12},{6,14},{8,0},{10,2},{12,4},{14,6},{16,24},{18,... | collective-permute-start | bytes 392 | tf_op jit(solution)/shard_map/ppermute | solution.py:139
  51.6 44.0 %collective-permute-start.2 = (s32[4,8]{1,0:T(4,128)S(1)}, s32[4,8]{1,0:T(4,128)S(1)}, u32[]{:S(2)}, u32[]{:S(2)}) collective-permute-start(s32[4,8]{1,0:T(4,128)S(1)} %get-tuple-element.57), channel_id=1, source_target_pairs={{0,10},{2,8},{4,14},{6,12},{8,2},{10,0},{12,6},{14,4},{16,26},{18,... | collective-permute-start | bytes 392 | tf_op jit(solution)/shard_map/ppermute | solution.py:139
  96.0 402.0 %collective-permute-start.3 = (bf16[512,4096]{1,0:T(8,128)(2,1)}, bf16[512,4096]{1,0:T(8,128)(2,1)}, u32[]{:S(2)}, u32[]{:S(2)}) collective-permute-start(bf16[512,4096]{1,0:T(8,128)(2,1)} %refs_0_.9), channel_id=1, source_target_pairs={{0,2},{2,0},{4,6},{6,4},{8,10},{10,8},{12,14},{14,12},{16,18},{18,... | collective-permute-start | bytes 12582920 | tf_op jit(solution)/shard_map/ppermute | solution.py:139
  97.6 400.8 %collective-permute-start.5 = (bf16[512,4096]{1,0:T(8,128)(2,1)}, bf16[512,4096]{1,0:T(8,128)(2,1)}, u32[]{:S(2)}, u32[]{:S(2)}) collective-permute-start(bf16[512,4096]{1,0:T(8,128)(2,1)} %collective-permute-done.4.refs_2_), channel_id=1, source_target_pairs={{0,2},{2,0},{4,6},{6,4},{8,10},{10,8},{12,14},{14,12},{16,18},{18,... | collective-permute-start | bytes 12582920 | tf_op jit(solution)/shard_map/ppermute | solution.py:139
  100.2 209.4 %collective-permute-start.59 = (bf16[2,512,256]{2,1,0:T(8,128)(2,1)S(1)}, bf16[2,512,256]{2,1,0:T(8,128)(2,1)}, u32[]{:S(2)}, u32[]{:S(2)}) collective-permute-start(bf16[2,512,256]{2,1,0:T(8,128)(2,1)S(1)} %dynamic-slice_bitcast_fusion.1), channel_id=1, source_target_pairs={{0,2},{2,0},{4,6},{6,4},{8,10},{10,8},{12,14},{14,12},{16,18},{18,... | collective-permute-start | bytes 1572872 | tf_op jit(solution)/shard_map/ppermute | solution.py:139
  109.1 201.8 %collective-permute-start.12 = (bf16[1024,256]{1,0:T(8,128)(2,1)S(1)}, bf16[1024,256]{1,0:T(8,128)(2,1)S(1)}, u32[]{:S(2)}, u32[]{:S(2)}) collective-permute-start(bf16[1024,256]{1,0:T(8,128)(2,1)S(1)} %pad_maximum_fusion.5), channel_id=1, source_target_pairs={{0,8},{2,10},{4,12},{6,14},{8,0},{10,2},{12,4},{14,6},{16,24},{18,... | collective-permute-start | bytes 1572872 | tf_op jit(solution)/shard_map/ppermute | solution.py:139
  120.4 194.2 %collective-permute-start.14 = (bf16[1024,256]{1,0:T(8,128)(2,1)S(1)}, bf16[1024,256]{1,0:T(8,128)(2,1)S(1)}, u32[]{:S(2)}, u32[]{:S(2)}) collective-permute-start(bf16[1024,256]{1,0:T(8,128)(2,1)S(1)} %pad_maximum_fusion.4.refs_8_), channel_id=1, source_target_pairs={{0,16},{2,18},{4,20},{6,22},{8,24},{10,26},{12,28},{14,30},{16,0},... | collective-permute-start | bytes 1572872 | tf_op jit(solution)/shard_map/ppermute | solution.py:139
  309.6 29.4 %collective-permute-start.26 = (bf16[2,8,2,128,128]{4,3,2,1,0:T(8,128)(2,1)S(1)}, bf16[2,8,2,128,128]{4,3,2,1,0:T(8,128)(2,1)S(1)}, u32[]{:S(2)}, u32[]{:S(2)}) collective-permute-start(bf16[2,8,2,128,128]{4,3,2,1,0:T(8,128)(2,1)S(1)} %dynamic-slice_bitcast_fusion), channel_id=1, source_target_pairs={{0,2},{2,0},{4,6},{6,4},{8,10},{10,8},{12,14},{14,12},{16,18},{18,... | collective-permute-start | bytes 3145736 | tf_op jit(solution)/shard_map/ppermute | solution.py:139
  324.5 31.6 %collective-permute-start.20 = (bf16[1024,256]{1,0:T(8,128)(2,1)S(1)}, bf16[1024,256]{1,0:T(8,128)(2,1)S(1)}, u32[]{:S(2)}, u32[]{:S(2)}) collective-permute-start(bf16[1024,256]{1,0:T(8,128)(2,1)S(1)} %pad_maximum_fusion.7), channel_id=1, source_target_pairs={{0,8},{2,10},{4,12},{6,14},{8,0},{10,2},{12,4},{14,6},{16,24},{18,... | collective-permute-start | bytes 1572872 | tf_op jit(solution)/shard_map/ppermute | solution.py:139
  335.4 38.3 %collective-permute-start.22 = (bf16[1024,256]{1,0:T(8,128)(2,1)S(1)}, bf16[1024,256]{1,0:T(8,128)(2,1)S(1)}, u32[]{:S(2)}, u32[]{:S(2)}) collective-permute-start(bf16[1024,256]{1,0:T(8,128)(2,1)S(1)} %pad_maximum_fusion.6.refs_8_), channel_id=1, source_target_pairs={{0,16},{2,18},{4,20},{6,22},{8,24},{10,26},{12,28},{14,30},{16,0},... | collective-permute-start | bytes 1572872 | tf_op jit(solution)/shard_map/ppermute | solution.py:139
  339.0 38.9 %collective-permute-start.24 = (bf16[1024,256]{1,0:T(8,128)(2,1)S(1)}, bf16[1024,256]{1,0:T(8,128)(2,1)S(1)}, u32[]{:S(2)}, u32[]{:S(2)}) collective-permute-start(bf16[1024,256]{1,0:T(8,128)(2,1)S(1)} %pad_maximum_fusion.7), channel_id=1, source_target_pairs={{0,24},{2,26},{4,28},{6,30},{8,16},{10,18},{12,20},{14,22},{16,8},... | collective-permute-start | bytes 1572872 | tf_op jit(solution)/shard_map/ppermute | solution.py:139
  378.0 50.9 %collective-permute-start.27 = (bf16[16,2,128,128]{3,2,1,0:T(8,128)(2,1)}, bf16[16,2,128,128]{3,2,1,0:T(8,128)(2,1)S(1)}, u32[]{:S(2)}, u32[]{:S(2)}) collective-permute-start(bf16[16,2,128,128]{3,2,1,0:T(8,128)(2,1)} %pad_maximum_fusion.2), channel_id=1, source_target_pairs={{0,4},{2,6},{4,0},{6,2},{8,12},{10,14},{12,8},{14,10},{16,20},{18,... | collective-permute-start | bytes 3145736 | tf_op jit(solution)/shard_map/ppermute | solution.py:139
  379.5 30.0 %collective-permute-start.13 = (bf16[1024,256]{1,0:T(8,128)(2,1)S(1)}, bf16[1024,256]{1,0:T(8,128)(2,1)S(1)}, u32[]{:S(2)}, u32[]{:S(2)}) collective-permute-start(bf16[1024,256]{1,0:T(8,128)(2,1)S(1)} %collective-permute-done.12.refs_10_), channel_id=1, source_target_pairs={{0,4},{2,6},{4,0},{6,2},{8,12},{10,14},{12,8},{14,10},{16,20},{18,... | collective-permute-start | bytes 1572872 | tf_op jit(solution)/shard_map/ppermute | solution.py:139
  383.7 38.0 %collective-permute-start.15 = (bf16[1024,256]{1,0:T(8,128)(2,1)S(1)}, bf16[1024,256]{1,0:T(8,128)(2,1)S(1)}, u32[]{:S(2)}, u32[]{:S(2)}) collective-permute-start(bf16[1024,256]{1,0:T(8,128)(2,1)S(1)} %collective-permute-done.14.refs_12_), channel_id=1, source_target_pairs={{0,4},{2,6},{4,0},{6,2},{8,12},{10,14},{12,8},{14,10},{16,20},{18,... | collective-permute-start | bytes 1572872 | tf_op jit(solution)/shard_map/ppermute | solution.py:139
  410.3 41.4 %collective-permute-start.28 = (bf16[16,2,128,128]{3,2,1,0:T(8,128)(2,1)}, bf16[16,2,128,128]{3,2,1,0:T(8,128)(2,1)}, u32[]{:S(2)}, u32[]{:S(2)}) collective-permute-start(bf16[16,2,128,128]{3,2,1,0:T(8,128)(2,1)} %pad_maximum_fusion.3), channel_id=1, source_target_pairs={{0,8},{2,10},{4,12},{6,14},{8,0},{10,2},{12,4},{14,6},{16,24},{18,... | collective-permute-start | bytes 3145736 | tf_op jit(solution)/shard_map/ppermute | solution.py:139
  422.5 75.5 %collective-permute-start.30 = (bf16[16,2,128,128]{3,2,1,0:T(8,128)(2,1)}, bf16[16,2,128,128]{3,2,1,0:T(8,128)(2,1)}, u32[]{:S(2)}, u32[]{:S(2)}) collective-permute-start(bf16[16,2,128,128]{3,2,1,0:T(8,128)(2,1)} %pad_maximum_fusion.2), channel_id=1, source_target_pairs={{0,16},{2,18},{4,20},{6,22},{8,24},{10,26},{12,28},{14,30},{16,0},... | collective-permute-start | bytes 3145736 | tf_op jit(solution)/shard_map/ppermute | solution.py:139
  429.8 70.1 %collective-permute-start.32 = (bf16[16,2,128,128]{3,2,1,0:T(8,128)(2,1)}, bf16[16,2,128,128]{3,2,1,0:T(8,128)(2,1)}, u32[]{:S(2)}, u32[]{:S(2)}) collective-permute-start(bf16[16,2,128,128]{3,2,1,0:T(8,128)(2,1)} %pad_maximum_fusion.3), channel_id=1, source_target_pairs={{0,24},{2,26},{4,28},{6,30},{8,16},{10,18},{12,20},{14,22},{16,8},... | collective-permute-start | bytes 3145736 | tf_op jit(solution)/shard_map/ppermute | solution.py:139
  451.7 138.5 %collective-permute-start.6 = (bf16[512,4096]{1,0:T(8,128)(2,1)}, bf16[512,4096]{1,0:T(8,128)(2,1)}, u32[]{:S(2)}, u32[]{:S(2)}) collective-permute-start(bf16[512,4096]{1,0:T(8,128)(2,1)} %refs_0_.9), channel_id=1, source_target_pairs={{0,1},{1,0},{2,3},{3,2},{4,5},{5,4},{6,7},{7,6},{8,9},{9,8},{10,11... | collective-permute-start | bytes 12582920 | tf_op jit(solution)/shard_map/ppermute | solution.py:308
  498.0 105.4 %collective-permute-start.8 = (bf16[512,4096]{1,0:T(8,128)(2,1)}, bf16[512,4096]{1,0:T(8,128)(2,1)}, u32[]{:S(2)}, u32[]{:S(2)}) collective-permute-start(bf16[512,4096]{1,0:T(8,128)(2,1)} %collective-permute-done.4.refs_2_), channel_id=1, source_target_pairs={{0,1},{1,0},{2,3},{3,2},{4,5},{5,4},{6,7},{7,6},{8,9},{9,8},{10,11... | collective-permute-start | bytes 12582920 | tf_op jit(solution)/shard_map/ppermute | solution.py:308
  498.0 106.9 %collective-permute-start.7 = (bf16[512,4096]{1,0:T(8,128)(2,1)}, bf16[512,4096]{1,0:T(8,128)(2,1)}, u32[]{:S(2)}, u32[]{:S(2)}) collective-permute-start(bf16[512,4096]{1,0:T(8,128)(2,1)} %collective-permute-done.3.refs_1_), channel_id=1, source_target_pairs={{0,1},{1,0},{2,3},{3,2},{4,5},{5,4},{6,7},{7,6},{8,9},{9,8},{10,11... | collective-permute-start | bytes 12582920 | tf_op jit(solution)/shard_map/ppermute | solution.py:308
  498.5 106.9 %collective-permute-start.9 = (bf16[512,4096]{1,0:T(8,128)(2,1)}, bf16[512,4096]{1,0:T(8,128)(2,1)}, u32[]{:S(2)}, u32[]{:S(2)}) collective-permute-start(bf16[512,4096]{1,0:T(8,128)(2,1)} %collective-permute-done.5.refs_3_), channel_id=1, source_target_pairs={{0,1},{1,0},{2,3},{3,2},{4,5},{5,4},{6,7},{7,6},{8,9},{9,8},{10,11... | collective-permute-start | bytes 12582920 | tf_op jit(solution)/shard_map/ppermute | solution.py:308
  499.9 25.9 %collective-permute-start.29 = (bf16[16,2,128,128]{3,2,1,0:T(8,128)(2,1)}, bf16[16,2,128,128]{3,2,1,0:T(8,128)(2,1)}, u32[]{:S(2)}, u32[]{:S(2)}) collective-permute-start(bf16[16,2,128,128]{3,2,1,0:T(8,128)(2,1)} %collective-permute-done.28), channel_id=1, source_target_pairs={{0,4},{2,6},{4,0},{6,2},{8,12},{10,14},{12,8},{14,10},{16,20},{18,... | collective-permute-start | bytes 3145736 | tf_op jit(solution)/shard_map/ppermute | solution.py:139
  525.8 25.0 %collective-permute-start.31 = (bf16[16,2,128,128]{3,2,1,0:T(8,128)(2,1)}, bf16[16,2,128,128]{3,2,1,0:T(8,128)(2,1)}, u32[]{:S(2)}, u32[]{:S(2)}) collective-permute-start(bf16[16,2,128,128]{3,2,1,0:T(8,128)(2,1)} %collective-permute-done.30), channel_id=1, source_target_pairs={{0,4},{2,6},{4,0},{6,2},{8,12},{10,14},{12,8},{14,10},{16,20},{18,... | collective-permute-start | bytes 3145736 | tf_op jit(solution)/shard_map/ppermute | solution.py:139
  586.6 47.8 %collective-permute-start.43 = (bf16[1024,256]{1,0:T(8,128)(2,1)S(1)}, bf16[1024,256]{1,0:T(8,128)(2,1)S(1)}, u32[]{:S(2)}, u32[]{:S(2)}) collective-permute-start(bf16[1024,256]{1,0:T(8,128)(2,1)S(1)} %copy-done.27), channel_id=1, source_target_pairs={{0,24},{2,26},{4,28},{6,30},{8,16},{10,18},{12,20},{14,22},{16,8},... | collective-permute-start | bytes 1572872 | tf_op jit(solution)/shard_map/ppermute | solution.py:139
  590.2 42.7 %collective-permute-start.41 = (bf16[1024,256]{1,0:T(8,128)(2,1)S(1)}, bf16[1024,256]{1,0:T(8,128)(2,1)S(1)}, u32[]{:S(2)}, u32[]{:S(2)}) collective-permute-start(bf16[1024,256]{1,0:T(8,128)(2,1)S(1)} %pad_maximum_fusion.8.refs_8_), channel_id=1, source_target_pairs={{0,16},{2,18},{4,20},{6,22},{8,24},{10,26},{12,28},{14,30},{16,0},... | collective-permute-start | bytes 1572872 | tf_op jit(solution)/shard_map/ppermute | solution.py:139
  603.4 31.8 %collective-permute-start.21 = (bf16[1024,256]{1,0:T(8,128)(2,1)S(1)}, bf16[1024,256]{1,0:T(8,128)(2,1)S(1)}, u32[]{:S(2)}, u32[]{:S(2)}) collective-permute-start(bf16[1024,256]{1,0:T(8,128)(2,1)S(1)} %collective-permute-done.20.refs_10_), channel_id=1, source_target_pairs={{0,4},{2,6},{4,0},{6,2},{8,12},{10,14},{12,8},{14,10},{16,20},{18,... | collective-permute-start | bytes 1572872 | tf_op jit(solution)/shard_map/ppermute | solution.py:139
  604.9 30.8 %collective-permute-start.23 = (bf16[1024,256]{1,0:T(8,128)(2,1)S(1)}, bf16[1024,256]{1,0:T(8,128)(2,1)S(1)}, u32[]{:S(2)}, u32[]{:S(2)}) collective-permute-start(bf16[1024,256]{1,0:T(8,128)(2,1)S(1)} %copy-done.1), channel_id=1, source_target_pairs={{0,4},{2,6},{4,0},{6,2},{8,12},{10,14},{12,8},{14,10},{16,20},{18,... | collective-permute-start | bytes 1572872 | tf_op jit(solution)/shard_map/ppermute | solution.py:139
  605.4 31.8 %collective-permute-start.25 = (bf16[1024,256]{1,0:T(8,128)(2,1)S(1)}, bf16[1024,256]{1,0:T(8,128)(2,1)S(1)}, u32[]{:S(2)}, u32[]{:S(2)}) collective-permute-start(bf16[1024,256]{1,0:T(8,128)(2,1)S(1)} %copy-done.7), channel_id=1, source_target_pairs={{0,4},{2,6},{4,0},{6,2},{8,12},{10,14},{12,8},{14,10},{16,20},{18,... | collective-permute-start | bytes 1572872 | tf_op jit(solution)/shard_map/ppermute | solution.py:139
  634.4 67.5 %collective-permute-start.50 = (bf16[1024,256]{1,0:T(8,128)(2,1)S(1)}, bf16[1024,256]{1,0:T(8,128)(2,1)S(1)}, u32[]{:S(2)}, u32[]{:S(2)}) collective-permute-start(bf16[1024,256]{1,0:T(8,128)(2,1)S(1)} %pad_maximum_fusion.11), channel_id=1, source_target_pairs={{0,8},{2,10},{4,12},{6,14},{8,0},{10,2},{12,4},{14,6},{16,24},{18,... | collective-permute-start | bytes 1572872 | tf_op jit(solution)/shard_map/ppermute | solution.py:139
  635.7 34.5 %collective-permute-start.42 = (bf16[1024,256]{1,0:T(8,128)(2,1)S(1)}, bf16[1024,256]{1,0:T(8,128)(2,1)S(1)}, u32[]{:S(2)}, u32[]{:S(2)}) collective-permute-start(bf16[1024,256]{1,0:T(8,128)(2,1)S(1)} %collective-permute-done.41.refs_12_), channel_id=1, source_target_pairs={{0,4},{2,6},{4,0},{6,2},{8,12},{10,14},{12,8},{14,10},{16,20},{18,... | collective-permute-start | bytes 1572872 | tf_op jit(solution)/shard_map/ppermute | solution.py:139
  637.2 44.2 %collective-permute-start.44 = (bf16[1024,256]{1,0:T(8,128)(2,1)S(1)}, bf16[1024,256]{1,0:T(8,128)(2,1)S(1)}, u32[]{:S(2)}, u32[]{:S(2)}) collective-permute-start(bf16[1024,256]{1,0:T(8,128)(2,1)S(1)} %collective-permute-done.43.refs_14_), channel_id=1, source_target_pairs={{0,4},{2,6},{4,0},{6,2},{8,12},{10,14},{12,8},{14,10},{16,20},{18,... | collective-permute-start | bytes 1572872 | tf_op jit(solution)/shard_map/ppermute | solution.py:139
  657.2 70.2 %collective-permute-start.54 = (bf16[1024,256]{1,0:T(8,128)(2,1)S(1)}, bf16[1024,256]{1,0:T(8,128)(2,1)S(1)}, u32[]{:S(2)}, u32[]{:S(2)}) collective-permute-start(bf16[1024,256]{1,0:T(8,128)(2,1)S(1)} %pad_maximum_fusion.11), channel_id=1, source_target_pairs={{0,24},{2,26},{4,28},{6,30},{8,16},{10,18},{12,20},{14,22},{16,8},... | collective-permute-start | bytes 1572872 | tf_op jit(solution)/shard_map/ppermute | solution.py:139
  659.8 67.6 %collective-permute-start.52 = (bf16[1024,256]{1,0:T(8,128)(2,1)S(1)}, bf16[1024,256]{1,0:T(8,128)(2,1)S(1)}, u32[]{:S(2)}, u32[]{:S(2)}) collective-permute-start(bf16[1024,256]{1,0:T(8,128)(2,1)S(1)} %pad_maximum_fusion.10.refs_8_), channel_id=1, source_target_pairs={{0,16},{2,18},{4,20},{6,22},{8,24},{10,26},{12,28},{14,30},{16,0},... | collective-permute-start | bytes 1572872 | tf_op jit(solution)/shard_map/ppermute | solution.py:139
  670.1 58.8 %collective-permute-start.49 = (bf16[1024,256]{1,0:T(8,128)(2,1)S(1)}, bf16[1024,256]{1,0:T(8,128)(2,1)S(1)}, u32[]{:S(2)}, u32[]{:S(2)}) collective-permute-start(bf16[1024,256]{1,0:T(8,128)(2,1)S(1)} %pad_maximum_fusion.10.refs_8_), channel_id=1, source_target_pairs={{0,4},{2,6},{4,0},{6,2},{8,12},{10,14},{12,8},{14,10},{16,20},{18,... | collective-permute-start | bytes 1572872 | tf_op jit(solution)/shard_map/ppermute | solution.py:139
  681.4 48.1 %collective-permute-start.61 = (bf16[1024,256]{1,0:T(8,128)(2,1)S(1)}, bf16[1024,256]{1,0:T(8,128)(2,1)S(1)}, u32[]{:S(2)}, u32[]{:S(2)}) collective-permute-start(bf16[1024,256]{1,0:T(8,128)(2,1)S(1)} %pad_maximum_fusion.13), channel_id=1, source_target_pairs={{0,8},{2,10},{4,12},{6,14},{8,0},{10,2},{12,4},{14,6},{16,24},{18,... | collective-permute-start | bytes 1572872 | tf_op jit(solution)/shard_map/ppermute | solution.py:139
  701.9 48.3 %collective-permute-start.65 = (bf16[1024,256]{1,0:T(8,128)(2,1)S(1)}, bf16[1024,256]{1,0:T(8,128)(2,1)S(1)}, u32[]{:S(2)}, u32[]{:S(2)}) collective-permute-start(bf16[1024,256]{1,0:T(8,128)(2,1)S(1)} %pad_maximum_fusion.13), channel_id=1, source_target_pairs={{0,24},{2,26},{4,28},{6,30},{8,16},{10,18},{12,20},{14,22},{16,8},... | collective-permute-start | bytes 1572872 | tf_op jit(solution)/shard_map/ppermute | solution.py:139
  727.4 24.8 %collective-permute-start.51 = (bf16[1024,256]{1,0:T(8,128)(2,1)S(1)}, bf16[1024,256]{1,0:T(8,128)(2,1)S(1)}, u32[]{:S(2)}, u32[]{:S(2)}) collective-permute-start(bf16[1024,256]{1,0:T(8,128)(2,1)S(1)} %collective-permute-done.50.refs_10_), channel_id=1, source_target_pairs={{0,4},{2,6},{4,0},{6,2},{8,12},{10,14},{12,8},{14,10},{16,20},{18,... | collective-permute-start | bytes 1572872 | tf_op jit(solution)/shard_map/ppermute | solution.py:139
  729.5 35.2 %collective-permute-start.55 = (bf16[1024,256]{1,0:T(8,128)(2,1)S(1)}, bf16[1024,256]{1,0:T(8,128)(2,1)S(1)}, u32[]{:S(2)}, u32[]{:S(2)}) collective-permute-start(bf16[1024,256]{1,0:T(8,128)(2,1)S(1)} %collective-permute-done.54.refs_14_), channel_id=1, source_target_pairs={{0,4},{2,6},{4,0},{6,2},{8,12},{10,14},{12,8},{14,10},{16,20},{18,... | collective-permute-start | bytes 1572872 | tf_op jit(solution)/shard_map/ppermute | solution.py:139
  750.2 34.7 %collective-permute-start.60 = (bf16[1024,256]{1,0:T(8,128)(2,1)S(1)}, bf16[1024,256]{1,0:T(8,128)(2,1)S(1)}, u32[]{:S(2)}, u32[]{:S(2)}) collective-permute-start(bf16[1024,256]{1,0:T(8,128)(2,1)S(1)} %pad_maximum_fusion.12.refs_8_), channel_id=1, source_target_pairs={{0,4},{2,6},{4,0},{6,2},{8,12},{10,14},{12,8},{14,10},{16,20},{18,... | collective-permute-start | bytes 1572872 | tf_op jit(solution)/shard_map/ppermute | solution.py:139
  750.7 36.5 %collective-permute-start.62 = (bf16[1024,256]{1,0:T(8,128)(2,1)S(1)}, bf16[1024,256]{1,0:T(8,128)(2,1)S(1)}, u32[]{:S(2)}, u32[]{:S(2)}) collective-permute-start(bf16[1024,256]{1,0:T(8,128)(2,1)S(1)} %collective-permute-done.61.refs_10_), channel_id=1, source_target_pairs={{0,4},{2,6},{4,0},{6,2},{8,12},{10,14},{12,8},{14,10},{16,20},{18,... | collective-permute-start | bytes 1572872 | tf_op jit(solution)/shard_map/ppermute | solution.py:139
  752.2 46.2 %collective-permute-start.66 = (bf16[1024,256]{1,0:T(8,128)(2,1)S(1)}, bf16[1024,256]{1,0:T(8,128)(2,1)S(1)}, u32[]{:S(2)}, u32[]{:S(2)}) collective-permute-start(bf16[1024,256]{1,0:T(8,128)(2,1)S(1)} %collective-permute-done.65.refs_14_), channel_id=1, source_target_pairs={{0,4},{2,6},{4,0},{6,2},{8,12},{10,14},{12,8},{14,10},{16,20},{18,... | collective-permute-start | bytes 1572872 | tf_op jit(solution)/shard_map/ppermute | solution.py:139
  753.5 55.1 %collective-permute-start.64 = (bf16[1024,256]{1,0:T(8,128)(2,1)S(1)}, bf16[1024,256]{1,0:T(8,128)(2,1)S(1)}, u32[]{:S(2)}, u32[]{:S(2)}) collective-permute-start(bf16[1024,256]{1,0:T(8,128)(2,1)S(1)} %collective-permute-done.63.refs_12_), channel_id=1, source_target_pairs={{0,4},{2,6},{4,0},{6,2},{8,12},{10,14},{12,8},{14,10},{16,20},{18,... | collective-permute-start | bytes 1572872 | tf_op jit(solution)/shard_map/ppermute | solution.py:139
  764.7 81.2 %collective-permute-start.34 = (bf16[512,256]{1,0:T(8,128)(2,1)}, bf16[512,256]{1,0:T(8,128)(2,1)}, u32[]{:S(2)}, u32[]{:S(2)}) collective-permute-start(bf16[512,256]{1,0:T(8,128)(2,1)} %get-tuple-element.49), channel_id=1, source_target_pairs={{0,2},{2,0},{4,6},{6,4},{8,10},{10,8},{12,14},{14,12},{16,18},{18,... | collective-permute-start | bytes 786440 | tf_op jit(solution)/shard_map/ppermute | solution.py:139
  784.9 62.1 %collective-permute-start.35 = (bf16[512,256]{1,0:T(8,128)(2,1)}, bf16[512,256]{1,0:T(8,128)(2,1)S(1)}, u32[]{:S(2)}, u32[]{:S(2)}) collective-permute-start(bf16[512,256]{1,0:T(8,128)(2,1)} %get-tuple-element.48), channel_id=1, source_target_pairs={{0,8},{2,10},{4,12},{6,14},{8,0},{10,2},{12,4},{14,6},{16,24},{18,... | collective-permute-start | bytes 786440 | tf_op jit(solution)/shard_map/ppermute | solution.py:139
  787.2 59.8 %collective-permute-start.36 = (bf16[512,256]{1,0:T(8,128)(2,1)S(1)}, bf16[512,256]{1,0:T(8,128)(2,1)S(1)}, u32[]{:S(2)}, u32[]{:S(2)}) collective-permute-start(bf16[512,256]{1,0:T(8,128)(2,1)S(1)} %get-tuple-element.47), channel_id=1, source_target_pairs={{0,10},{2,8},{4,14},{6,12},{8,2},{10,0},{12,6},{14,4},{16,26},{18,... | collective-permute-start | bytes 786440 | tf_op jit(solution)/shard_map/ppermute | solution.py:139
  (53 other events, 1764.5 us)

commit v2 on v0

--- a/solution.py
+++ b/solution.py
@@ -1,6 +1,10 @@
+import functools
+
 import jax
 import jax.numpy as jnp
 from jax import lax
+from jax.experimental import pallas as pl
+from jax.experimental.pallas import tpu as pltpu
 from jax.sharding import PartitionSpec as P
 
 rope_base = 500000.0
@@ -130,9 +134,408 @@
     return mixed.astype(jnp.bfloat16).reshape(tok_rows, query_heads * head_dim)
 
 
+def stage(done, *values):
+    return lax.optimization_barrier(tuple(values) + tuple(done))[: len(values)]
+
+
+def swap(values, mask):
+    pairs = [(i, i ^ mask) for i in range(lax.axis_size("ctx"))]
+    return lax.ppermute(values, "ctx", pairs)
+
+
+def assemble_kernel(*refs):
+    parts, out = refs[:-1], refs[-1]
+    start = 0
+    for part in parts:
+        out[:, pl.ds(start, part.shape[1])] = part[...]
+        start += part.shape[1]
+
+
+def assemble(parts, rows):
+    width = sum(part.shape[1] for part in parts)
+    return pl.pallas_call(
+        assemble_kernel,
+        out_shape=jax.ShapeDtypeStruct((rows, 4 * width), parts[0].dtype),
+        grid=(4,),
+        in_specs=[pl.BlockSpec((rows, part.shape[1]), lambda k: (k, 0)) for part in parts],
+        out_specs=pl.BlockSpec((rows, width), lambda k: (0, k)),
+        compiler_params=pltpu.CompilerParams(vmem_limit_bytes=32 * 1024 * 1024),
+    )(*parts)
+
+
+def project_kernel(rotated, places, order, *refs):
+    own, other, pieces, turns = refs[0:4], refs[4:8], refs[8:16], refs[16:18]
+    out, total, columns, weights, tables, column_sems, weight_sems, table_sems = refs[18:]
+    rows, width = own[0].shape[0], out.shape[1]
+    depth, slots = 2 * rows, columns.shape[0]
+    swapped = order[24]
+
+    def column_copies(step, sources):
+        start = pl.multiple_of(order[step] * depth, depth)
+        return [
+            pltpu.make_async_copy(
+                sources[m].at[:, pl.ds(start, depth)],
+                columns.at[step % slots, m],
+                column_sems.at[step % slots, m],
+            )
+            for m in range(4)
+        ]
+
+    def weight_copies(step):
+        row, column = places[step]
+        return [
+            pltpu.make_async_copy(
+                pieces[step].at[pl.ds(row + h * rows, rows), pl.ds(column, width)],
+                weights.at[step, pl.ds(pl.multiple_of((swapped ^ h) * rows, rows), rows), :],
+                weight_sems.at[step, h],
+            )
+            for h in range(2)
+        ]
+
+    def start_columns(step):
+        @pl.when(order[16 + step] == 1)
+        def _():
+            for copy in column_copies(step, own):
+                copy.start()
+
+        @pl.when(order[16 + step] == 0)
+        def _():
+            for copy in column_copies(step, other):
+                copy.start()
+
+    table_copies = [
+        pltpu.make_async_copy(turn, tables.at[n], table_sems.at[n]) for n, turn in enumerate(turns)
+    ]
+    for step in range(8):
+        if step < slots - 1:
+            start_columns(step)
+        for copy in weight_copies(step):
+            copy.start()
+    for copy in table_copies:
+        copy.start()
+    for step in range(8):
+        if step + slots - 1 < 8:
+            start_columns(step + slots - 1)
+        for copy in column_copies(step, own) + weight_copies(step):
+            copy.wait()
+        for m in range(4):
+            part = pl.ds(m * rows, rows)
+            product = jnp.dot(
+                columns[step % slots, m], weights[step], preferred_element_type=jnp.float32
+            )
+            if step:
+                product += total[part, :]
+            total[part, :] = product
+    for copy in table_copies:
+        copy.wait()
+    for number, turn in enumerate(rotated):
+        part = pl.ds(number * 128, 128)
+        value = total[:, part]
+        if turn:
+            value = value * tables[0] + pltpu.roll(value, 64, 1) * tables[1]
+        out[:, part] = value.astype(out.dtype)
+
+
+def project(order, own, other, pieces, cosine, sine, rotated):
+    rows, width = own[0].shape[0], 128 * len(rotated)
+    depth, slots = 2 * rows, 3
+    places = [place for _, place in pieces]
+    return pl.pallas_call(
+        functools.partial(project_kernel, rotated, places),
+        out_shape=jax.ShapeDtypeStruct((4 * rows, width), jnp.bfloat16),
+        grid_spec=pltpu.PrefetchScalarGridSpec(
+            num_scalar_prefetch=1,
+            grid=(1,),
+            in_specs=[pl.BlockSpec(memory_space=pl.ANY)] * 18,
+            out_specs=pl.BlockSpec((4 * rows, width), lambda s, o: (0, 0)),
+            scratch_shapes=[
+                pltpu.VMEM((4 * rows, width), jnp.float32),
+                pltpu.VMEM((slots, 4, rows, depth), jnp.bfloat16),
+                pltpu.VMEM((8, depth, width), jnp.bfloat16),
+                pltpu.VMEM((2,) + cosine.shape, jnp.float32),
+                pltpu.SemaphoreType.DMA((slots, 4)),
+                pltpu.SemaphoreType.DMA((8, 2)),
+                pltpu.SemaphoreType.DMA((2,)),
+            ],
+        ),
+        compiler_params=pltpu.CompilerParams(vmem_limit_bytes=48 * 1024 * 1024),
+        cost_estimate=pl.CostEstimate(
+            flops=2 * 4 * rows * 8 * depth * width,
+            bytes_accessed=2 * 4 * rows * 8 * depth + 2 * 8 * depth * width,
+            transcendentals=0,
+        ),
+    )(order, *own, *other, *(array for array, _ in pieces), cosine, sine)
+
+
+def attend_kernel(together, chosen, alive, query, fresh, *refs):
+    sources, (out, cache, sems) = refs[:-3], refs[-3:]
+    tokens, heads, slots = 128, query.shape[1] // 128, 8
+
+    @pl.when(pl.program_id(0) == 0)
+    def _():
+        size = sources[0].shape[0]
+        copies = [
+            pltpu.make_async_copy(source, cache.at[pl.ds(n * size, size)], sems.at[n])
+            for n, source in enumerate(sources)
+        ]
+        for copy in copies:
+            copy.start()
+        for copy in copies:
+            copy.wait()
+
+    scaling = 1.4426950408889634 / 128.0**0.5
+    row = lax.broadcasted_iota(jnp.int32, (heads * tokens, tokens), 0) & (tokens - 1)
+    column = lax.broadcasted_iota(jnp.int32, (heads * tokens, tokens), 1)
+    causal = row >= column
+    ones = jnp.where(lax.broadcasted_iota(jnp.int32, ((slots + 1) * 128, 128), 1) == 0, 1.0, 0.0)
+    ones = ones.astype(jnp.bfloat16)
+    for number in range(together):
+        first = (pl.program_id(0) * together + number) * slots
+        rows = pl.ds(number * tokens, tokens)
+        places = [chosen[first + s] for s in range(slots)]
+        stacked = jnp.concatenate([query[rows, pl.ds(h * 128, 128)] for h in range(heads)], axis=0)
+        keys = [cache[p, 0] for p in places] + [fresh[rows, pl.ds(0, 128)]]
+        values = [cache[p, 1] for p in places] + [fresh[rows, pl.ds(128, 128)]]
+        values = jnp.concatenate([jnp.concatenate(values, axis=0), ones], axis=1)
+        scores = lax.dot_general(
+            stacked,
+            jnp.concatenate(keys, axis=0),
+            (((1,), (1,)), ((), ())),
+            preferred_element_type=jnp.float32,
+        )
+        parts = [
+            jnp.where(alive[first + s] > 0, scores[:, s * 128 : (s + 1) * 128], neg_fill)
+            for s in range(slots)
+        ]
+        parts.append(jnp.where(causal, scores[:, slots * 128 :], neg_fill))
+        top = jnp.max(functools.reduce(jnp.maximum, parts), axis=1, keepdims=True) * scaling
+        weights = [jnp.exp2(part * scaling - top).astype(jnp.bfloat16) for part in parts]
+        mixed = jnp.dot(
+            jnp.concatenate(weights, axis=1), values, preferred_element_type=jnp.float32
+        )
+        mixed = mixed[:, :128] / mixed[:, 128:129]
+        for h in range(heads):
+            out[rows, pl.ds(h * 128, 128)] = mixed[h * tokens : (h + 1) * tokens].astype(out.dtype)
+
+
+def attend_chunk(chosen, alive, mine, query, place, width, fresh, cache):
+    rows, heads = query.shape[0], width // 128
+    together = 4 if heads <= 2 else 2
+    size = 128 * together
+    flip = mine * (rows // size // 4)
+    alive = jnp.concatenate([alive, flip[None]])
+    return pl.pallas_call(
+        functools.partial(attend_kernel, together),
+        out_shape=jax.ShapeDtypeStruct((rows, width), jnp.bfloat16),
+        grid_spec=pltpu.PrefetchScalarGridSpec(
+            num_scalar_prefetch=2,
+            grid=(rows // size,),
+            in_specs=[
+                pl.BlockSpec((size, width), lambda b, c, a: (b, place)),
+                pl.BlockSpec((size, 256), lambda b, c, a: (b, 0)),
+                *[pl.BlockSpec(memory_space=pl.ANY)] * len(cache),
+            ],
+            out_specs=pl.BlockSpec((size, width), lambda b, c, a: (b ^ a[rows // 128 * 8], 0)),
+            scratch_shapes=[
+                pltpu.VMEM((len(cache) * cache[0].shape[0],) + cache[0].shape[1:], cache[0].dtype),
+                pltpu.SemaphoreType.DMA((len(cache),)),
+            ],
+        ),
+        compiler_params=pltpu.CompilerParams(vmem_limit_bytes=48 * 1024 * 1024),
+        cost_estimate=pl.CostEstimate(
+            flops=16 * rows * heads * 1152 * 128,
+            bytes_accessed=len(cache) * cache[0].size * 2 + rows * width * 4,
+            transcendentals=rows * heads * 1152,
+        ),
+    )(chosen, alive, query, fresh, *cache)
+
+
+def grouped(
+    tokens,
+    w_query,
+    key_weight,
+    value_weight,
+    prefix_cache_blocks,
+    selected_owner,
+    selected_offset,
+    selected_alive_mask,
+):
+    rows = tokens.shape[0]
+    heads, blocks_dev, _, block_len, head_dim = prefix_cache_blocks.shape
+    query_blocks, selections = selected_owner.shape[1:]
+    ctx_devices = lax.axis_size("ctx")
+    me = lax.axis_index("ctx")
+    x, y, z = me & 1, (me >> 1) & 1, me >> 2
+    mine = 2 * (z & 1) + x
+    group = (0, 1, 4, 5)
+    per_head = w_query.shape[1] // heads
+    chunks = ((True, 0, 2), (False, 2, 4), (False, 6, 2))
+    along_x, along_y, along_z = 1, 2, 4
+    lines = [[i + 4 * q for q in range(4)] for i in range(4)]
+
+    def columns(chunk):
+        with_fresh, first, count = chunk
+
+        def of_head(k):
+            start = k * per_head + first * head_dim
+            part = lax.dynamic_slice(w_query, (0, start), (rows, count * head_dim))
+            if with_fresh:
+                fresh = [
+                    lax.dynamic_slice(w, (0, k * head_dim), (rows, head_dim))
+                    for w in (key_weight, value_weight)
+                ]
+                part = jnp.concatenate(fresh + [part], axis=1)
+            return part
+
+        return of_head
+
+    def cached(k):
+        return lax.dynamic_index_in_dim(prefix_cache_blocks, k, 0, keepdims=False)
+
+    def given(of_head):
+        return jnp.concatenate([of_head(1 - x), of_head(3 - x)], axis=0)
+
+    def joined(of_head, got):
+        even, odd = jnp.split(got, 2, axis=0)
+        even = jnp.concatenate([of_head(x), even], axis=0)
+        odd = jnp.concatenate([of_head(2 + x), odd], axis=0)
+        return even, odd
+
+    def over_z(even_odd_twice, *beside):
+        planes = lax.all_to_all(even_odd_twice, "ctx", 0, 0, axis_index_groups=lines, tiled=True)
+        return stage(beside, planes)[0] if beside else planes
+
+    def twice(even, odd):
+        return jnp.concatenate([even, odd, even, odd], axis=0)
+
+    def over_tp(values):
+        return lax.ppermute(values, "tp", [(0, 1), (1, 0)])
+
+    def listed(planes, planes_y):
+        return [(array, (q * 2 * rows, 0)) for q in range(4) for array in (planes, planes_y)]
+
+    start = blocks_dev * ctx_devices * block_len
+    positions = jnp.concatenate(
+        [start + (me ^ m) * rows + jnp.arange(rows, dtype=jnp.int32) for m in group]
+    )
+    steps = jnp.arange(head_dim // 2).astype(jnp.float32)
+    inverse = jnp.power(jnp.float32(rope_base), -2.0 * steps / head_dim)
+    angle = positions.astype(jnp.float32)[:, None] * inverse[None, :]
+    cosine, sine = jnp.cos(angle), jnp.sin(angle)
+    cosine = jnp.concatenate([cosine, cosine], axis=1)
+    sine = jnp.concatenate([-sine, sine], axis=1)
+
+    q_0, q_1, q_2, q_3 = jnp.split(tokens, 4, axis=0)
+    late_chunk = (False, 2, 6)
+    a_got = swap(given(columns(chunks[0])), along_x)
+    z_0 = swap(q_0, along_z)
+    tokens_other = over_tp(tokens)
+
+    sends = (twice(*joined(columns(chunks[0]), a_got)), given(cached), given(columns(late_chunk)), q_0, q_1)
+    sends = stage((a_got, z_0, tokens_other), *sends)
+    a_planes = over_z(sends[0])
+    cache_got, late_got, x_0 = (swap(s, along_x) for s in sends[1:4])
+    z_1 = swap(sends[4], along_z)
+
+    late_even, late_odd = joined(columns(late_chunk), late_got)
+
+    def late_twice(c):
+        first = (chunks[c][1] - late_chunk[1]) * head_dim
+        part = slice(first, first + chunks[c][2] * head_dim)
+        return twice(late_even[:, part], late_odd[:, part])
+
+    sends = (twice(*joined(cached, cache_got)), q_1, q_2, q_3, z_0, z_1, q_2, q_3, a_planes)
+    sends = stage((a_planes, cache_got, late_got, x_0, z_1), *sends)
+    cache_planes = over_z(sends[0])
+    x_1, x_2, x_3, xz_0, xz_1 = (swap(s, along_x) for s in sends[1:6])
+    z_2, z_3 = (swap(s, along_z) for s in sends[6:8])
+    a_planes_y = swap(sends[8], along_y)
+
+    tokens_x = jnp.concatenate([x_0, x_1, x_2, x_3], axis=0)
+    sends = (late_twice(1), z_2, z_3, cache_planes, tokens_x)
+    done = (cache_planes, x_1, x_2, x_3, xz_0, xz_1, z_2, z_3, a_planes_y, cosine, sine)
+    sends = stage(done, *sends)
+    b_planes = over_z(sends[0])
+    xz_2, xz_3 = (swap(s, along_x) for s in sends[1:3])
+    cache_planes_y = swap(sends[3], along_y)
+    tokens_x_other = over_tp(sends[4])
+    codes = (selected_owner * blocks_dev + selected_offset) * 2 + selected_alive_mask
+    code = lambda m: lax.dynamic_index_in_dim(codes, mine ^ m, 0, keepdims=False)
+    codes = [code(0)] + [swap(code(m), group[m]) for m in (1, 2, 3)]
+
+    tokens_z = jnp.concatenate([z_0, z_1, z_2, z_3], axis=0)
+    tokens_xz = jnp.concatenate([xz_0, xz_1, xz_2, xz_3], axis=0)
+    sends = (late_twice(2), b_planes, tokens_z, tokens_xz)
+    done = (b_planes, xz_2, xz_3, cache_planes_y, tokens_x_other, *codes[1:])
+    sends = stage(done, *sends)
+    c_send = sends[0]
+    b_planes_y = swap(sends[1], along_y)
+    tokens_z_other, tokens_xz_other = (over_tp(s) for s in sends[2:])
+    own = [tokens, tokens_x, tokens_z, tokens_xz]
+    other = [tokens_other, tokens_x_other, tokens_z_other, tokens_xz_other]
+    cache = (cache_planes, cache_planes_y)
+
+    codes = jnp.stack(codes).reshape(-1)
+    alive = codes & 1
+    offset = (codes >> 1) % blocks_dev
+    owner = (codes >> 1) // blocks_dev
+    piece = (((owner >> 1) & 1) ^ y) * 4 + (owner >> 2)
+    chosen = (piece * 2 + ((owner & 1) ^ x)) * blocks_dev + offset
+
+    place = jnp.arange(8, dtype=jnp.int32)
+    column = ((place >> 1) * 2 + ((place & 1) ^ y)) & 3
+    own_first = lax.axis_index("tp") == 0
+    order = jnp.concatenate(
+        [column, column, ((place < 4) == own_first).astype(jnp.int32), x[None]]
+    )
+
+    out = jnp.zeros((rows, heads * per_head), tokens.dtype)
+    fresh = None
+
+    def compute(chunk, *pieces):
+        with_fresh, first, count = chunk
+        turned = (True, False) * with_fresh + (True,) * count
+        query = project(order, own, other, pieces, cosine, sine, turned)
+        width = count * head_dim
+        mixed = attend_chunk(
+            chosen, alive, mine, query, int(with_fresh), width, query if with_fresh else fresh, cache
+        )
+        return query, mixed
+
+    squares = [[8 * p + 2 * q + m for m in group] for p in range(2) for q in range(2)]
+
+    def home(mixed):
+        return lax.all_to_all(mixed, "ctx", 0, 0, axis_index_groups=squares, tiled=True)
+
+    fresh, a_mixed = compute(chunks[0], *listed(a_planes, a_planes_y))
+    c_planes = over_z(c_send, a_mixed)
+    (send,) = stage((c_planes, b_planes_y, a_mixed), c_planes)
+    c_planes_y = swap(send, along_y)
+    a_out = home(a_mixed)
+    _, b_mixed = compute(chunks[1], *listed(b_planes, b_planes_y))
+    (c_planes,) = stage((b_mixed, a_out), c_planes)
+    b_out = home(b_mixed)
+    _, c_mixed = compute(chunks[2], *listed(c_planes, c_planes_y))
+    return assemble([a_out, b_out, home(c_mixed)], rows)
+
+
 def solution(mesh):
+    def per_shard(*args):
+        tokens, w_query, cache = args[0], args[1], args[4]
+        fits = (
+            mesh.shape["ctx"] == 16
+            and mesh.shape["tp"] == 2
+            and cache.shape[0] == 4
+            and cache.shape[3] == 128
+            and cache.shape[4] == 128
+            and w_query.shape[1] == 4096
+            and tokens.shape == (512, 4096)
+            and args[5].shape[2] == 8
+        )
+        return grouped(*args) if fits else per_device(*args)
+
     return jax.shard_map(
-        per_device,
+        per_shard,
         mesh=mesh,
         in_specs=(
             P("ctx", "tp"),

time: 1360 us -> 571 us (0.42)
  waiting for transfers between devices: 1080 us -> 296 us
  matrix products: 137 us -> 0 us
  Pallas kernels: 0 us -> 121 us
  starting transfers between devices: 5.36 us -> 56.7 us
  other arithmetic: 49.8 us -> 13.2 us
    all_gather x4 -> x0, waiting for transfers between devices: 1070 us -> none  [the longest x1 639 us: per_device(): lax.all_gather(w_query, 'ctx', axis=0, tiled=True)]
    ppermute x0 -> x26, waiting for transfers between devices: none -> 292 us  [the longest x22 284 us: swap(): return lax.ppermute(values, 'ctx', pairs)]
    pallas_call x0 -> x7, Pallas kernels: none -> 121 us  [the longest x3 71.9 us: project(): pl.pallas_call(functools.partial(project_kernel, rotated, places), out_sh...]
    dot_general x7 -> x0, matrix products: 93.3 us -> none  [the longest x1 30.1 us: attend(): jnp.einsum('bhgisk,hbskd->bihgd', far_prob, selected[:, :, :, 1], preferr...]
    reshape x1 -> x0, matrix products: 43.6 us -> none  [per_device(): query_proj.reshape(tok_rows, query_heads, head_dim)]
    unnamed x14 -> x67, local copies, waits for them, and re-layouts: 3.23 us -> 40 us
    ppermute x0 -> x26, starting transfers between devices: none -> 29.5 us  [the longest x22 28.5 us: swap(): return lax.ppermute(values, 'ctx', pairs)]
    reduce_sum x3 -> x0, other arithmetic: 24.3 us -> none  [the longest x2 24 us: attend(): denominator = jnp.sum(far_exp, axis=(4, 5)) + jnp.sum(near_exp, axis=4)]
  transfers between devices with their start and end apart: 5 -> 32, of which waited for: 3 -> 18; matrix products, arithmetic and copies ran while one was open for 5% -> 10% of each run, Pallas kernels for 0% -> 21%
where the time goes in v2:
time: 571 us; the launch traced here: 561 us
  waiting for transfers between devices  296 us (52%)
  Pallas kernels  121 us (21%)
  starting transfers between devices  56.7 us (10%)
  local copies, waits for them, and re-layouts  56.1 us (10%)
  blocking collectives  17.6 us (3%)
  other arithmetic  13.2 us (2%)
    ppermute x22, waiting for transfers between devices, swap(): return lax.ppermute(values, 'ctx', pairs)  284 us
    pallas_call x3, Pallas kernels, project(): pl.pallas_call(functools.partial(project_kernel, rotated, places), out_sh...  71.9 us
    pallas_call x3, Pallas kernels, attend_chunk(): pl.pallas_call(functools.partial(attend_kernel, together), out_shape=jax....  44.7 us
    unnamed x67, local copies, waits for them, and re-layouts  40 us
    ppermute x22, starting transfers between devices, swap(): return lax.ppermute(values, 'ctx', pairs)  28.5 us
    all_to_all x4, starting transfers between devices, over_z(): lax.all_to_all(even_odd_twice, 'ctx', 0, 0, axis_index_groups=lines, tile...  18.6 us
    all_to_all x1, blocking collectives, home(): lax.all_to_all(mixed, 'ctx', 0, 0, axis_index_groups=squares, tiled=True)  17.6 us
  transfers between devices with their start and end apart: 32, of which 18 were waited for; matrix products, arithmetic and copies ran while one was open for 10% of the time, Pallas kernels for 21%

profile of v2, /device:TPU:0, one launch (start us, length us, event | category | flops | bytes accessed | tf_op | source)
XLA Modules:
  0.0 561.0 jit_solution(5742371558975794133)
XLA Ops:
  1.9 2.2 constant_dynamic-slice_fusion.5
  5.2 2.5 collective-permute-start.3
  7.6 2.1 fusion.11
  16.4 15.4 %collective-permute-done.3 = bf16[1024,512]{1,0:T(8,128)(2,1)} collective-permute-done((bf16[1024,512]{1,0:T(8,128)(2,1)}, bf16[1024,512]{1,0:T(8,128)(2,1)}, u32[]{:S(2)}, u32[]{:S(2)}) %collective-permute-start.3) | collective-permute-done | bytes 1048608 | tf_op jit(solution)/shard_map/ppermute | solution.py:143
  36.3 2.0 copy-done.10
  38.3 5.1 all-to-all-start
  47.9 2.0 collective-permute-start.8
  49.8 20.0 %collective-permute-done.7 = bf16[16,2,128,128]{3,2,1,0:T(8,128)(2,1)} collective-permute-done((bf16[16,2,128,128]{3,2,1,0:T(8,128)(2,1)}, bf16[16,2,128,128]{3,2,1,0:T(8,128)(2,1)}, u32[]{:S(2)}, u32[]{:S(2)}) %collective-permute-start.7) | collective-permute-done | bytes 1048608 | tf_op jit(solution)/shard_map/ppermute | solution.py:143
  75.3 1.9 slice_dynamic-update-slice_fusion.3
  79.9 44.9 %collective-permute-done.6 = bf16[128,4096]{1,0:T(8,128)(2,1)} collective-permute-done((bf16[128,4096]{1,0:T(8,128)(2,1)}, bf16[128,4096]{1,0:T(8,128)(2,1)}, u32[]{:S(2)}, u32[]{:S(2)}) %collective-permute-start.6) | collective-permute-done | bytes 1048608 | tf_op jit(solution)/shard_map/ppermute | solution.py:143
  124.8 9.0 %collective-permute-done.8 = bf16[128,4096]{1,0:T(8,128)(2,1)} collective-permute-done((bf16[128,4096]{1,0:T(8,128)(2,1)}, bf16[128,4096]{1,0:T(8,128)(2,1)}, u32[]{:S(2)}, u32[]{:S(2)}) %collective-permute-start.8) | collective-permute-done | bytes 1048608 | tf_op jit(solution)/shard_map/ppermute | solution.py:143
  133.7 3.1 all-to-all-done
  136.8 4.8 all-to-all-start.1
  143.3 3.7 fusion.2
  148.8 2.3 constant_dynamic-update-slice_fusion.3
  156.2 2.2 pad_maximum_fusion
  160.3 16.9 %collective-permute-done.10 = bf16[128,4096]{1,0:T(8,128)(2,1)S(1)} collective-permute-done((bf16[128,4096]{1,0:T(8,128)(2,1)S(1)}, bf16[128,4096]{1,0:T(8,128)(2,1)S(1)}, u32[]{:S(2)}, u32[]{:S(2)}) %collective-permute-start.10) | collective-permute-done | bytes 1048608 | tf_op jit(solution)/shard_map/ppermute | solution.py:143
  179.0 20.6 %collective-permute-done.11 = bf16[128,4096]{1,0:T(8,128)(2,1)S(1)} collective-permute-done((bf16[128,4096]{1,0:T(8,128)(2,1)S(1)}, bf16[128,4096]{1,0:T(8,128)(2,1)S(1)}, u32[]{:S(2)}, u32[]{:S(2)}) %collective-permute-start.11) | collective-permute-done | bytes 1048608 | tf_op jit(solution)/shard_map/ppermute | solution.py:143
  201.1 21.0 %collective-permute-done.12 = bf16[128,4096]{1,0:T(8,128)(2,1)S(1)} collective-permute-done((bf16[128,4096]{1,0:T(8,128)(2,1)S(1)}, bf16[128,4096]{1,0:T(8,128)(2,1)S(1)}, u32[]{:S(2)}, u32[]{:S(2)}) %collective-permute-start.12) | collective-permute-done | bytes 1048608 | tf_op jit(solution)/shard_map/ppermute | solution.py:143
  226.8 8.5 %collective-permute-done.13 = bf16[128,4096]{1,0:T(8,128)(2,1)} collective-permute-done((bf16[128,4096]{1,0:T(8,128)(2,1)S(1)}, bf16[128,4096]{1,0:T(8,128)(2,1)}, u32[]{:S(2)}, u32[]{:S(2)}) %collective-permute-start.13) | collective-permute-done | bytes 1048608 | tf_op jit(solution)/shard_map/ppermute | solution.py:143
  235.3 20.5 %collective-permute-done.14 = bf16[128,4096]{1,0:T(8,128)(2,1)} collective-permute-done((bf16[128,4096]{1,0:T(8,128)(2,1)S(1)}, bf16[128,4096]{1,0:T(8,128)(2,1)}, u32[]{:S(2)}, u32[]{:S(2)}) %collective-permute-start.14) | collective-permute-done | bytes 1048608 | tf_op jit(solution)/shard_map/ppermute | solution.py:143
  255.8 9.0 %collective-permute-done.16 = bf16[128,4096]{1,0:T(8,128)(2,1)} collective-permute-done((bf16[128,4096]{1,0:T(8,128)(2,1)}, bf16[128,4096]{1,0:T(8,128)(2,1)}, u32[]{:S(2)}, u32[]{:S(2)}) %collective-permute-start.16) | collective-permute-done | bytes 1048608 | tf_op jit(solution)/shard_map/ppermute | solution.py:143
  264.8 5.0 all-to-all-start.2
  269.9 2.9 collective-permute-start.2
  273.3 2.3 constant_dynamic-update-slice_fusion.7
  275.7 2.3 constant_dynamic-update-slice_fusion.6
  279.6 2.3 constant_dynamic-update-slice_fusion.11
  282.4 2.3 constant_dynamic-update-slice_fusion.5
  286.3 2.3 constant_dynamic-update-slice_fusion.4.refs_2_
  288.6 2.3 constant_dynamic-update-slice_fusion.10
  290.9 17.2 %collective-permute-done.18 = bf16[128,4096]{1,0:T(8,128)(2,1)S(1)} collective-permute-done((bf16[128,4096]{1,0:T(8,128)(2,1)}, bf16[128,4096]{1,0:T(8,128)(2,1)S(1)}, u32[]{:S(2)}, u32[]{:S(2)}) %collective-permute-start.18) | collective-permute-done | bytes 1048608 | tf_op jit(solution)/shard_map/ppermute | solution.py:143
  309.3 20.7 %collective-permute-done.19 = bf16[128,4096]{1,0:T(8,128)(2,1)S(1)} collective-permute-done((bf16[128,4096]{1,0:T(8,128)(2,1)}, bf16[128,4096]{1,0:T(8,128)(2,1)S(1)}, u32[]{:S(2)}, u32[]{:S(2)}) %collective-permute-start.19) | collective-permute-done | bytes 1048608 | tf_op jit(solution)/shard_map/ppermute | solution.py:143
  331.5 4.3 collective-permute-done.2
  335.8 30.4 %collective-permute-done.21.refs_1_ = bf16[64,2,128,128]{3,2,1,0:T(8,128)(2,1)} collective-permute-done((bf16[64,2,128,128]{3,2,1,0:T(8,128)(2,1)}, bf16[64,2,128,128]{3,2,1,0:T(8,128)(2,1)}, u32[]{:S(2)}, u32[]{:S(2)}) %collective-permute-start.21) | collective-permute-done | bytes 4194336 | tf_op jit(solution)/shard_map/ppermute | solution.py:143
  367.2 3.6 all-to-all-start.5
  371.1 2.5 collective-permute-done.22.refs_6_
  373.6 6.0 %collective-permute-done.23.refs_7_ = bf16[512,4096]{1,0:T(8,128)(2,1)} collective-permute-done((bf16[512,4096]{1,0:T(8,128)(2,1)}, bf16[512,4096]{1,0:T(8,128)(2,1)}, u32[]{:S(2)}, u32[]{:S(2)}) %collective-permute-start.23) | collective-permute-done | bytes 4194336 | tf_op jit(solution)/shard_map/ppermute | solution.py:412
  380.9 33.7 %shard_map.82.query.fresh = bf16[2048,512]{1,0:T(8,128)(2,1)S(1)} custom-call(s32[25]{0:T(128)S(1)} %pad_add_fusion.3.order, bf16[512,4096]{1,0:T(8,128)(2,1)} %refs_0_.5, bf16[512,4096]{1,0:T(8,128)(2,1)} %constant_dynamic-update-slice_fusion.refs_1_, bf16[512,4096]{1,0:T(8,128)(2,1)} %constant_dynamic-update-slice_fusion.4.refs_2_, ...), custom_call_target="tpu_custom_call" | custom-call | flops 17179869184 | bytes 41943040 | tf_op jit(solution)/shard_map/pallas_call | solution.py:243
  414.6 12.5 %shard_map.83 = bf16[2048,256]{1,0:T(8,128)(2,1)S(1)} custom-call(s32[128]{0:T(128)S(1)} %fusion.10.chosen, s32[129]{0:T(256)S(1)} %get-tuple-element.91.alive, bf16[2048,512]{1,0:T(8,128)(2,1)S(1)} %shard_map.82.query.fresh, bf16[2048,512]{1,0:T(8,128)(2,1)S(1)} %shard_map.82.query.fresh, bf16[64,2,128,128]{3,2,1,0:T(8,128)(2,1)} %all-to-all-done.1.refs_0_, ...), custom_call_target="tpu_custom_call" | custom-call | flops 9663676416 | bytes 10485760 | tf_op jit(solution)/shard_map/pallas_call | solution.py:327
  429.5 4.2 all-to-all-start.3
  433.7 25.7 %collective-permute-done.24.refs_9_.refs_11_.refs_13_.refs_15_ = bf16[4096,512]{1,0:T(8,128)(2,1)} collective-permute-done((bf16[4096,512]{1,0:T(8,128)(2,1)}, bf16[4096,512]{1,0:T(8,128)(2,1)}, u32[]{:S(2)}, u32[]{:S(2)}) %collective-permute-start.24) | collective-permute-done | bytes 4194336 | tf_op jit(solution)/shard_map/ppermute | solution.py:143
  461.2 23.9 %shard_map.84.query = bf16[2048,512]{1,0:T(8,128)(2,1)S(1)} custom-call(s32[25]{0:T(128)S(1)} %pad_add_fusion.3.order, bf16[512,4096]{1,0:T(8,128)(2,1)} %refs_0_.5, bf16[512,4096]{1,0:T(8,128)(2,1)} %constant_dynamic-update-slice_fusion.refs_1_, bf16[512,4096]{1,0:T(8,128)(2,1)} %constant_dynamic-update-slice_fusion.4.refs_2_, ...), custom_call_target="tpu_custom_call" | custom-call | flops 17179869184 | bytes 41943040 | tf_op jit(solution)/shard_map/pallas_call | solution.py:243
  485.0 19.7 %shard_map.85 = bf16[2048,512]{1,0:T(8,128)(2,1)S(1)} custom-call(s32[128]{0:T(128)S(1)} %fusion.10.chosen, s32[129]{0:T(256)S(1)} %get-tuple-element.90.alive, bf16[2048,512]{1,0:T(8,128)(2,1)S(1)} %shard_map.84.query, bf16[2048,512]{1,0:T(8,128)(2,1)} %copy-done.4, bf16[64,2,128,128]{3,2,1,0:T(8,128)(2,1)} %all-to-all-done.1.refs_0_, ...), custom_call_target="tpu_custom_call" | custom-call | flops 19327352832 | bytes 12582912 | tf_op jit(solution)/shard_map/pallas_call | solution.py:327
  506.1 4.4 all-to-all-start.4
  511.8 14.3 %shard_map.86.query = bf16[2048,256]{1,0:T(8,128)(2,1)S(1)} custom-call(s32[25]{0:T(128)S(1)} %pad_add_fusion.3.order, bf16[512,4096]{1,0:T(8,128)(2,1)} %refs_0_.5, bf16[512,4096]{1,0:T(8,128)(2,1)} %constant_dynamic-update-slice_fusion.refs_1_, bf16[512,4096]{1,0:T(8,128)(2,1)} %constant_dynamic-update-slice_fusion.4.refs_2_, ...), custom_call_target="tpu_custom_call" | custom-call | flops 8589934592 | bytes 37748736 | tf_op jit(solution)/shard_map/pallas_call | solution.py:243
  526.1 12.5 %shard_map.87 = bf16[2048,256]{1,0:T(8,128)(2,1)S(1)} custom-call(s32[128]{0:T(128)S(1)} %fusion.10.chosen, s32[129]{0:T(256)S(1)} %get-tuple-element.91.alive, bf16[2048,256]{1,0:T(8,128)(2,1)S(1)} %shard_map.86.query, bf16[2048,512]{1,0:T(8,128)(2,1)S(1)} %copy-done.5, bf16[64,2,128,128]{3,2,1,0:T(8,128)(2,1)} %all-to-all-done.1.refs_0_, ...), custom_call_target="tpu_custom_call" | custom-call | flops 9663676416 | bytes 10485760 | tf_op jit(solution)/shard_map/pallas_call | solution.py:327
  538.6 17.6 %all_to_all.72 = bf16[4,512,256]{2,1,0:T(8,128)(2,1)S(1)} all-to-all(bf16[4,512,256]{2,1,0:T(8,128)(2,1)S(1)} %bitcast.42), channel_id=1, replica_groups={{0,2,8,10},{4,6,12,14},{16,18,24,26},{20,22,28,30},{1,3,9,11},{5,7,13,1..., dimensions={0} | all-to-all | bytes 2097152 | tf_op jit(solution)/shard_map/all_to_all | solution.py:508
  556.2 4.5 shard_map.88
  (132 shorter events, 61.1 us)
Async XLA Ops:
  0.0 36.3 %collective-permute-start.5 = (bf16[512,4096]{1,0:T(8,128)(2,1)}, bf16[512,4096]{1,0:T(8,128)(2,1)}, u32[]{:S(2)}, u32[]{:S(2)}) collective-permute-start(bf16[512,4096]{1,0:T(8,128)(2,1)} %refs_0_.5), channel_id=1, source_target_pairs={{0,1},{1,0},{2,3},{3,2},{4,5},{5,4},{6,7},{7,6},{8,9},{9,8},{10,11... | collective-permute-start | bytes 12582920 | tf_op jit(solution)/shard_map/ppermute | solution.py:412
  0.5 7.2 %copy-start.7 = (bf16[512,4096]{1,0:T(8,128)(2,1)S(1)}, bf16[512,4096]{1,0:T(8,128)(2,1)}, u32[]{:S(2)}) copy-start(bf16[512,4096]{1,0:T(8,128)(2,1)} %refs_0_.5) | copy-start | bytes 12582916
  4.1 7.3 %copy-start.14 = (bf16[512,128]{1,0:T(8,128)(2,1)}, bf16[512,128]{1,0:T(8,128)(2,1)S(1)}, u32[]{:S(2)}) copy-start(bf16[512,128]{1,0:T(8,128)(2,1)S(1)} %get-tuple-element.79) | copy-start | bytes 393220
  4.1 7.3 %copy-start.16 = (bf16[512,128]{1,0:T(8,128)(2,1)}, bf16[512,128]{1,0:T(8,128)(2,1)S(1)}, u32[]{:S(2)}) copy-start(bf16[512,128]{1,0:T(8,128)(2,1)S(1)} %get-tuple-element.93) | copy-start | bytes 393220
  5.1 6.2 %copy-start.11 = (bf16[4,8,2,128,128]{4,3,2,1,0:T(8,128)(2,1)S(1)}, bf16[4,8,2,128,128]{4,3,2,1,0:T(8,128)(2,1)}, u32[]{:S(2)}) copy-start(bf16[4,8,2,128,128]{4,3,2,1,0:T(8,128)(2,1)} %param.12) | copy-start | bytes 6291460
  5.2 26.6 %collective-permute-start.3 = (bf16[1024,512]{1,0:T(8,128)(2,1)}, bf16[1024,512]{1,0:T(8,128)(2,1)}, u32[]{:S(2)}, u32[]{:S(2)}) collective-permute-start(bf16[1024,512]{1,0:T(8,128)(2,1)} %maximum_maximum_fusion), channel_id=1, source_target_pairs={{0,2},{2,0},{4,6},{6,4},{8,10},{10,8},{12,14},{14,12},{16,18},{18,... | collective-permute-start | bytes 3145736 | tf_op jit(solution)/shard_map/ppermute | solution.py:143
  9.8 26.6 %collective-permute-start.4 = (bf16[128,4096]{1,0:T(8,128)(2,1)}, bf16[128,4096]{1,0:T(8,128)(2,1)}, u32[]{:S(2)}, u32[]{:S(2)}) collective-permute-start(bf16[128,4096]{1,0:T(8,128)(2,1)} %get-tuple-element.31), channel_id=1, source_target_pairs={{0,8},{2,10},{4,12},{6,14},{8,0},{10,2},{12,4},{14,6},{16,24},{18,... | collective-permute-start | bytes 3145736 | tf_op jit(solution)/shard_map/ppermute | solution.py:143
  13.9 19.0 %copy-start.13 = (bf16[512,128]{1,0:T(8,128)(2,1)S(1)}, bf16[512,128]{1,0:T(8,128)(2,1)}, u32[]{:S(2)}) copy-start(bf16[512,128]{1,0:T(8,128)(2,1)} %get-tuple-element.95) | copy-start | bytes 393220
  15.1 18.9 %copy-start.15 = (bf16[512,128]{1,0:T(8,128)(2,1)S(1)}, bf16[512,128]{1,0:T(8,128)(2,1)}, u32[]{:S(2)}) copy-start(bf16[512,128]{1,0:T(8,128)(2,1)} %copy-done.14) | copy-start | bytes 393220
  15.1 18.9 %copy-start.17 = (bf16[512,128]{1,0:T(8,128)(2,1)S(1)}, bf16[512,128]{1,0:T(8,128)(2,1)}, u32[]{:S(2)}) copy-start(bf16[512,128]{1,0:T(8,128)(2,1)} %copy-done.16) | copy-start | bytes 393220
  38.3 98.5 %all-to-all-start = ((bf16[4,1024,512]{2,1,0:T(8,128)(2,1)}), bf16[4,1024,512]{2,1,0:T(8,128)(2,1)}, u32[]{:S(2)}, u32[]{:S(2)}) async-start(bf16[4,1024,512]{2,1,0:T(8,128)(2,1)} %bitcast.45), calls=%async_computation | async-start | bytes 8388608 | tf_op jit(solution)/shard_map/all_to_all | solution.py:405
  43.4 26.4 %collective-permute-start.7 = (bf16[16,2,128,128]{3,2,1,0:T(8,128)(2,1)}, bf16[16,2,128,128]{3,2,1,0:T(8,128)(2,1)}, u32[]{:S(2)}, u32[]{:S(2)}) collective-permute-start(bf16[16,2,128,128]{3,2,1,0:T(8,128)(2,1)} %pad_maximum_fusion.3), channel_id=1, source_target_pairs={{0,2},{2,0},{4,6},{6,4},{8,10},{10,8},{12,14},{14,12},{16,18},{18,... | collective-permute-start | bytes 3145736 | tf_op jit(solution)/shard_map/ppermute | solution.py:143
  45.0 88.7 %collective-permute-start.9 = (bf16[1024,768]{1,0:T(8,128)(2,1)}, bf16[1024,768]{1,0:T(8,128)(2,1)}, u32[]{:S(2)}, u32[]{:S(2)}) collective-permute-start(bf16[1024,768]{1,0:T(8,128)(2,1)} %pad_maximum_fusion.2), channel_id=1, source_target_pairs={{0,2},{2,0},{4,6},{6,4},{8,10},{10,8},{12,14},{14,12},{16,18},{18,... | collective-permute-start | bytes 4718600 | tf_op jit(solution)/shard_map/ppermute | solution.py:143
  46.3 78.4 %collective-permute-start.6 = (bf16[128,4096]{1,0:T(8,128)(2,1)}, bf16[128,4096]{1,0:T(8,128)(2,1)}, u32[]{:S(2)}, u32[]{:S(2)}) collective-permute-start(bf16[128,4096]{1,0:T(8,128)(2,1)} %get-tuple-element.31), channel_id=1, source_target_pairs={{0,2},{2,0},{4,6},{6,4},{8,10},{10,8},{12,14},{14,12},{16,18},{18,... | collective-permute-start | bytes 3145736 | tf_op jit(solution)/shard_map/ppermute | solution.py:143
  47.9 85.9 %collective-permute-start.8 = (bf16[128,4096]{1,0:T(8,128)(2,1)}, bf16[128,4096]{1,0:T(8,128)(2,1)}, u32[]{:S(2)}, u32[]{:S(2)}) collective-permute-start(bf16[128,4096]{1,0:T(8,128)(2,1)} %get-tuple-element.36), channel_id=1, source_target_pairs={{0,8},{2,10},{4,12},{6,14},{8,0},{10,2},{12,4},{14,6},{16,24},{18,... | collective-permute-start | bytes 3145736 | tf_op jit(solution)/shard_map/ppermute | solution.py:143
  136.8 128.0 %all-to-all-start.1 = ((bf16[64,2,128,128]{3,2,1,0:T(8,128)(2,1)}), bf16[64,2,128,128]{3,2,1,0:T(8,128)(2,1)}, u32[]{:S(2)}, u32[]{:S(2)}) async-start(bf16[64,2,128,128]{3,2,1,0:T(8,128)(2,1)} %slice_dynamic-update-slice_fusion.1), calls=%async_computation.1 | async-start | bytes 8388608 | tf_op jit(solution)/shard_map/all_to_all | solution.py:405
  141.7 123.1 %collective-permute-start.17 = (bf16[4096,512]{1,0:T(8,128)(2,1)}, bf16[4096,512]{1,0:T(8,128)(2,1)}, u32[]{:S(2)}, u32[]{:S(2)}) collective-permute-start(bf16[4096,512]{1,0:T(8,128)(2,1)} %bitcast.13.refs_8_.refs_10_.refs_12_.refs_14_), channel_id=1, source_target_pairs={{0,4},{2,6},{4,0},{6,2},{8,12},{10,14},{12,8},{14,10},{16,20},{18,... | collective-permute-start | bytes 12582920 | tf_op jit(solution)/shard_map/ppermute | solution.py:143
  147.0 4.0 copy-start.20
  147.0 5.5 copy-start.19
  147.0 6.1 %copy-start.18 = (bf16[128,4096]{1,0:T(8,128)(2,1)S(1)}, bf16[128,4096]{1,0:T(8,128)(2,1)}, u32[]{:S(2)}) copy-start(bf16[128,4096]{1,0:T(8,128)(2,1)} %get-tuple-element.40) | copy-start | bytes 3145732
  148.4 7.6 %copy-start.8 = (bf16[512,768]{1,0:T(8,128)(2,1)S(1)}, bf16[512,768]{1,0:T(8,128)(2,1)}, u32[]{:S(2)}) copy-start(bf16[512,768]{1,0:T(8,128)(2,1)} %get-tuple-element.57) | copy-start | bytes 2359300
  151.1 26.1 %collective-permute-start.10 = (bf16[128,4096]{1,0:T(8,128)(2,1)S(1)}, bf16[128,4096]{1,0:T(8,128)(2,1)S(1)}, u32[]{:S(2)}, u32[]{:S(2)}) collective-permute-start(bf16[128,4096]{1,0:T(8,128)(2,1)S(1)} %copy-done.20), channel_id=1, source_target_pairs={{0,2},{2,0},{4,6},{6,4},{8,10},{10,8},{12,14},{14,12},{16,18},{18,... | collective-permute-start | bytes 3145736 | tf_op jit(solution)/shard_map/ppermute | solution.py:143
  152.6 47.1 %collective-permute-start.11 = (bf16[128,4096]{1,0:T(8,128)(2,1)S(1)}, bf16[128,4096]{1,0:T(8,128)(2,1)S(1)}, u32[]{:S(2)}, u32[]{:S(2)}) collective-permute-start(bf16[128,4096]{1,0:T(8,128)(2,1)S(1)} %copy-done.19), channel_id=1, source_target_pairs={{0,2},{2,0},{4,6},{6,4},{8,10},{10,8},{12,14},{14,12},{16,18},{18,... | collective-permute-start | bytes 3145736 | tf_op jit(solution)/shard_map/ppermute | solution.py:143
  153.1 69.0 %collective-permute-start.12 = (bf16[128,4096]{1,0:T(8,128)(2,1)S(1)}, bf16[128,4096]{1,0:T(8,128)(2,1)S(1)}, u32[]{:S(2)}, u32[]{:S(2)}) collective-permute-start(bf16[128,4096]{1,0:T(8,128)(2,1)S(1)} %copy-done.18), channel_id=1, source_target_pairs={{0,2},{2,0},{4,6},{6,4},{8,10},{10,8},{12,14},{14,12},{16,18},{18,... | collective-permute-start | bytes 3145736 | tf_op jit(solution)/shard_map/ppermute | solution.py:143
  158.4 76.9 %collective-permute-start.13 = (bf16[128,4096]{1,0:T(8,128)(2,1)S(1)}, bf16[128,4096]{1,0:T(8,128)(2,1)}, u32[]{:S(2)}, u32[]{:S(2)}) collective-permute-start(bf16[128,4096]{1,0:T(8,128)(2,1)S(1)} %copy-done.19), channel_id=1, source_target_pairs={{0,8},{2,10},{4,12},{6,14},{8,0},{10,2},{12,4},{14,6},{16,24},{18,... | collective-permute-start | bytes 3145736 | tf_op jit(solution)/shard_map/ppermute | solution.py:143
  177.2 78.6 %collective-permute-start.14 = (bf16[128,4096]{1,0:T(8,128)(2,1)S(1)}, bf16[128,4096]{1,0:T(8,128)(2,1)}, u32[]{:S(2)}, u32[]{:S(2)}) collective-permute-start(bf16[128,4096]{1,0:T(8,128)(2,1)S(1)} %copy-done.18), channel_id=1, source_target_pairs={{0,8},{2,10},{4,12},{6,14},{8,0},{10,2},{12,4},{14,6},{16,24},{18,... | collective-permute-start | bytes 3145736 | tf_op jit(solution)/shard_map/ppermute | solution.py:143
  199.6 56.1 %collective-permute-start.15 = (bf16[128,4096]{1,0:T(8,128)(2,1)}, bf16[128,4096]{1,0:T(8,128)(2,1)}, u32[]{:S(2)}, u32[]{:S(2)}) collective-permute-start(bf16[128,4096]{1,0:T(8,128)(2,1)} %collective-permute-done.4), channel_id=1, source_target_pairs={{0,2},{2,0},{4,6},{6,4},{8,10},{10,8},{12,14},{14,12},{16,18},{18,... | collective-permute-start | bytes 3145736 | tf_op jit(solution)/shard_map/ppermute | solution.py:143
  222.1 42.7 %collective-permute-start.16 = (bf16[128,4096]{1,0:T(8,128)(2,1)}, bf16[128,4096]{1,0:T(8,128)(2,1)}, u32[]{:S(2)}, u32[]{:S(2)}) collective-permute-start(bf16[128,4096]{1,0:T(8,128)(2,1)} %collective-permute-done.8), channel_id=1, source_target_pairs={{0,2},{2,0},{4,6},{6,4},{8,10},{10,8},{12,14},{14,12},{16,18},{18,... | collective-permute-start | bytes 3145736 | tf_op jit(solution)/shard_map/ppermute | solution.py:143
  264.8 5.0 copy-start.21
  264.8 5.0 copy-start.22
  264.8 5.0 copy-start.23
  264.8 101.3 %all-to-all-start.2 = ((bf16[4,1024,512]{2,1,0:T(8,128)(2,1)}), bf16[4,1024,512]{2,1,0:T(8,128)(2,1)}, u32[]{:S(2)}, u32[]{:S(2)}) async-start(bf16[4,1024,512]{2,1,0:T(8,128)(2,1)} %bitcast.43), calls=%async_computation.2 | async-start | bytes 8388608 | tf_op jit(solution)/shard_map/all_to_all | solution.py:405
  269.9 8.1 %copy-start.9 = (bf16[512,768]{1,0:T(8,128)(2,1)S(1)}, bf16[512,768]{1,0:T(8,128)(2,1)}, u32[]{:S(2)}) copy-start(bf16[512,768]{1,0:T(8,128)(2,1)} %get-tuple-element.57) | copy-start | bytes 2359300
  269.9 65.8 %collective-permute-start.2 = (s32[4,8]{1,0:T(4,128)S(1)}, s32[4,8]{1,0:T(4,128)S(1)}, u32[]{:S(2)}, u32[]{:S(2)}) collective-permute-start(s32[4,8]{1,0:T(4,128)S(1)} %get-tuple-element.87), channel_id=1, source_target_pairs={{0,10},{2,8},{4,14},{6,12},{8,2},{10,0},{12,6},{14,4},{16,26},{18,... | collective-permute-start | bytes 392 | tf_op jit(solution)/shard_map/ppermute | solution.py:143
  272.8 62.9 %collective-permute-start.20 = (bf16[512,4096]{1,0:T(8,128)(2,1)}, bf16[512,4096]{1,0:T(8,128)(2,1)}, u32[]{:S(2)}, u32[]{:S(2)}) collective-permute-start(bf16[512,4096]{1,0:T(8,128)(2,1)} %constant_dynamic-update-slice_fusion.refs_1_), channel_id=1, source_target_pairs={{0,1},{1,0},{2,3},{3,2},{4,5},{5,4},{6,7},{7,6},{8,9},{9,8},{10,11... | collective-permute-start | bytes 12582920 | tf_op jit(solution)/shard_map/ppermute | solution.py:412
  272.8 93.3 %collective-permute-start.21 = (bf16[64,2,128,128]{3,2,1,0:T(8,128)(2,1)}, bf16[64,2,128,128]{3,2,1,0:T(8,128)(2,1)}, u32[]{:S(2)}, u32[]{:S(2)}) collective-permute-start(bf16[64,2,128,128]{3,2,1,0:T(8,128)(2,1)} %all-to-all-done.1.refs_0_), channel_id=1, source_target_pairs={{0,4},{2,6},{4,0},{6,2},{8,12},{10,14},{12,8},{14,10},{16,20},{18,... | collective-permute-start | bytes 12582920 | tf_op jit(solution)/shard_map/ppermute | solution.py:143
  282.0 26.2 %collective-permute-start.18 = (bf16[128,4096]{1,0:T(8,128)(2,1)}, bf16[128,4096]{1,0:T(8,128)(2,1)S(1)}, u32[]{:S(2)}, u32[]{:S(2)}) collective-permute-start(bf16[128,4096]{1,0:T(8,128)(2,1)} %collective-permute-done.13), channel_id=1, source_target_pairs={{0,2},{2,0},{4,6},{6,4},{8,10},{10,8},{12,14},{14,12},{16,18},{18,... | collective-permute-start | bytes 3145736 | tf_op jit(solution)/shard_map/ppermute | solution.py:143
  284.8 45.2 %collective-permute-start.19 = (bf16[128,4096]{1,0:T(8,128)(2,1)}, bf16[128,4096]{1,0:T(8,128)(2,1)S(1)}, u32[]{:S(2)}, u32[]{:S(2)}) collective-permute-start(bf16[128,4096]{1,0:T(8,128)(2,1)} %collective-permute-done.14), channel_id=1, source_target_pairs={{0,2},{2,0},{4,6},{6,4},{8,10},{10,8},{12,14},{14,12},{16,18},{18,... | collective-permute-start | bytes 3145736 | tf_op jit(solution)/shard_map/ppermute | solution.py:143
  308.2 27.6 %collective-permute-start.1 = (s32[4,8]{1,0:T(4,128)S(1)}, s32[4,8]{1,0:T(4,128)S(1)}, u32[]{:S(2)}, u32[]{:S(2)}) collective-permute-start(s32[4,8]{1,0:T(4,128)S(1)} %get-tuple-element.88), channel_id=1, source_target_pairs={{0,8},{2,10},{4,12},{6,14},{8,0},{10,2},{12,4},{14,6},{16,24},{18,... | collective-permute-start | bytes 392 | tf_op jit(solution)/shard_map/ppermute | solution.py:143
  330.0 5.8 %collective-permute-start = (s32[4,8]{1,0:T(4,128)S(1)}, s32[4,8]{1,0:T(4,128)S(1)}, u32[]{:S(2)}, u32[]{:S(2)}) collective-permute-start(s32[4,8]{1,0:T(4,128)S(1)} %get-tuple-element.89), channel_id=1, source_target_pairs={{0,2},{2,0},{4,6},{6,4},{8,10},{10,8},{12,14},{14,12},{16,18},{18,... | collective-permute-start | bytes 392 | tf_op jit(solution)/shard_map/ppermute | solution.py:143
  366.1 7.5 %collective-permute-start.22 = (bf16[512,4096]{1,0:T(8,128)(2,1)}, bf16[512,4096]{1,0:T(8,128)(2,1)}, u32[]{:S(2)}, u32[]{:S(2)}) collective-permute-start(bf16[512,4096]{1,0:T(8,128)(2,1)} %constant_dynamic-update-slice_fusion.4.refs_2_), channel_id=1, source_target_pairs={{0,1},{1,0},{2,3},{3,2},{4,5},{5,4},{6,7},{7,6},{8,9},{9,8},{10,11... | collective-permute-start | bytes 12582920 | tf_op jit(solution)/shard_map/ppermute | solution.py:412
  366.1 13.5 %collective-permute-start.23 = (bf16[512,4096]{1,0:T(8,128)(2,1)}, bf16[512,4096]{1,0:T(8,128)(2,1)}, u32[]{:S(2)}, u32[]{:S(2)}) collective-permute-start(bf16[512,4096]{1,0:T(8,128)(2,1)} %constant_dynamic-update-slice_fusion.8.refs_3_), channel_id=1, source_target_pairs={{0,1},{1,0},{2,3},{3,2},{4,5},{5,4},{6,7},{7,6},{8,9},{9,8},{10,11... | collective-permute-start | bytes 12582920 | tf_op jit(solution)/shard_map/ppermute | solution.py:412
  366.7 92.8 %collective-permute-start.24 = (bf16[4096,512]{1,0:T(8,128)(2,1)}, bf16[4096,512]{1,0:T(8,128)(2,1)}, u32[]{:S(2)}, u32[]{:S(2)}) collective-permute-start(bf16[4096,512]{1,0:T(8,128)(2,1)} %bitcast.15.refs_8_.refs_10_.refs_12_.refs_14_), channel_id=1, source_target_pairs={{0,4},{2,6},{4,0},{6,2},{8,12},{10,14},{12,8},{14,10},{16,20},{18,... | collective-permute-start | bytes 12582920 | tf_op jit(solution)/shard_map/ppermute | solution.py:143
  367.2 62.3 %all-to-all-start.5 = ((bf16[4,1024,256]{2,1,0:T(8,128)(2,1)}), bf16[4,1024,256]{2,1,0:T(8,128)(2,1)S(1)}, u32[]{:S(2)}, u32[]{:S(2)}) async-start(bf16[4,1024,256]{2,1,0:T(8,128)(2,1)} %bitcast.44), calls=%async_computation.5 | async-start | bytes 4194304 | tf_op jit(solution)/shard_map/all_to_all | solution.py:405
  429.5 76.6 %all-to-all-start.3 = ((bf16[4,512,256]{2,1,0:T(8,128)(2,1)}), bf16[4,512,256]{2,1,0:T(8,128)(2,1)}, u32[]{:S(2)}, u32[]{:S(2)}) async-start(bf16[4,512,256]{2,1,0:T(8,128)(2,1)} %bitcast.41), calls=%async_computation.3 | async-start | bytes 2097152 | tf_op jit(solution)/shard_map/all_to_all | solution.py:508
  459.5 51.1 %collective-permute-start.25 = (bf16[4096,256]{1,0:T(8,128)(2,1)S(1)}, bf16[4096,256]{1,0:T(8,128)(2,1)}, u32[]{:S(2)}, u32[]{:S(2)}) collective-permute-start(bf16[4096,256]{1,0:T(8,128)(2,1)S(1)} %bitcast.34), channel_id=1, source_target_pairs={{0,4},{2,6},{4,0},{6,2},{8,12},{10,14},{12,8},{14,10},{16,20},{18,... | collective-permute-start | bytes 6291464 | tf_op jit(solution)/shard_map/ppermute | solution.py:143
  506.1 32.5 %all-to-all-start.4 = ((bf16[4,512,512]{2,1,0:T(8,128)(2,1)}), bf16[4,512,512]{2,1,0:T(8,128)(2,1)}, u32[]{:S(2)}, u32[]{:S(2)}) async-start(bf16[4,512,512]{2,1,0:T(8,128)(2,1)} %bitcast.40), calls=%async_computation.4 | async-start | bytes 4194304 | tf_op jit(solution)/shard_map/all_to_all | solution.py:508
  511.8 14.3 %copy-start.5 = (bf16[2048,512]{1,0:T(8,128)(2,1)S(1)}, bf16[2048,512]{1,0:T(8,128)(2,1)}, u32[]{:S(2)}) copy-start(bf16[2048,512]{1,0:T(8,128)(2,1)} %copy-done.4) | copy-start | bytes 6291460
  (8 other events, 11.9 us)

commit v3 on v2

--- a/solution.py
+++ b/solution.py
@@ -143,49 +143,80 @@
     return lax.ppermute(values, "ctx", pairs)
 
 
-def assemble_kernel(*refs):
+def copy_kernel(places, source, target):
+    target[...] = source[...]
+
+
+def take_planes(places, values, column, width):
+    size = values.shape[0] // 4
+    return pl.pallas_call(
+        copy_kernel,
+        out_shape=jax.ShapeDtypeStruct((3 * size, width), values.dtype),
+        grid_spec=pltpu.PrefetchScalarGridSpec(
+            num_scalar_prefetch=1,
+            grid=(3,),
+            in_specs=[pl.BlockSpec((size, width), lambda i, p: (p[i], column))],
+            out_specs=pl.BlockSpec((size, width), lambda i, p: (i, 0)),
+        ),
+        compiler_params=pltpu.CompilerParams(vmem_limit_bytes=32 * 1024 * 1024),
+    )(places, values)
+
+
+def assemble_kernel(mine, *refs):
     parts, out = refs[:-1], refs[-1]
-    start = 0
-    for part in parts:
-        out[:, pl.ds(start, part.shape[1])] = part[...]
-        start += part.shape[1]
-
-
-def assemble(parts, rows):
-    width = sum(part.shape[1] for part in parts)
+    for m in range(4):
+
+        @pl.when(pl.program_id(0) == m)
+        def _(m=m):
+            start = 0
+            for part in parts[m::4]:
+                out[:, pl.ds(start, part.shape[1])] = part[...]
+                start += part.shape[1]
+
+
+def assemble(mine, chunks):
+    parts = [part for chunk in chunks for part in chunk]
+    rows, width = parts[0].shape[0], sum(chunk[0].shape[1] for chunk in chunks)
     return pl.pallas_call(
         assemble_kernel,
         out_shape=jax.ShapeDtypeStruct((rows, 4 * width), parts[0].dtype),
-        grid=(4,),
-        in_specs=[pl.BlockSpec((rows, part.shape[1]), lambda k: (k, 0)) for part in parts],
-        out_specs=pl.BlockSpec((rows, width), lambda k: (0, k)),
+        grid_spec=pltpu.PrefetchScalarGridSpec(
+            num_scalar_prefetch=1,
+            grid=(4,),
+            in_specs=[pl.BlockSpec(part.shape, lambda m, k: (0, 0)) for part in parts],
+            out_specs=pl.BlockSpec((rows, width), lambda m, k: (0, m ^ k[0])),
+        ),
         compiler_params=pltpu.CompilerParams(vmem_limit_bytes=32 * 1024 * 1024),
-    )(*parts)
-
-
-def project_kernel(rotated, places, order, *refs):
-    own, other, pieces, turns = refs[0:4], refs[4:8], refs[8:16], refs[16:18]
-    out, total, columns, weights, tables, column_sems, weight_sems, table_sems = refs[18:]
-    rows, width = own[0].shape[0], out.shape[1]
-    depth, slots = 2 * rows, columns.shape[0]
+    )(mine[None], *parts)
+
+
+def project_kernel(rotated, places, starts, order, *refs):
+    count = len(starts)
+    own, other, refs = refs[:count], refs[count : 2 * count], refs[2 * count :]
+    pieces, turns = refs[:8], refs[8:10]
+    out, total, columns, weights, tables, column_sems, weight_sems, table_sems = refs[10:]
+    slots, depth, width = columns.shape[0], columns.shape[2], out.shape[1]
+    rows = depth // 2
     swapped = order[24]
 
     def column_copies(step, sources):
         start = pl.multiple_of(order[step] * depth, depth)
         return [
             pltpu.make_async_copy(
-                sources[m].at[:, pl.ds(start, depth)],
-                columns.at[step % slots, m],
-                column_sems.at[step % slots, m],
+                source.at[:, pl.ds(start, depth)],
+                columns.at[step % slots, pl.ds(starts[n], source.shape[0]), :],
+                column_sems.at[step % slots, n],
             )
-            for m in range(4)
+            for n, source in enumerate(sources)
         ]
 
     def weight_copies(step):
-        row, column = places[step]
+        plane, row, column = places[step]
+        if plane is not None:
+            row = order[25 + plane] * depth
         return [
             pltpu.make_async_copy(
-                pieces[step].at[pl.ds(row + h * rows, rows), pl.ds(column, width)],
+                pieces[step].at[pl.ds(pl.multiple_of(row + h * rows, rows), rows), pl.ds(column, width)],
                 weights.at[step, pl.ds(pl.multiple_of((swapped ^ h) * rows, rows), rows), :],
                 weight_sems.at[step, h],
             )
@@ -221,7 +252,7 @@
         for m in range(4):
             part = pl.ds(m * rows, rows)
             product = jnp.dot(
-                columns[step % slots, m], weights[step], preferred_element_type=jnp.float32
+                columns[step % slots, part, :], weights[step], preferred_element_type=jnp.float32
             )
             if step:
                 product += total[part, :]
@@ -239,21 +270,22 @@
 def project(order, own, other, pieces, cosine, sine, rotated):
     rows, width = own[0].shape[0], 128 * len(rotated)
     depth, slots = 2 * rows, 3
+    starts = [sum(part.shape[0] for part in own[:n]) for n in range(len(own))]
     places = [place for _, place in pieces]
     return pl.pallas_call(
-        functools.partial(project_kernel, rotated, places),
+        functools.partial(project_kernel, rotated, places, starts),
         out_shape=jax.ShapeDtypeStruct((4 * rows, width), jnp.bfloat16),
         grid_spec=pltpu.PrefetchScalarGridSpec(
             num_scalar_prefetch=1,
             grid=(1,),
-            in_specs=[pl.BlockSpec(memory_space=pl.ANY)] * 18,
+            in_specs=[pl.BlockSpec(memory_space=pl.ANY)] * (2 * len(own) + 10),
             out_specs=pl.BlockSpec((4 * rows, width), lambda s, o: (0, 0)),
             scratch_shapes=[
                 pltpu.VMEM((4 * rows, width), jnp.float32),
-                pltpu.VMEM((slots, 4, rows, depth), jnp.bfloat16),
+                pltpu.VMEM((slots, 4 * rows, depth), jnp.bfloat16),
                 pltpu.VMEM((8, depth, width), jnp.bfloat16),
                 pltpu.VMEM((2,) + cosine.shape, jnp.float32),
-                pltpu.SemaphoreType.DMA((slots, 4)),
+                pltpu.SemaphoreType.DMA((slots, len(own))),
                 pltpu.SemaphoreType.DMA((8, 2)),
                 pltpu.SemaphoreType.DMA((2,)),
             ],
@@ -318,12 +350,10 @@
             out[rows, pl.ds(h * 128, 128)] = mixed[h * tokens : (h + 1) * tokens].astype(out.dtype)
 
 
-def attend_chunk(chosen, alive, mine, query, place, width, fresh, cache):
+def attend_chunk(chosen, alive, query, place, width, fresh, cache):
     rows, heads = query.shape[0], width // 128
     together = 4 if heads <= 2 else 2
     size = 128 * together
-    flip = mine * (rows // size // 4)
-    alive = jnp.concatenate([alive, flip[None]])
     return pl.pallas_call(
         functools.partial(attend_kernel, together),
         out_shape=jax.ShapeDtypeStruct((rows, width), jnp.bfloat16),
@@ -335,7 +365,7 @@
                 pl.BlockSpec((size, 256), lambda b, c, a: (b, 0)),
                 *[pl.BlockSpec(memory_space=pl.ANY)] * len(cache),
             ],
-            out_specs=pl.BlockSpec((size, width), lambda b, c, a: (b ^ a[rows // 128 * 8], 0)),
+            out_specs=pl.BlockSpec((size, width), lambda b, c, a: (b, 0)),
             scratch_shapes=[
                 pltpu.VMEM((len(cache) * cache[0].shape[0],) + cache[0].shape[1:], cache[0].dtype),
                 pltpu.SemaphoreType.DMA((len(cache),)),
@@ -369,7 +399,7 @@
     mine = 2 * (z & 1) + x
     group = (0, 1, 4, 5)
     per_head = w_query.shape[1] // heads
-    chunks = ((True, 0, 2), (False, 2, 4), (False, 6, 2))
+    chunks = ((True, 0, 2), (False, 2, 2), (False, 4, 2), (False, 6, 2))
     along_x, along_y, along_z = 1, 2, 4
     lines = [[i + 4 * q for q in range(4)] for i in range(4)]
 
@@ -412,7 +442,16 @@
         return lax.ppermute(values, "tp", [(0, 1), (1, 0)])
 
     def listed(planes, planes_y):
-        return [(array, (q * 2 * rows, 0)) for q in range(4) for array in (planes, planes_y)]
+        return [(array, (r, 0, 0)) for r in range(4) for array in (planes, planes_y)]
+
+    def late_listed(c, planes, column, others_y):
+        pieces = [(planes, (0, 0, column)), (late_here_y, (None, 0, late_start(c)))]
+        for r in (1, 2, 3):
+            pieces += [(planes, (r, 0, column)), (others_y, (None, (r - 1) * 2 * rows, 0))]
+        return pieces
+
+    def others(planes, block=0):
+        return take_planes(jnp.stack([z ^ 1, z ^ 2, z ^ 3]), planes, block, 256)
 
     start = blocks_dev * ctx_devices * block_len
     positions = jnp.concatenate(
@@ -425,11 +464,25 @@
     cosine = jnp.concatenate([cosine, cosine], axis=1)
     sine = jnp.concatenate([-sine, sine], axis=1)
 
-    q_0, q_1, q_2, q_3 = jnp.split(tokens, 4, axis=0)
+    place = jnp.arange(8, dtype=jnp.int32)
+    planes = (place >> 1) ^ z
+    column = (planes * 2 + ((place & 1) ^ y)) & 3
+    own_half = (planes >> 1) == lax.axis_index("tp")
+    order = jnp.concatenate(
+        [column, column, own_half.astype(jnp.int32), x[None], planes[::2]]
+    )
+
+    out = jnp.zeros((rows, heads * per_head), tokens.dtype)
+
+    cut = rows * 5 // 16
+    q_0, q_1, q_2 = tokens[:cut], tokens[cut : 2 * cut], tokens[2 * cut :]
     late_chunk = (False, 2, 6)
     a_got = swap(given(columns(chunks[0])), along_x)
     z_0 = swap(q_0, along_z)
     tokens_other = over_tp(tokens)
+    codes = (selected_owner * blocks_dev + selected_offset) * 2 + selected_alive_mask
+    code = lambda m: lax.dynamic_index_in_dim(codes, mine ^ m, 0, keepdims=False)
+    codes = [code(0)] + [swap(code(m), group[m]) for m in (1, 2, 3)]
 
     sends = (twice(*joined(columns(chunks[0]), a_got)), given(cached), given(columns(late_chunk)), q_0, q_1)
     sends = stage((a_got, z_0, tokens_other), *sends)
@@ -439,40 +492,39 @@
 
     late_even, late_odd = joined(columns(late_chunk), late_got)
 
-    def late_twice(c):
-        first = (chunks[c][1] - late_chunk[1]) * head_dim
-        part = slice(first, first + chunks[c][2] * head_dim)
+    late_here_y = swap(jnp.where(z & 1 == 0, late_even, late_odd), along_y)
+
+    def late_start(c):
+        return (chunks[c][1] - late_chunk[1]) * head_dim
+
+    def late_twice(c, count=1):
+        part = slice(late_start(c), late_start(c) + count * 256)
         return twice(late_even[:, part], late_odd[:, part])
 
-    sends = (twice(*joined(cached, cache_got)), q_1, q_2, q_3, z_0, z_1, q_2, q_3, a_planes)
-    sends = stage((a_planes, cache_got, late_got, x_0, z_1), *sends)
+    sends = (twice(*joined(cached, cache_got)), q_1, q_2, z_0, q_2, a_planes, x_0, z_0, z_1)
+    sends = stage((a_planes, cache_got, late_got, x_0, z_1, late_here_y, cosine, sine, *codes[1:]), *sends)
     cache_planes = over_z(sends[0])
-    x_1, x_2, x_3, xz_0, xz_1 = (swap(s, along_x) for s in sends[1:6])
-    z_2, z_3 = (swap(s, along_z) for s in sends[6:8])
-    a_planes_y = swap(sends[8], along_y)
-
-    tokens_x = jnp.concatenate([x_0, x_1, x_2, x_3], axis=0)
-    sends = (late_twice(1), z_2, z_3, cache_planes, tokens_x)
-    done = (cache_planes, x_1, x_2, x_3, xz_0, xz_1, z_2, z_3, a_planes_y, cosine, sine)
-    sends = stage(done, *sends)
-    b_planes = over_z(sends[0])
-    xz_2, xz_3 = (swap(s, along_x) for s in sends[1:3])
+    x_1, x_2, xz_0 = (swap(s, along_x) for s in sends[1:4])
+    z_2 = swap(sends[4], along_z)
+    a_planes_y = swap(sends[5], along_y)
+    x_0o, z_0o, z_1o = (over_tp(s) for s in sends[6:])
+
+    sends = (late_twice(1, 2), z_1, z_2, cache_planes, x_1, x_2, z_2, xz_0)
+    sends = stage((cache_planes, x_1, x_2, xz_0, z_2, a_planes_y, x_0o, z_0o, z_1o), *sends)
+    bc_planes = over_z(sends[0])
+    xz_1, xz_2 = (swap(s, along_x) for s in sends[1:3])
     cache_planes_y = swap(sends[3], along_y)
-    tokens_x_other = over_tp(sends[4])
-    codes = (selected_owner * blocks_dev + selected_offset) * 2 + selected_alive_mask
-    code = lambda m: lax.dynamic_index_in_dim(codes, mine ^ m, 0, keepdims=False)
-    codes = [code(0)] + [swap(code(m), group[m]) for m in (1, 2, 3)]
-
-    tokens_z = jnp.concatenate([z_0, z_1, z_2, z_3], axis=0)
-    tokens_xz = jnp.concatenate([xz_0, xz_1, xz_2, xz_3], axis=0)
-    sends = (late_twice(2), b_planes, tokens_z, tokens_xz)
-    done = (b_planes, xz_2, xz_3, cache_planes_y, tokens_x_other, *codes[1:])
-    sends = stage(done, *sends)
-    c_send = sends[0]
-    b_planes_y = swap(sends[1], along_y)
-    tokens_z_other, tokens_xz_other = (over_tp(s) for s in sends[2:])
-    own = [tokens, tokens_x, tokens_z, tokens_xz]
-    other = [tokens_other, tokens_x_other, tokens_z_other, tokens_xz_other]
+    x_1o, x_2o, z_2o, xz_0o = (over_tp(s) for s in sends[4:])
+
+    xz_1o, xz_2o = over_tp(xz_1), over_tp(xz_2)
+    own = [tokens, x_0, x_1, x_2, z_0, z_1, z_2, xz_0, xz_1, xz_2]
+    other = [tokens_other, x_0o, x_1o, x_2o, z_0o, z_1o, z_2o, xz_0o, xz_1o, xz_2o]
+    fresh = project(order, own, other, listed(a_planes, a_planes_y), cosine, sine, (True, False, True, True))
+
+    sends = (late_twice(3), others(bc_planes), bc_planes, fresh)
+    d_send, send, bc_planes, fresh = stage((bc_planes, cache_planes_y, fresh), *sends)
+    b_others_y = swap(send, along_y)
+    c_others_y = swap(others(bc_planes, 1), along_y)
     cache = (cache_planes, cache_planes_y)
 
     codes = jnp.stack(codes).reshape(-1)
@@ -482,41 +534,31 @@
     piece = (((owner >> 1) & 1) ^ y) * 4 + (owner >> 2)
     chosen = (piece * 2 + ((owner & 1) ^ x)) * blocks_dev + offset
 
-    place = jnp.arange(8, dtype=jnp.int32)
-    column = ((place >> 1) * 2 + ((place & 1) ^ y)) & 3
-    own_first = lax.axis_index("tp") == 0
-    order = jnp.concatenate(
-        [column, column, ((place < 4) == own_first).astype(jnp.int32), x[None]]
-    )
-
-    out = jnp.zeros((rows, heads * per_head), tokens.dtype)
-    fresh = None
-
-    def compute(chunk, *pieces):
-        with_fresh, first, count = chunk
-        turned = (True, False) * with_fresh + (True,) * count
-        query = project(order, own, other, pieces, cosine, sine, turned)
-        width = count * head_dim
-        mixed = attend_chunk(
-            chosen, alive, mine, query, int(with_fresh), width, query if with_fresh else fresh, cache
-        )
-        return query, mixed
-
-    squares = [[8 * p + 2 * q + m for m in group] for p in range(2) for q in range(2)]
+    def attend(query, place, width):
+        return attend_chunk(chosen, alive, query, place, width, fresh, cache)
+
+    def projected(chunk, pieces):
+        return project(order, own, other, pieces, cosine, sine, (True,) * chunk[2])
 
     def home(mixed):
-        return lax.all_to_all(mixed, "ctx", 0, 0, axis_index_groups=squares, tiled=True)
-
-    fresh, a_mixed = compute(chunks[0], *listed(a_planes, a_planes_y))
-    c_planes = over_z(c_send, a_mixed)
-    (send,) = stage((c_planes, b_planes_y, a_mixed), c_planes)
-    c_planes_y = swap(send, along_y)
+        mixed = mixed.reshape((4, rows) + mixed.shape[1:])
+        return [mixed[0]] + [swap(mixed[m], group[m]) for m in (1, 2, 3)]
+
+    a_mixed = attend(fresh, 1, 256)
+    d_planes = over_z(d_send, a_mixed)
+    (send,) = stage((d_planes, b_others_y, a_mixed), others(d_planes))
+    d_others_y = swap(send, along_y)
     a_out = home(a_mixed)
-    _, b_mixed = compute(chunks[1], *listed(b_planes, b_planes_y))
-    (c_planes,) = stage((b_mixed, a_out), c_planes)
+    b_mixed = attend(projected(chunks[1], late_listed(1, bc_planes, 0, b_others_y)), 0, 256)
     b_out = home(b_mixed)
-    _, c_mixed = compute(chunks[2], *listed(c_planes, c_planes_y))
-    return assemble([a_out, b_out, home(c_mixed)], rows)
+    (c_planes,) = stage((b_mixed, *a_out[1:]), bc_planes)
+    c_mixed = attend(projected(chunks[2], late_listed(2, c_planes, 256, c_others_y)), 0, 256)
+    c_out = home(c_mixed)
+    (d_planes,) = stage((c_mixed, *b_out[1:]), d_planes)
+    query = projected(chunks[3], late_listed(3, d_planes, 0, d_others_y))
+    (query,) = stage(tuple(c_out[1:]), query)
+    d_out = home(attend(query, 0, 256))
+    return assemble(mine, [a_out, b_out, c_out, d_out])
 
 
 def solution(mesh):

time: 571 us -> 520 us (0.911)
  waiting for transfers between devices: 296 us -> 255 us
  local copies, waits for them, and re-layouts: 56.1 us -> 31 us
  starting transfers between devices: 56.7 us -> 75.4 us
  blocking collectives: 17.6 us -> 0 us
  Pallas kernels: 121 us -> 132 us
    ppermute x22 -> x33, waiting for transfers between devices: 284 us -> 249 us  [swap(): return lax.ppermute(values, 'ctx', pairs)]
    unnamed x67 -> x84, local copies, waits for them, and re-layouts: 40 us -> 14.1 us
    all_to_all x1 -> x0, blocking collectives: 17.6 us -> none  [home(): lax.all_to_all(mixed, 'ctx', 0, 0, axis_index_groups=squares, tiled=True)]
    ppermute x22 -> x33, starting transfers between devices: 28.5 us -> 43.8 us  [swap(): return lax.ppermute(values, 'ctx', pairs)]
    all_to_all x4, starting transfers between devices: 18.6 us -> 29.1 us  [over_z(): lax.all_to_all(even_odd_twice, 'ctx', 0, 0, axis_index_groups=lines, tile...]
    all_to_all x2 -> x0, starting transfers between devices: 8.67 us -> none  [home(): lax.all_to_all(mixed, 'ctx', 0, 0, axis_index_groups=squares, tiled=True)]
    pallas_call x3 -> x7, Pallas kernels: 71.9 us -> 78 us  [the longest x4 69.4 us: project(): pl.pallas_call(functools.partial(project_kernel, rotated, places, starts)...]
    slice x0 -> x7, local copies, waits for them, and re-layouts: none -> 5.78 us  [the longest x2 4.38 us: grouped(): q_0, q_1, q_2 = (tokens[:cut], tokens[cut:2 * cut], tokens[2 * cut:])]
  transfers between devices with their start and end apart: 32 -> 47, of which waited for: 18 -> 17; matrix products, arithmetic and copies ran while one was open for 10% -> 8% of each run, Pallas kernels for 21% -> 23%
where the time goes in v3:
time: 520 us; the launch traced here: 511 us
  waiting for transfers between devices  255 us (49%)
  Pallas kernels  132 us (25%)
  starting transfers between devices  75.4 us (15%)
  local copies, waits for them, and re-layouts  31 us (6%)
  other arithmetic  16.4 us (3%)
    ppermute x33, waiting for transfers between devices, swap(): return lax.ppermute(values, 'ctx', pairs)  249 us
    pallas_call x4, Pallas kernels, project(): pl.pallas_call(functools.partial(project_kernel, rotated, places, starts)...  69.4 us
    pallas_call x4, Pallas kernels, attend_chunk(): pl.pallas_call(functools.partial(attend_kernel, together), out_shape=jax....  49.9 us
    ppermute x33, starting transfers between devices, swap(): return lax.ppermute(values, 'ctx', pairs)  43.8 us
    all_to_all x4, starting transfers between devices, over_z(): lax.all_to_all(even_odd_twice, 'ctx', 0, 0, axis_index_groups=lines, tile...  29.1 us
    unnamed x84, local copies, waits for them, and re-layouts  14.1 us
  transfers between devices with their start and end apart: 47, of which 17 were waited for; matrix products, arithmetic and copies ran while one was open for 8% of the time, Pallas kernels for 23%

profile of v3, /device:TPU:0, one launch (start us, length us, event | category | flops | bytes accessed | tf_op | source)
XLA Modules:
  0.0 511.1 jit_solution(6198647017606293174)
XLA Ops:
  0.5 1.9 constant_dynamic-slice_fusion.5
  2.4 1.8 constant_dynamic-slice_fusion.4
  4.2 2.1 constant_dynamic-slice_fusion.3
  7.4 2.5 collective-permute-start.3
  9.9 1.7 fusion.14
  18.4 15.7 %collective-permute-done.3 = bf16[1024,512]{1,0:T(8,128)(2,1)} collective-permute-done((bf16[1024,512]{1,0:T(8,128)(2,1)}, bf16[1024,512]{1,0:T(8,128)(2,1)}, u32[]{:S(2)}, u32[]{:S(2)}) %collective-permute-start.3) | collective-permute-done | bytes 1048608 | tf_op jit(solution)/shard_map/ppermute | solution.py:143
  38.6 4.1 collective-permute-done.4.refs_4_
  42.7 5.0 all-to-all-start
  48.4 1.6 collective-permute-start
  50.0 2.0 collective-permute-start.1
  51.9 2.7 slice.94
  54.7 3.7 fusion.5
  60.2 25.3 %collective-permute-done.6 = bf16[1024,768]{1,0:T(8,128)(2,1)} collective-permute-done((bf16[1024,768]{1,0:T(8,128)(2,1)}, bf16[1024,768]{1,0:T(8,128)(2,1)}, u32[]{:S(2)}, u32[]{:S(2)}) %collective-permute-start.6) | collective-permute-done | bytes 1572896 | tf_op jit(solution)/shard_map/ppermute | solution.py:143
  89.4 2.0 collective-permute-start.7
  91.4 14.9 %collective-permute-done.8 = bf16[16,2,128,128]{3,2,1,0:T(8,128)(2,1)S(1)} collective-permute-done((bf16[16,2,128,128]{3,2,1,0:T(8,128)(2,1)S(1)}, bf16[16,2,128,128]{3,2,1,0:T(8,128)(2,1)S(1)}, u32[]{:S(2)}, u32[]{:S(2)}) %collective-permute-start.8) | collective-permute-done | bytes 1048608 | tf_op jit(solution)/shard_map/ppermute | solution.py:143
  112.0 2.4 collective-permute-start.2
  116.7 29.0 %collective-permute-done.2 = s32[4,8]{1,0:T(4,128)S(1)} collective-permute-done((s32[4,8]{1,0:T(4,128)S(1)}, s32[4,8]{1,0:T(4,128)S(1)}, u32[]{:S(2)}, u32[]{:S(2)}) %collective-permute-start.2) | collective-permute-done | bytes 160 | tf_op jit(solution)/shard_map/ppermute | solution.py:143
  145.6 4.9 all-to-all-start.1
  154.1 1.9 collective-permute-start.11
  156.0 28.1 %collective-permute-done.12.refs_2_ = bf16[160,4096]{1,0:T(8,128)(2,1)} collective-permute-done((bf16[160,4096]{1,0:T(8,128)(2,1)}, bf16[160,4096]{1,0:T(8,128)(2,1)}, u32[]{:S(2)}, u32[]{:S(2)}) %collective-permute-start.12) | collective-permute-done | bytes 1310752 | tf_op jit(solution)/shard_map/ppermute | solution.py:143
  185.5 26.7 %collective-permute-done.14.refs_7_ = bf16[160,4096]{1,0:T(8,128)(2,1)} collective-permute-done((bf16[160,4096]{1,0:T(8,128)(2,1)S(1)}, bf16[160,4096]{1,0:T(8,128)(2,1)}, u32[]{:S(2)}, u32[]{:S(2)}) %collective-permute-start.14) | collective-permute-done | bytes 1310752 | tf_op jit(solution)/shard_map/ppermute | solution.py:143
  212.7 1.7 fusion.1
  214.4 2.2 pad_maximum_fusion
  219.2 33.7 %collective-permute-done.11.refs_6_ = bf16[192,4096]{1,0:T(8,128)(2,1)} collective-permute-done((bf16[192,4096]{1,0:T(8,128)(2,1)}, bf16[192,4096]{1,0:T(8,128)(2,1)}, u32[]{:S(2)}, u32[]{:S(2)}) %collective-permute-start.11) | collective-permute-done | bytes 1572896 | tf_op jit(solution)/shard_map/ppermute | solution.py:143
  252.9 4.8 all-to-all-start.2
  261.9 58.7 %collective-permute-done.19.refs_8_ = bf16[160,4096]{1,0:T(8,128)(2,1)} collective-permute-done((bf16[160,4096]{1,0:T(8,128)(2,1)}, bf16[160,4096]{1,0:T(8,128)(2,1)}, u32[]{:S(2)}, u32[]{:S(2)}) %collective-permute-start.19) | collective-permute-done | bytes 1310752 | tf_op jit(solution)/shard_map/ppermute | solution.py:143
  324.8 1.8 collective-permute-done.23.refs_16_
  326.6 4.1 collective-permute-done.25.refs_18_
  330.7 24.6 %shard_map.83.query.fresh = bf16[2048,512]{1,0:T(8,128)(2,1)} custom-call(s32[29]{0:T(128)S(1)} %concatenate.77.order, bf16[512,4096]{1,0:T(8,128)(2,1)} %refs_0_.7, bf16[160,4096]{1,0:T(8,128)(2,1)} %collective-permute-done.9.refs_1_, bf16[160,4096]{1,0:T(8,128)(2,1)} %collective-permute-done.12.refs_2_, bf16[192,4096]{1,0:T(8,128)(2,1)} %collective-permute-done.13.refs_3_, ...), custom_call_target="tpu_custom_call" | custom-call | flops 17179869184 | bytes 41943040 | tf_op jit(solution)/shard_map/pallas_call | solution.py:275
  355.4 3.9 shard_map.82
  360.9 14.3 %all-to-all-start.3 = ((bf16[4,1024,256]{2,1,0:T(8,128)(2,1)}), bf16[4,1024,256]{2,1,0:T(8,128)(2,1)S(1)}, u32[]{:S(2)}, u32[]{:S(2)}) async-start(bf16[4,1024,256]{2,1,0:T(8,128)(2,1)} %bitcast.36), calls=%async_computation.3 | async-start | bytes 4194304 | tf_op jit(solution)/shard_map/all_to_all | solution.py:435
  375.4 1.6 copy-done.5
  377.0 12.5 %shard_map.84 = bf16[2048,256]{1,0:T(8,128)(2,1)S(1)} custom-call(s32[128]{0:T(128)S(1)} %fusion.13.chosen, s32[128]{0:T(128)S(1)} %and.47.alive, bf16[2048,512]{1,0:T(8,128)(2,1)S(1)} %copy-done.5, bf16[2048,512]{1,0:T(8,128)(2,1)S(1)} %copy-done.5, bf16[64,2,128,128]{3,2,1,0:T(8,128)(2,1)} %all-to-all-done.1.refs_0_, ...), custom_call_target="tpu_custom_call" | custom-call | flops 9663676416 | bytes 10485760 | tf_op jit(solution)/shard_map/pallas_call | solution.py:357
  390.8 2.0 collective-permute-start.29
  393.1 3.9 shard_map.87
  397.6 14.9 %shard_map.85.query = bf16[2048,256]{1,0:T(8,128)(2,1)S(1)} custom-call(s32[29]{0:T(128)S(1)} %concatenate.77.order, bf16[512,4096]{1,0:T(8,128)(2,1)} %refs_0_.7, bf16[160,4096]{1,0:T(8,128)(2,1)} %collective-permute-done.9.refs_1_, bf16[160,4096]{1,0:T(8,128)(2,1)} %collective-permute-done.12.refs_2_, bf16[192,4096]{1,0:T(8,128)(2,1)} %collective-permute-done.13.refs_3_, ...), custom_call_target="tpu_custom_call" | custom-call | flops 8589934592 | bytes 37748736 | tf_op jit(solution)/shard_map/pallas_call | solution.py:275
  412.5 12.5 %shard_map.86 = bf16[2048,256]{1,0:T(8,128)(2,1)S(1)} custom-call(s32[128]{0:T(128)S(1)} %fusion.13.chosen, s32[128]{0:T(128)S(1)} %and.47.alive, bf16[2048,256]{1,0:T(8,128)(2,1)S(1)} %shard_map.85.query, bf16[2048,512]{1,0:T(8,128)(2,1)S(1)} %copy-done.6, bf16[64,2,128,128]{3,2,1,0:T(8,128)(2,1)} %all-to-all-done.1.refs_0_, ...), custom_call_target="tpu_custom_call" | custom-call | flops 9663676416 | bytes 10485760 | tf_op jit(solution)/shard_map/pallas_call | solution.py:357
  427.3 2.0 collective-permute-start.33
  432.1 14.9 %shard_map.88.query = bf16[2048,256]{1,0:T(8,128)(2,1)S(1)} custom-call(s32[29]{0:T(128)S(1)} %concatenate.77.order, bf16[512,4096]{1,0:T(8,128)(2,1)} %refs_0_.7, bf16[160,4096]{1,0:T(8,128)(2,1)} %collective-permute-done.9.refs_1_, bf16[160,4096]{1,0:T(8,128)(2,1)} %collective-permute-done.12.refs_2_, bf16[192,4096]{1,0:T(8,128)(2,1)} %collective-permute-done.13.refs_3_, ...), custom_call_target="tpu_custom_call" | custom-call | flops 8589934592 | bytes 37748736 | tf_op jit(solution)/shard_map/pallas_call | solution.py:275
  447.0 12.5 %shard_map.89 = bf16[2048,256]{1,0:T(8,128)(2,1)S(1)} custom-call(s32[128]{0:T(128)S(1)} %fusion.13.chosen, s32[128]{0:T(128)S(1)} %and.47.alive, bf16[2048,256]{1,0:T(8,128)(2,1)S(1)} %shard_map.88.query, bf16[2048,512]{1,0:T(8,128)(2,1)S(1)} %copy-done.7, bf16[64,2,128,128]{3,2,1,0:T(8,128)(2,1)} %all-to-all-done.1.refs_0_, ...), custom_call_target="tpu_custom_call" | custom-call | flops 9663676416 | bytes 10485760 | tf_op jit(solution)/shard_map/pallas_call | solution.py:357
  460.8 2.0 collective-permute-start.37
  463.2 2.2 collective-permute-done.39.refs_23_.refs_25_.refs_27_
  466.6 14.9 %shard_map.91.query = bf16[2048,256]{1,0:T(8,128)(2,1)S(1)} custom-call(s32[29]{0:T(128)S(1)} %concatenate.77.order, bf16[512,4096]{1,0:T(8,128)(2,1)} %refs_0_.7, bf16[160,4096]{1,0:T(8,128)(2,1)} %collective-permute-done.9.refs_1_, bf16[160,4096]{1,0:T(8,128)(2,1)} %collective-permute-done.12.refs_2_, bf16[192,4096]{1,0:T(8,128)(2,1)} %collective-permute-done.13.refs_3_, ...), custom_call_target="tpu_custom_call" | custom-call | flops 8589934592 | bytes 37748736 | tf_op jit(solution)/shard_map/pallas_call | solution.py:275
  481.6 12.4 %shard_map.92 = bf16[2048,256]{1,0:T(8,128)(2,1)S(1)} custom-call(s32[128]{0:T(128)S(1)} %fusion.13.chosen, s32[128]{0:T(128)S(1)} %and.47.alive, bf16[2048,256]{1,0:T(8,128)(2,1)S(1)} %shard_map.91.query, bf16[2048,512]{1,0:T(8,128)(2,1)S(1)} %copy-done.7, bf16[64,2,128,128]{3,2,1,0:T(8,128)(2,1)} %all-to-all-done.1.refs_0_, ...), custom_call_target="tpu_custom_call" | custom-call | flops 9663676416 | bytes 10485760 | tf_op jit(solution)/shard_map/pallas_call | solution.py:357
  495.3 1.6 collective-permute-start.41
  497.7 5.7 %collective-permute-done.40.refs_13_ = bf16[512,256]{1,0:T(8,128)(2,1)S(1)} collective-permute-done((bf16[512,256]{1,0:T(8,128)(2,1)S(1)}, bf16[512,256]{1,0:T(8,128)(2,1)S(1)}, u32[]{:S(2)}, u32[]{:S(2)}) %collective-permute-start.40) | collective-permute-done | bytes 262176 | tf_op jit(solution)/shard_map/ppermute | solution.py:143
  503.7 3.2 collective-permute-done.42.refs_15_
  506.9 3.7 shard_map.93
  (187 shorter events, 57.4 us)
Async XLA Ops:
  0.0 42.7 %collective-permute-start.5 = (bf16[512,4096]{1,0:T(8,128)(2,1)}, bf16[512,4096]{1,0:T(8,128)(2,1)}, u32[]{:S(2)}, u32[]{:S(2)}) collective-permute-start(bf16[512,4096]{1,0:T(8,128)(2,1)} %refs_0_.7), channel_id=1, source_target_pairs={{0,1},{1,0},{2,3},{3,2},{4,5},{5,4},{6,7},{7,6},{8,9},{9,8},{10,11... | collective-permute-start | bytes 12582920 | tf_op jit(solution)/shard_map/ppermute | solution.py:442
  7.4 26.6 %collective-permute-start.3 = (bf16[1024,512]{1,0:T(8,128)(2,1)}, bf16[1024,512]{1,0:T(8,128)(2,1)}, u32[]{:S(2)}, u32[]{:S(2)}) collective-permute-start(bf16[1024,512]{1,0:T(8,128)(2,1)} %maximum_maximum_fusion), channel_id=1, source_target_pairs={{0,2},{2,0},{4,6},{6,4},{8,10},{10,8},{12,14},{14,12},{16,18},{18,... | collective-permute-start | bytes 3145736 | tf_op jit(solution)/shard_map/ppermute | solution.py:143
  11.6 31.1 %collective-permute-start.4 = (bf16[160,4096]{1,0:T(8,128)(2,1)}, bf16[160,4096]{1,0:T(8,128)(2,1)S(1)}, u32[]{:S(2)}, u32[]{:S(2)}) collective-permute-start(bf16[160,4096]{1,0:T(8,128)(2,1)} %get-tuple-element.40), channel_id=1, source_target_pairs={{0,8},{2,10},{4,12},{6,14},{8,0},{10,2},{12,4},{14,6},{16,24},{18,... | collective-permute-start | bytes 3932168 | tf_op jit(solution)/shard_map/ppermute | solution.py:143
  42.7 288.0 %copy-start.4 = (bf16[160,4096]{1,0:T(8,128)(2,1)}, bf16[160,4096]{1,0:T(8,128)(2,1)S(1)}, u32[]{:S(2)}) copy-start(bf16[160,4096]{1,0:T(8,128)(2,1)S(1)} %collective-permute-done.4.refs_4_) | copy-start | bytes 3932164
  42.7 102.9 %all-to-all-start = ((bf16[4,1024,512]{2,1,0:T(8,128)(2,1)}), bf16[4,1024,512]{2,1,0:T(8,128)(2,1)}, u32[]{:S(2)}, u32[]{:S(2)}) async-start(bf16[4,1024,512]{2,1,0:T(8,128)(2,1)} %bitcast.37), calls=%async_computation | async-start | bytes 8388608 | tf_op jit(solution)/shard_map/all_to_all | solution.py:435
  47.8 37.7 %collective-permute-start.6 = (bf16[1024,768]{1,0:T(8,128)(2,1)}, bf16[1024,768]{1,0:T(8,128)(2,1)}, u32[]{:S(2)}, u32[]{:S(2)}) collective-permute-start(bf16[1024,768]{1,0:T(8,128)(2,1)} %pad_maximum_fusion.4), channel_id=1, source_target_pairs={{0,2},{2,0},{4,6},{6,4},{8,10},{10,8},{12,14},{14,12},{16,18},{18,... | collective-permute-start | bytes 4718600 | tf_op jit(solution)/shard_map/ppermute | solution.py:143
  48.4 63.6 %collective-permute-start = (s32[4,8]{1,0:T(4,128)S(1)}, s32[4,8]{1,0:T(4,128)S(1)}, u32[]{:S(2)}, u32[]{:S(2)}) collective-permute-start(s32[4,8]{1,0:T(4,128)S(1)} %get-tuple-element.113), channel_id=1, source_target_pairs={{0,2},{2,0},{4,6},{6,4},{8,10},{10,8},{12,14},{14,12},{16,18},{18,... | collective-permute-start | bytes 392 | tf_op jit(solution)/shard_map/ppermute | solution.py:143
  50.0 66.7 %collective-permute-start.1 = (s32[4,8]{1,0:T(4,128)S(1)}, s32[4,8]{1,0:T(4,128)S(1)}, u32[]{:S(2)}, u32[]{:S(2)}) collective-permute-start(s32[4,8]{1,0:T(4,128)S(1)} %get-tuple-element.112), channel_id=1, source_target_pairs={{0,8},{2,10},{4,12},{6,14},{8,0},{10,2},{12,4},{14,6},{16,24},{18,... | collective-permute-start | bytes 392 | tf_op jit(solution)/shard_map/ppermute | solution.py:143
  58.5 47.8 %collective-permute-start.8 = (bf16[16,2,128,128]{3,2,1,0:T(8,128)(2,1)S(1)}, bf16[16,2,128,128]{3,2,1,0:T(8,128)(2,1)S(1)}, u32[]{:S(2)}, u32[]{:S(2)}) collective-permute-start(bf16[16,2,128,128]{3,2,1,0:T(8,128)(2,1)S(1)} %copy-done.33), channel_id=1, source_target_pairs={{0,2},{2,0},{4,6},{6,4},{8,10},{10,8},{12,14},{14,12},{16,18},{18,... | collective-permute-start | bytes 3145736 | tf_op jit(solution)/shard_map/ppermute | solution.py:143
  87.4 58.2 %collective-permute-start.10 = (bf16[1024,768]{1,0:T(8,128)(2,1)S(1)}, bf16[1024,768]{1,0:T(8,128)(2,1)}, u32[]{:S(2)}, u32[]{:S(2)}) collective-permute-start(bf16[1024,768]{1,0:T(8,128)(2,1)S(1)} %fusion), channel_id=1, source_target_pairs={{0,4},{2,6},{4,0},{6,2},{8,12},{10,14},{12,8},{14,10},{16,20},{18,... | collective-permute-start | bytes 4718600 | tf_op jit(solution)/shard_map/ppermute | solution.py:143
  89.4 56.3 %collective-permute-start.7 = (bf16[160,4096]{1,0:T(8,128)(2,1)S(1)}, bf16[160,4096]{1,0:T(8,128)(2,1)}, u32[]{:S(2)}, u32[]{:S(2)}) collective-permute-start(bf16[160,4096]{1,0:T(8,128)(2,1)S(1)} %copy-done.29), channel_id=1, source_target_pairs={{0,8},{2,10},{4,12},{6,14},{8,0},{10,2},{12,4},{14,6},{16,24},{18,... | collective-permute-start | bytes 3932168 | tf_op jit(solution)/shard_map/ppermute | solution.py:143
  106.3 39.4 %collective-permute-start.9 = (bf16[160,4096]{1,0:T(8,128)(2,1)}, bf16[160,4096]{1,0:T(8,128)(2,1)}, u32[]{:S(2)}, u32[]{:S(2)}) collective-permute-start(bf16[160,4096]{1,0:T(8,128)(2,1)} %get-tuple-element.40), channel_id=1, source_target_pairs={{0,2},{2,0},{4,6},{6,4},{8,10},{10,8},{12,14},{14,12},{16,18},{18,... | collective-permute-start | bytes 3932168 | tf_op jit(solution)/shard_map/ppermute | solution.py:143
  112.0 33.6 %collective-permute-start.2 = (s32[4,8]{1,0:T(4,128)S(1)}, s32[4,8]{1,0:T(4,128)S(1)}, u32[]{:S(2)}, u32[]{:S(2)}) collective-permute-start(s32[4,8]{1,0:T(4,128)S(1)} %get-tuple-element.111), channel_id=1, source_target_pairs={{0,10},{2,8},{4,14},{6,12},{8,2},{10,0},{12,6},{14,4},{16,26},{18,... | collective-permute-start | bytes 392 | tf_op jit(solution)/shard_map/ppermute | solution.py:143
  145.6 107.2 %all-to-all-start.1 = ((bf16[64,2,128,128]{3,2,1,0:T(8,128)(2,1)}), bf16[64,2,128,128]{3,2,1,0:T(8,128)(2,1)}, u32[]{:S(2)}, u32[]{:S(2)}) async-start(bf16[64,2,128,128]{3,2,1,0:T(8,128)(2,1)} %slice_dynamic-update-slice_fusion.1), calls=%async_computation.1 | async-start | bytes 8388608 | tf_op jit(solution)/shard_map/all_to_all | solution.py:435
  150.5 102.3 %collective-permute-start.15 = (bf16[4096,512]{1,0:T(8,128)(2,1)}, bf16[4096,512]{1,0:T(8,128)(2,1)}, u32[]{:S(2)}, u32[]{:S(2)}) collective-permute-start(bf16[4096,512]{1,0:T(8,128)(2,1)} %bitcast.15.refs_20_.refs_22_.refs_24_.refs_26_), channel_id=1, source_target_pairs={{0,4},{2,6},{4,0},{6,2},{8,12},{10,14},{12,8},{14,10},{16,20},{18,... | collective-permute-start | bytes 12582920 | tf_op jit(solution)/shard_map/ppermute | solution.py:143
  152.1 32.0 %collective-permute-start.12 = (bf16[160,4096]{1,0:T(8,128)(2,1)}, bf16[160,4096]{1,0:T(8,128)(2,1)}, u32[]{:S(2)}, u32[]{:S(2)}) collective-permute-start(bf16[160,4096]{1,0:T(8,128)(2,1)} %get-tuple-element.43), channel_id=1, source_target_pairs={{0,2},{2,0},{4,6},{6,4},{8,10},{10,8},{12,14},{14,12},{16,18},{18,... | collective-permute-start | bytes 3932168 | tf_op jit(solution)/shard_map/ppermute | solution.py:143
  153.5 58.7 %collective-permute-start.14 = (bf16[160,4096]{1,0:T(8,128)(2,1)S(1)}, bf16[160,4096]{1,0:T(8,128)(2,1)}, u32[]{:S(2)}, u32[]{:S(2)}) collective-permute-start(bf16[160,4096]{1,0:T(8,128)(2,1)S(1)} %collective-permute-done.4.refs_4_), channel_id=1, source_target_pairs={{0,2},{2,0},{4,6},{6,4},{8,10},{10,8},{12,14},{14,12},{16,18},{18,... | collective-permute-start | bytes 3932168 | tf_op jit(solution)/shard_map/ppermute | solution.py:143
  154.1 58.1 %collective-permute-start.16 = (bf16[160,4096]{1,0:T(8,128)(2,1)}, bf16[160,4096]{1,0:T(8,128)(2,1)}, u32[]{:S(2)}, u32[]{:S(2)}) collective-permute-start(bf16[160,4096]{1,0:T(8,128)(2,1)} %collective-permute-done.9.refs_1_), channel_id=1, source_target_pairs={{0,1},{1,0},{2,3},{3,2},{4,5},{5,4},{6,7},{7,6},{8,9},{9,8},{10,11... | collective-permute-start | bytes 3932168 | tf_op jit(solution)/shard_map/ppermute | solution.py:442
  154.1 98.8 %collective-permute-start.11 = (bf16[192,4096]{1,0:T(8,128)(2,1)}, bf16[192,4096]{1,0:T(8,128)(2,1)}, u32[]{:S(2)}, u32[]{:S(2)}) collective-permute-start(bf16[192,4096]{1,0:T(8,128)(2,1)} %slice.94), channel_id=1, source_target_pairs={{0,8},{2,10},{4,12},{6,14},{8,0},{10,2},{12,4},{14,6},{16,24},{18,... | collective-permute-start | bytes 4718600 | tf_op jit(solution)/shard_map/ppermute | solution.py:143
  184.1 68.8 %collective-permute-start.13 = (bf16[192,4096]{1,0:T(8,128)(2,1)}, bf16[192,4096]{1,0:T(8,128)(2,1)}, u32[]{:S(2)}, u32[]{:S(2)}) collective-permute-start(bf16[192,4096]{1,0:T(8,128)(2,1)} %slice.94), channel_id=1, source_target_pairs={{0,2},{2,0},{4,6},{6,4},{8,10},{10,8},{12,14},{14,12},{16,18},{18,... | collective-permute-start | bytes 4718600 | tf_op jit(solution)/shard_map/ppermute | solution.py:143
  212.2 4.8 collective-permute-start.17
  212.2 5.9 %collective-permute-start.18 = (bf16[160,4096]{1,0:T(8,128)(2,1)}, bf16[160,4096]{1,0:T(8,128)(2,1)S(1)}, u32[]{:S(2)}, u32[]{:S(2)}) collective-permute-start(bf16[160,4096]{1,0:T(8,128)(2,1)} %collective-permute-done.7.refs_5_), channel_id=1, source_target_pairs={{0,1},{1,0},{2,3},{3,2},{4,5},{5,4},{6,7},{7,6},{8,9},{9,8},{10,11... | collective-permute-start | bytes 3932168 | tf_op jit(solution)/shard_map/ppermute | solution.py:442
  252.9 102.5 %all-to-all-start.2 = ((bf16[4,1024,512]{2,1,0:T(8,128)(2,1)}), bf16[4,1024,512]{2,1,0:T(8,128)(2,1)}, u32[]{:S(2)}, u32[]{:S(2)}) async-start(bf16[4,1024,512]{2,1,0:T(8,128)(2,1)} %bitcast.35), calls=%async_computation.2 | async-start | bytes 8388608 | tf_op jit(solution)/shard_map/all_to_all | solution.py:435
  257.7 63.4 %collective-permute-start.20 = (bf16[192,4096]{1,0:T(8,128)(2,1)}, bf16[192,4096]{1,0:T(8,128)(2,1)}, u32[]{:S(2)}, u32[]{:S(2)}) collective-permute-start(bf16[192,4096]{1,0:T(8,128)(2,1)} %collective-permute-done.11.refs_6_), channel_id=1, source_target_pairs={{0,2},{2,0},{4,6},{6,4},{8,10},{10,8},{12,14},{14,12},{16,18},{18,... | collective-permute-start | bytes 4718600 | tf_op jit(solution)/shard_map/ppermute | solution.py:143
  258.9 61.7 %collective-permute-start.19 = (bf16[160,4096]{1,0:T(8,128)(2,1)}, bf16[160,4096]{1,0:T(8,128)(2,1)}, u32[]{:S(2)}, u32[]{:S(2)}) collective-permute-start(bf16[160,4096]{1,0:T(8,128)(2,1)} %collective-permute-done.7.refs_5_), channel_id=1, source_target_pairs={{0,2},{2,0},{4,6},{6,4},{8,10},{10,8},{12,14},{14,12},{16,18},{18,... | collective-permute-start | bytes 3932168 | tf_op jit(solution)/shard_map/ppermute | solution.py:143
  259.8 60.8 %collective-permute-start.21 = (bf16[160,4096]{1,0:T(8,128)(2,1)}, bf16[160,4096]{1,0:T(8,128)(2,1)}, u32[]{:S(2)}, u32[]{:S(2)}) collective-permute-start(bf16[160,4096]{1,0:T(8,128)(2,1)} %collective-permute-done.12.refs_2_), channel_id=1, source_target_pairs={{0,1},{1,0},{2,3},{3,2},{4,5},{5,4},{6,7},{7,6},{8,9},{9,8},{10,11... | collective-permute-start | bytes 3932168 | tf_op jit(solution)/shard_map/ppermute | solution.py:442
  259.8 61.4 %collective-permute-start.24 = (bf16[160,4096]{1,0:T(8,128)(2,1)}, bf16[160,4096]{1,0:T(8,128)(2,1)}, u32[]{:S(2)}, u32[]{:S(2)}) collective-permute-start(bf16[160,4096]{1,0:T(8,128)(2,1)} %collective-permute-done.14.refs_7_), channel_id=1, source_target_pairs={{0,1},{1,0},{2,3},{3,2},{4,5},{5,4},{6,7},{7,6},{8,9},{9,8},{10,11... | collective-permute-start | bytes 3932168 | tf_op jit(solution)/shard_map/ppermute | solution.py:442
  260.3 99.0 %collective-permute-start.27 = (bf16[64,2,128,128]{3,2,1,0:T(8,128)(2,1)}, bf16[64,2,128,128]{3,2,1,0:T(8,128)(2,1)}, u32[]{:S(2)}, u32[]{:S(2)}) collective-permute-start(bf16[64,2,128,128]{3,2,1,0:T(8,128)(2,1)} %all-to-all-done.1.refs_0_), channel_id=1, source_target_pairs={{0,4},{2,6},{4,0},{6,2},{8,12},{10,14},{12,8},{14,10},{16,20},{18,... | collective-permute-start | bytes 12582920 | tf_op jit(solution)/shard_map/ppermute | solution.py:143
  320.6 4.2 collective-permute-start.22
  320.6 6.0 %collective-permute-start.23 = (bf16[192,4096]{1,0:T(8,128)(2,1)}, bf16[192,4096]{1,0:T(8,128)(2,1)}, u32[]{:S(2)}, u32[]{:S(2)}) collective-permute-start(bf16[192,4096]{1,0:T(8,128)(2,1)} %collective-permute-done.11.refs_6_), channel_id=1, source_target_pairs={{0,1},{1,0},{2,3},{3,2},{4,5},{5,4},{6,7},{7,6},{8,9},{9,8},{10,11... | collective-permute-start | bytes 4718600 | tf_op jit(solution)/shard_map/ppermute | solution.py:442
  321.1 9.6 %collective-permute-start.26 = (bf16[192,4096]{1,0:T(8,128)(2,1)}, bf16[192,4096]{1,0:T(8,128)(2,1)}, u32[]{:S(2)}, u32[]{:S(2)}) collective-permute-start(bf16[192,4096]{1,0:T(8,128)(2,1)} %collective-permute-done.20.refs_9_), channel_id=1, source_target_pairs={{0,1},{1,0},{2,3},{3,2},{4,5},{5,4},{6,7},{7,6},{8,9},{9,8},{10,11... | collective-permute-start | bytes 4718600 | tf_op jit(solution)/shard_map/ppermute | solution.py:442
  321.2 9.5 %collective-permute-start.25 = (bf16[160,4096]{1,0:T(8,128)(2,1)}, bf16[160,4096]{1,0:T(8,128)(2,1)}, u32[]{:S(2)}, u32[]{:S(2)}) collective-permute-start(bf16[160,4096]{1,0:T(8,128)(2,1)} %collective-permute-done.19.refs_8_), channel_id=1, source_target_pairs={{0,1},{1,0},{2,3},{3,2},{4,5},{5,4},{6,7},{7,6},{8,9},{9,8},{10,11... | collective-permute-start | bytes 3932168 | tf_op jit(solution)/shard_map/ppermute | solution.py:442
  359.3 38.3 %collective-permute-start.31 = (bf16[3072,256]{1,0:T(8,128)(2,1)}, bf16[3072,256]{1,0:T(8,128)(2,1)}, u32[]{:S(2)}, u32[]{:S(2)}) collective-permute-start(bf16[3072,256]{1,0:T(8,128)(2,1)} %shard_map.82), channel_id=1, source_target_pairs={{0,4},{2,6},{4,0},{6,2},{8,12},{10,14},{12,8},{14,10},{16,20},{18,... | collective-permute-start | bytes 4718600 | tf_op jit(solution)/shard_map/ppermute | solution.py:143
  360.9 68.8 %all-to-all-start.3 = ((bf16[4,1024,256]{2,1,0:T(8,128)(2,1)}), bf16[4,1024,256]{2,1,0:T(8,128)(2,1)S(1)}, u32[]{:S(2)}, u32[]{:S(2)}) async-start(bf16[4,1024,256]{2,1,0:T(8,128)(2,1)} %bitcast.36), calls=%async_computation.3 | async-start | bytes 4194304 | tf_op jit(solution)/shard_map/all_to_all | solution.py:435
  389.6 35.5 %collective-permute-start.28 = (bf16[512,256]{1,0:T(8,128)(2,1)S(1)}, bf16[512,256]{1,0:T(8,128)(2,1)S(1)}, u32[]{:S(2)}, u32[]{:S(2)}) collective-permute-start(bf16[512,256]{1,0:T(8,128)(2,1)S(1)} %get-tuple-element.95), channel_id=1, source_target_pairs={{0,2},{2,0},{4,6},{6,4},{8,10},{10,8},{12,14},{14,12},{16,18},{18,... | collective-permute-start | bytes 786440 | tf_op jit(solution)/shard_map/ppermute | solution.py:143
  390.8 34.3 %collective-permute-start.29 = (bf16[512,256]{1,0:T(8,128)(2,1)S(1)}, bf16[512,256]{1,0:T(8,128)(2,1)S(1)}, u32[]{:S(2)}, u32[]{:S(2)}) collective-permute-start(bf16[512,256]{1,0:T(8,128)(2,1)S(1)} %get-tuple-element.94), channel_id=1, source_target_pairs={{0,8},{2,10},{4,12},{6,14},{8,0},{10,2},{12,4},{14,6},{16,24},{18,... | collective-permute-start | bytes 786440 | tf_op jit(solution)/shard_map/ppermute | solution.py:143
  392.8 32.3 %collective-permute-start.30 = (bf16[512,256]{1,0:T(8,128)(2,1)S(1)}, bf16[512,256]{1,0:T(8,128)(2,1)S(1)}, u32[]{:S(2)}, u32[]{:S(2)}) collective-permute-start(bf16[512,256]{1,0:T(8,128)(2,1)S(1)} %get-tuple-element.93), channel_id=1, source_target_pairs={{0,10},{2,8},{4,14},{6,12},{8,2},{10,0},{12,6},{14,4},{16,26},{18,... | collective-permute-start | bytes 786440 | tf_op jit(solution)/shard_map/ppermute | solution.py:143
  397.1 35.0 %collective-permute-start.35 = (bf16[3072,256]{1,0:T(8,128)(2,1)}, bf16[3072,256]{1,0:T(8,128)(2,1)}, u32[]{:S(2)}, u32[]{:S(2)}) collective-permute-start(bf16[3072,256]{1,0:T(8,128)(2,1)} %shard_map.87), channel_id=1, source_target_pairs={{0,4},{2,6},{4,0},{6,2},{8,12},{10,14},{12,8},{14,10},{16,20},{18,... | collective-permute-start | bytes 4718600 | tf_op jit(solution)/shard_map/ppermute | solution.py:143
  426.2 34.6 %collective-permute-start.32 = (bf16[512,256]{1,0:T(8,128)(2,1)}, bf16[512,256]{1,0:T(8,128)(2,1)}, u32[]{:S(2)}, u32[]{:S(2)}) collective-permute-start(bf16[512,256]{1,0:T(8,128)(2,1)} %get-tuple-element.91), channel_id=1, source_target_pairs={{0,2},{2,0},{4,6},{6,4},{8,10},{10,8},{12,14},{14,12},{16,18},{18,... | collective-permute-start | bytes 786440 | tf_op jit(solution)/shard_map/ppermute | solution.py:143
  427.3 35.5 %collective-permute-start.33 = (bf16[512,256]{1,0:T(8,128)(2,1)}, bf16[512,256]{1,0:T(8,128)(2,1)}, u32[]{:S(2)}, u32[]{:S(2)}) collective-permute-start(bf16[512,256]{1,0:T(8,128)(2,1)} %get-tuple-element.90), channel_id=1, source_target_pairs={{0,8},{2,10},{4,12},{6,14},{8,0},{10,2},{12,4},{14,6},{16,24},{18,... | collective-permute-start | bytes 786440 | tf_op jit(solution)/shard_map/ppermute | solution.py:143
  429.3 33.9 %collective-permute-start.34 = (bf16[512,256]{1,0:T(8,128)(2,1)}, bf16[512,256]{1,0:T(8,128)(2,1)}, u32[]{:S(2)}, u32[]{:S(2)}) collective-permute-start(bf16[512,256]{1,0:T(8,128)(2,1)} %get-tuple-element.89), channel_id=1, source_target_pairs={{0,10},{2,8},{4,14},{6,12},{8,2},{10,0},{12,6},{14,4},{16,26},{18,... | collective-permute-start | bytes 786440 | tf_op jit(solution)/shard_map/ppermute | solution.py:143
  430.5 35.0 %collective-permute-start.39 = (bf16[3072,256]{1,0:T(8,128)(2,1)S(1)}, bf16[3072,256]{1,0:T(8,128)(2,1)S(1)}, u32[]{:S(2)}, u32[]{:S(2)}) collective-permute-start(bf16[3072,256]{1,0:T(8,128)(2,1)S(1)} %shard_map.90), channel_id=1, source_target_pairs={{0,4},{2,6},{4,0},{6,2},{8,12},{10,14},{12,8},{14,10},{16,20},{18,... | collective-permute-start | bytes 4718600 | tf_op jit(solution)/shard_map/ppermute | solution.py:143
  459.6 22.0 %collective-permute-start.36 = (bf16[512,256]{1,0:T(8,128)(2,1)S(1)}, bf16[512,256]{1,0:T(8,128)(2,1)S(1)}, u32[]{:S(2)}, u32[]{:S(2)}) collective-permute-start(bf16[512,256]{1,0:T(8,128)(2,1)S(1)} %get-tuple-element.87), channel_id=1, source_target_pairs={{0,2},{2,0},{4,6},{6,4},{8,10},{10,8},{12,14},{14,12},{16,18},{18,... | collective-permute-start | bytes 786440 | tf_op jit(solution)/shard_map/ppermute | solution.py:143
  460.8 20.8 %collective-permute-start.37 = (bf16[512,256]{1,0:T(8,128)(2,1)S(1)}, bf16[512,256]{1,0:T(8,128)(2,1)S(1)}, u32[]{:S(2)}, u32[]{:S(2)}) collective-permute-start(bf16[512,256]{1,0:T(8,128)(2,1)S(1)} %get-tuple-element.86), channel_id=1, source_target_pairs={{0,8},{2,10},{4,12},{6,14},{8,0},{10,2},{12,4},{14,6},{16,24},{18,... | collective-permute-start | bytes 786440 | tf_op jit(solution)/shard_map/ppermute | solution.py:143
  462.8 18.8 %collective-permute-start.38 = (bf16[512,256]{1,0:T(8,128)(2,1)S(1)}, bf16[512,256]{1,0:T(8,128)(2,1)S(1)}, u32[]{:S(2)}, u32[]{:S(2)}) collective-permute-start(bf16[512,256]{1,0:T(8,128)(2,1)S(1)} %get-tuple-element.85), channel_id=1, source_target_pairs={{0,10},{2,8},{4,14},{6,12},{8,2},{10,0},{12,6},{14,4},{16,26},{18,... | collective-permute-start | bytes 786440 | tf_op jit(solution)/shard_map/ppermute | solution.py:143
  494.1 9.2 %collective-permute-start.40 = (bf16[512,256]{1,0:T(8,128)(2,1)S(1)}, bf16[512,256]{1,0:T(8,128)(2,1)S(1)}, u32[]{:S(2)}, u32[]{:S(2)}) collective-permute-start(bf16[512,256]{1,0:T(8,128)(2,1)S(1)} %get-tuple-element.83), channel_id=1, source_target_pairs={{0,2},{2,0},{4,6},{6,4},{8,10},{10,8},{12,14},{14,12},{16,18},{18,... | collective-permute-start | bytes 786440 | tf_op jit(solution)/shard_map/ppermute | solution.py:143
  495.3 8.4 %collective-permute-start.41 = (bf16[512,256]{1,0:T(8,128)(2,1)S(1)}, bf16[512,256]{1,0:T(8,128)(2,1)S(1)}, u32[]{:S(2)}, u32[]{:S(2)}) collective-permute-start(bf16[512,256]{1,0:T(8,128)(2,1)S(1)} %get-tuple-element.82), channel_id=1, source_target_pairs={{0,8},{2,10},{4,12},{6,14},{8,0},{10,2},{12,4},{14,6},{16,24},{18,... | collective-permute-start | bytes 786440 | tf_op jit(solution)/shard_map/ppermute | solution.py:143
  496.9 10.0 %collective-permute-start.42 = (bf16[512,256]{1,0:T(8,128)(2,1)S(1)}, bf16[512,256]{1,0:T(8,128)(2,1)S(1)}, u32[]{:S(2)}, u32[]{:S(2)}) collective-permute-start(bf16[512,256]{1,0:T(8,128)(2,1)S(1)} %get-tuple-element.81), channel_id=1, source_target_pairs={{0,10},{2,8},{4,14},{6,12},{8,2},{10,0},{12,6},{14,4},{16,26},{18,... | collective-permute-start | bytes 786440 | tf_op jit(solution)/shard_map/ppermute | solution.py:143
  (36 other events, 641.6 us)
